TPU v7x, 32 devices: a whole 2x2x4 slice. The times are simulated.
32 devices in a mesh: dp: 4 (over y, core), blk: 8 (over z, x).
Axes of the slice: x: 2, y: 2, z: 4, core: 2. Of those that a mesh axis runs over, the one named last changes fastest.
Arguments:
- dec_in: bfloat16 [4, 4096, 768], P('dp', 'blk'), may hold values from -6 to 6
- encodings: bfloat16 [4, 1024, 768], P('dp', 'blk'), may hold values from -6 to 6
- enc_question: int32 [4, 1024], P('dp', 'blk'), may hold values from 0 to 3, as said below
- enc_valid: int32 [4, 1024], P('dp', 'blk'), may hold values from 0 to 1, as said below
- tgt_question: int32 [4, 128], P('dp', 'blk'), may hold values from 0 to 3, as said below
- gain_self: float32 [768], replicated, may hold values from 0.5 to 1.5
- w_qkv: bfloat16 [768, 2304], replicated, may hold values from -0.109375 to 0.109375
- rel_bias: float32 [32, 12], replicated, may hold values from -4 to 4
- w_self_out: bfloat16 [768, 768], replicated, may hold values from -0.875 to 0.875
- gain_cross: float32 [768], replicated, may hold values from 0.5 to 1.5
- w_cross_q: bfloat16 [768, 768], replicated, may hold values from -0.0546875 to 0.0546875
- w_cross_kv: bfloat16 [768, 1536], replicated, may hold values from -0.21875 to 0.21875
- w_cross_out: bfloat16 [768, 768], replicated, may hold values from -0.875 to 0.875
- gain_ff: float32 [768], replicated, may hold values from 0.5 to 1.5
- w_ff_in: bfloat16 [768, 3072], replicated, may hold values from -0.21875 to 0.21875
- w_ff_out: bfloat16 [3072, 768], replicated, may hold values from -0.109375 to 0.109375
- grad_out: bfloat16 [4, 4096, 768], P('dp', 'blk'), may hold values from -6 to 6
Outputs:
- dec_out: bfloat16 [4, 4096, 768], P('dp', 'blk')
- grad_dec: float32 [4, 4096, 768], P('dp', 'blk')
- grad_enc: float32 [4, 1024, 768], P('dp', 'blk')
- grad_gain_self: float32 [768], P('blk')
- grad_qkv: float32 [768, 2304], P('blk')
- grad_rel_bias: float32 [32, 12], P('blk')
- grad_self_out: float32 [768, 768], P('blk')
- grad_gain_cross: float32 [768], P('blk')
- grad_cross_q: float32 [768, 768], P('blk')
- grad_cross_kv: float32 [768, 1536], P('blk')
- grad_cross_out: float32 [768, 768], P('blk')
- grad_gain_ff: float32 [768], P('blk')
- grad_ff_in: float32 [768, 3072], P('blk')
- grad_ff_out: float32 [3072, 768], P('blk')
Inputs may be any that keep to these rules, and one draw needn't show every extreme that they name: `enc_question`: passages of 64 to 384 tokens lie end to end (the last one cut at the group's end); all tokens of a passage share its question; each passage has valid tokens from its start on, at least half of it; one question, drawn from the seed, holds the passages at the group's first, middle and last token, which are fully valid. `enc_valid`: padding lies at the end of each passage. `tgt_question`: each target names a question that has valid encoding tokens in its group; the first target of a group names the question that spans the group.
All inputs are finite; a program needn't handle non-finite values.
Results may differ from a plain program's by a relative error of at most 0.025.
Values may be sent and summed in bfloat16 or wider, within the bound.
No kernel may reach another device: no remote copies, remote signals or barrier semaphores. Data moves between devices by JAX's collectives and lax.ppermute only.
A program may use at most 192 MiB of HBM per device.

v0:
```python
import functools
import math

import jax
import jax.numpy as jnp
import numpy as np
from jax import lax
from jax.experimental import pallas as pl
from jax.experimental.pallas import tpu as pltpu
from jax.sharding import PartitionSpec as P

TLEN = 32
EPSILON = 1e-06
NEG_LARGE = -1e30
GROUP = 128
LOG2E = 1.4426950408889634
BF = jnp.bfloat16
F32 = jnp.float32
VMEM = pl.BlockSpec(memory_space=pltpu.VMEM)
SMEM = pl.BlockSpec(memory_space=pltpu.SMEM)
ANY = pl.BlockSpec(memory_space=pl.ANY)
HBM, STREAM, DRAIN, NEAR, PAIR = "hbm", "stream", "drain", "near", "pair"
MIB = 2**20
LIMITS = dict(
    self_attention=24, self_project=12, cross_forward=30, hidden_gradient=10, feed_hidden=26, feed_weights=18,
    feed_back=12, feed_out=12, cross_backward=20, cross_query_back=12, cross_weights=34, self_backward=14,
    self_weights=24, sum_kernel=16, finish=24, shadow=1, join_encodings=8,
)


def bucket_of(distance, bucket_count):
    exact_count = bucket_count // 2
    if distance < exact_count:
        return distance
    scaled = math.log(distance / exact_count) / math.log(128.0 / exact_count) * exact_count
    return min(bucket_count - 1, exact_count + int(scaled))


def bucket_firsts(bucket_count):
    firsts = {}
    for distance in range(TLEN):
        firsts.setdefault(bucket_of(distance, bucket_count), distance)
    return sorted(firsts.items())


def dot_nn(a, b):
    return jnp.dot(a, b, preferred_element_type=F32)


def dot_nt(a, b):
    return lax.dot_general(a, b, (((1,), (1,)), ((), ())), preferred_element_type=F32)


def dot_tn(a, b):
    return lax.dot_general(a, b, (((0,), (0,)), ((), ())), preferred_element_type=F32)


def inv_rms(v):
    return lax.rsqrt(jnp.mean(v * v, axis=-1, keepdims=True) + EPSILON)


def rms_back(dy, v, gain):
    r = inv_rms(v)
    vr = v * r
    dg = dy * gain
    dv = r * (dg - vr * jnp.mean(dg * vr, axis=-1, keepdims=True))
    return dv, jnp.sum(dy * vr, axis=0, keepdims=True)


def half_masks(rows):
    lane = lax.broadcasted_iota(jnp.int32, (rows, 128), 1)
    low = (lane < 64).astype(F32)
    return low.astype(BF), (1.0 - low).astype(BF)


def chunk_place(chunk, blk, bits):
    rel = jnp.bitwise_xor(chunk, blk)
    place = jnp.int32(0)
    for bit in bits:
        place = place * 2 + jnp.where(jnp.bitwise_and(rel, bit) != 0, 1, 0)
    return place


def chunk_spot(rel, bits):
    spot = 0
    for bit in bits:
        spot = spot * 2 + (1 if rel & bit else 0)
    return spot


def query_block(rows, tokens):
    return max(GROUP, min(rows, rows * 1024 // tokens))


def big(tokens):
    return 61 if tokens > 1024 else None


class Stream:
    def __init__(self, copy, ref):
        self.copy, self.ref, self.waited = copy, ref, False

    def ready(self):
        if not self.waited:
            self.copy.wait()
            self.waited = True
        return self.ref


class Drain:
    def __init__(self, copy, ref):
        self.copy, self.ref, self.started = copy, ref, False

    def flush(self):
        self.copy.start()
        self.started = True


ORDER = []
ROOMY = [True]


class Pair:
    def __init__(self, drains, ref):
        self.drains, self.ref = drains, ref


def in_hbm(x):
    return pltpu.with_memory_space_constraint(x, pltpu.HBM)


def call(
    name, body, out_shape, in_specs, out_specs, operands, scratch=(), grid=(), prefetch=0,
    limit=None, cost=0.001, ahead=(),
):
    operands, in_specs = list(operands), list(in_specs)
    after = list(ORDER)
    wanted = ahead
    ahead = wanted if ROOMY[0] else ()
    outs = isinstance(out_shape, (tuple, list))
    out_shape = list(out_shape) if outs else [out_shape]
    out_specs = list(out_specs) if outs else [out_specs]
    streams, drains, pairs = [], [], []
    extra_scratch = []
    for i, spec in enumerate(in_specs):
        at = prefetch + i
        if spec == STREAM:
            streams.append(at)
            in_specs[i] = ANY
            operands[at] = in_hbm(operands[at])
            extra_scratch += [pltpu.VMEM(operands[at].shape, operands[at].dtype), pltpu.SemaphoreType.DMA]
        elif isinstance(spec, tuple):
            in_specs[i] = spec[1]
            operands[at] = in_hbm(operands[at])
    real = prefetch + len(in_specs)
    for i, spec in enumerate(out_specs):
        shape = out_shape[i]
        if spec == PAIR:
            pairs.append(i)
            out_specs[i] = ANY
            out_shape[i] = pltpu.HBM(shape.shape, shape.dtype)
            if len(pairs) % 2:
                extra_scratch += [
                    pltpu.VMEM((2, *shape.shape), shape.dtype), pltpu.SemaphoreType.DMA((2,))
                ]
        elif spec == DRAIN:
            drains.append(i)
            out_specs[i] = ANY
            out_shape[i] = pltpu.HBM(shape.shape, shape.dtype)
            extra_scratch += [pltpu.VMEM(shape.shape, shape.dtype), pltpu.SemaphoreType.DMA]
        elif spec == NEAR or isinstance(spec, tuple):
            space = pltpu.VMEM if spec == NEAR or spec[0] == NEAR else pltpu.HBM
            out_specs[i] = VMEM if spec == NEAR else spec[1]
            if ROOMY[0] or space is pltpu.HBM:
                out_shape[i] = space(shape.shape, shape.dtype)
    count = len(out_shape)
    for array in ahead:
        out_specs.append(VMEM if not grid else ANY)
        out_shape.append(pltpu.VMEM(array.shape, array.dtype))
    if ahead:
        extra_scratch.append(pltpu.SemaphoreType.DMA((len(ahead),)))
    after = [in_hbm(array) for array in ahead] + after
    out_specs.append(ANY)
    out_shape.append(pltpu.HBM((8, 128), F32))

    def ordered(*refs):
        ins = list(refs[:real])
        results = list(refs[real + len(after) : real + len(after) + len(out_shape) - 1])
        rest = list(refs[real + len(after) + len(out_shape) :])
        early = [
            pltpu.make_async_copy(refs[real + i], results[count + i], rest[-1].at[i])
            for i in range(len(ahead))
        ]
        del results[count:]
        own, extra = rest[: len(scratch)], rest[len(scratch) :]
        made, ends = [], []
        for n, i in enumerate(streams):
            copy = pltpu.make_async_copy(ins[i], extra[2 * n], extra[2 * n + 1])
            copy.start()
            ins[i] = Stream(copy, extra[2 * n])
            made.append(ins[i])
        extra = extra[2 * len(streams) :]
        for i in sorted(drains + pairs[::2]):
            held, sem = extra[:2]
            extra = extra[2:]
            if i in drains:
                results[i] = Drain(pltpu.make_async_copy(held, results[i], sem), held)
                ends.append(results[i])
            else:
                copies = [
                    pltpu.make_async_copy(held.at[k], results[i + k], sem.at[k]) for k in range(2)
                ]
                results[i] = Pair([Drain(copy, held) for copy in copies], held)
                ends += results[i].drains
        for i in reversed(pairs[1::2]):
            del results[i]
        for n, copy in enumerate(early):
            if grid:
                pl.when(pl.program_id(0) == 0)(copy.start)
            else:
                copy.start()
        body(*ins, *results, *own)
        for copy in early:
            if grid:
                pl.when(pl.program_id(0) == grid[0] - 1)(copy.wait)
            else:
                copy.wait()
        for stream in made:
            stream.ready()
        for end in ends:
            if not end.started:
                end.flush()
        for end in ends:
            end.copy.wait()

    got = pl.pallas_call(
        ordered,
        out_shape=tuple(out_shape),
        grid_spec=pltpu.PrefetchScalarGridSpec(
            num_scalar_prefetch=prefetch,
            grid=grid,
            in_specs=in_specs + [ANY] * len(after),
            out_specs=tuple(out_specs),
            scratch_shapes=list(scratch) + extra_scratch,
        ),
        compiler_params=pltpu.CompilerParams(vmem_limit_bytes=(limit or LIMITS[name]) * MIB),
        name=name,
        cost_estimate=pl.CostEstimate(
            flops=int(cost * 1153 * 10**6), bytes_accessed=0, transcendentals=0
        ),
    )(*operands, *after)
    ORDER[:] = [in_hbm(got[-1])]
    got = (*got[:count], *(got[count:-1] if ahead else wanted))
    return got if outs or wanted else got[0]


def shadow(cost):
    call("shadow", lambda: None, (), (), (), (), cost=cost)


def whole(*shape):
    return pl.BlockSpec(shape, lambda *_: (0,) * len(shape))


def shape_of(dtype, *shape):
    return jax.ShapeDtypeStruct(shape, dtype)


class Columns:
    def __init__(self, names, sections, y_parts, chunks, part):
        self.names, self.y_parts, self.chunks, self.part = names, y_parts, chunks, part
        self.sections = []
        first = unit = 0
        for blocks, order in sections:
            if blocks:
                self.sections.append((first, blocks, order, unit))
            first, unit = first + blocks, unit + chunks * blocks
        self.blocks, self.units = first, unit

    def shape(self, more=0):
        return shape_of(BF, self.units + more, self.part, 128)

    def first(self, name):
        done = 0
        for other, width in self.names:
            if other == name:
                return done
            done += width // 128

    def find(self, block):
        for i, (first, blocks, order, _) in enumerate(self.sections):
            if first <= block < first + blocks:
                if order != "y":
                    return i, None, block - first
                y, k = divmod(block - first, blocks // self.y_parts)
                return i, y, k

    def table(self, spots, y_spots):
        units = []
        for c in range(self.chunks):
            for block in range(self.blocks):
                i, y, k = self.find(block)
                _, blocks, order, unit = self.sections[i]
                if y is None:
                    units.append(unit + spots[order][c] * blocks + k)
                else:
                    units.append(unit + (y_spots[y] * self.chunks + spots[0][c]) * (blocks // self.y_parts) + k)
        return units

    def store(self, ref, half, name, value, place_ref, chunks=None, block=0):
        chunks = range(self.chunks) if chunks is None else chunks
        start = self.first(name) + block
        slot = jnp.bitwise_xor(place_ref[0], half)
        for n, c in enumerate(chunks):
            for j in range(value.shape[1] // 128):
                unit = place_ref[self.at + c * self.blocks + start + j]
                ref[slot, unit] = value[n * self.part : (n + 1) * self.part, j * 128 : (j + 1) * 128].astype(BF)


def self_attention(x, gain_self, w_qkv, rel_bias, ahead):
    rows, width = x.shape
    bucket_count, heads = rel_bias.shape
    pairs = heads // 2
    groups = rows // GROUP
    firsts = bucket_firsts(bucket_count)

    def body(
        x, gs_ref, wqkv, rb_ref, a1_out, qkv_out, p1_out, o1_ref, o1_out, bias
    ):
        a1_ref, qkv_ref, p1_ref = a1_out.ref, qkv_out.ref, p1_out.ref
        xf = x.ready()[...].astype(F32)
        a1 = (xf * inv_rms(xf) * gs_ref[...]).astype(BF)
        a1_ref[...] = a1
        a1_out.flush()
        wqkv_ref = wqkv.ready()

        def project(t, carry):
            at = pl.ds(pl.multiple_of(t * width, 128), width)
            qkv_ref[:, at] = dot_nn(a1_ref[...], wqkv_ref[:, at]).astype(BF)
            return carry

        lax.fori_loop(0, 3, project, 0)
        qkv_out.flush()
        row = lax.broadcasted_iota(jnp.int32, (GROUP, GROUP), 0)
        col = lax.broadcasted_iota(jnp.int32, (GROUP, GROUP), 1)
        distance = row - col
        allowed = jnp.logical_and(distance >= 0, row // TLEN == col // TLEN)

        def make_bias(h, carry):
            val = jnp.full((GROUP, GROUP), NEG_LARGE, F32)
            for b, first in firsts:
                val = jnp.where(distance >= first, rb_ref[h, b], val)
            bias[h] = jnp.where(allowed, val, NEG_LARGE)
            return carry

        lax.fori_loop(0, heads, make_bias, 0)
        m0, m1 = half_masks(GROUP)

        def attend(g, carry):
            at = pl.ds(pl.multiple_of(g * GROUP, GROUP), GROUP)
            for pair in range(pairs):
                lo = pair * 128
                q = qkv_ref[at, lo : lo + 128]
                k = qkv_ref[at, width + lo : width + lo + 128]
                v = qkv_ref[at, 2 * width + lo : 2 * width + lo + 128]
                s = dot_nt(jnp.concatenate([q * m0, q * m1], 0), k)
                s = s + jnp.concatenate([bias[2 * pair], bias[2 * pair + 1]], 0)
                e = jnp.exp(s - jnp.max(s, -1, keepdims=True))
                p = (e / jnp.sum(e, -1, keepdims=True)).astype(BF)
                p1_ref[g, pair] = p
                o = dot_nn(
                    jnp.concatenate([p[:GROUP], p[GROUP:]], 1),
                    jnp.concatenate([v * m0, v * m1], 0),
                )
                o1_ref[at, lo : lo + 128] = o.astype(BF)
            return carry

        lax.fori_loop(0, groups, attend, 0)
        p1_out.flush()
        o1_out.ref[...] = o1_ref[...]
        o1_out.flush()

    return call(
        "self_attention",
        body,
        (
            shape_of(BF, rows, width),
            shape_of(BF, rows, 3 * width),
            shape_of(BF, groups, pairs, 2 * GROUP, GROUP),
            shape_of(BF, rows, width),
            shape_of(BF, rows, width),
        ),
        [STREAM, VMEM, STREAM, SMEM],
        (DRAIN, DRAIN, DRAIN, NEAR, DRAIN),
        (x, gain_self.reshape(1, width), w_qkv, rel_bias.T),
        ahead=ahead,
        scratch=[pltpu.VMEM((heads, GROUP, GROUP), F32)],
    )


def self_project(x, o1, w_self_out, gain_cross, w_cross_q, ahead):
    rows, width = x.shape

    def body(x_ref, o1_ref, wso_ref, gc_ref, wcq_ref, h1_ref, cq_ref, h1_out, a2_out, cq_out):
        h1 = dot_nn(o1_ref[...], wso_ref[...]) + x_ref[...].astype(F32)
        h1_ref[...] = h1
        h1_out.ref[...] = h1
        h1_out.flush()
        a2 = (h1 * inv_rms(h1) * gc_ref[...]).astype(BF)
        a2_out.ref[...] = a2
        a2_out.flush()
        cq = dot_nn(a2, wcq_ref[...]).astype(BF)
        cq_ref[...] = cq
        cq_out.ref[...] = cq

    low, full = shape_of(BF, rows, width), shape_of(F32, rows, width)
    return call(
        "self_project",
        body,
        (full, low, full, low, low),
        [VMEM] * 5,
        (NEAR, NEAR, DRAIN, DRAIN, DRAIN),
        (x, o1, w_self_out, gain_cross.reshape(1, width), w_cross_q),
        ahead=ahead,
    )


def cross_forward(
    pieces, order, shard_rows, tgt_question, cq, h1, w_cross_kv, w_cross_out, gain_ff, ahead
):
    rows, width = cq.shape
    pairs = width // 128
    tokens = sum(len(o) for o in order) * shard_rows
    targets = rows // TLEN
    block_rows = query_block(rows, tokens)
    blocks = rows // block_rows
    steps = pairs * blocks

    def body(*refs):
        piece_refs = refs[: len(pieces)]
        (
            tq_ref, cq_ref, h1_ref, wkv_ref, wco_ref, gf_ref,
            enc_out, kv_out, e_ref, inv_out, o2_out, h2_out, a3_ref,
            kfeat, qfeat, ebuf, sem,
        ) = refs[len(pieces) :]
        enc_ref, kv_ref, inv_ref, o2_ref = enc_out.ref, kv_out.ref, inv_out.ref, o2_out.ref
        lane = lax.rem(lax.broadcasted_iota(jnp.int32, (shard_rows, 128), 1), 64).astype(F32)
        for ref, places in zip(piece_refs, order):
            for j, spot in enumerate(places):
                at = slice(spot * shard_rows, (spot + 1) * shard_rows)
                enc_ref[at, :] = ref[j, :shard_rows, :]
                tag = ref[j, shard_rows : shard_rows + 1, :shard_rows].astype(F32)
                tag = jnp.transpose(jnp.broadcast_to(tag, (128, shard_rows)))
                kfeat[at, :] = jnp.where(tag == lane, 0.0, NEG_LARGE).astype(BF)
        lane_t = lax.rem(lax.broadcasted_iota(jnp.int32, (TLEN, 128), 1), 64)
        for t in range(targets):
            qfeat[t * TLEN : (t + 1) * TLEN, :] = jnp.where(lane_t == tq_ref[t], 1.0, 0.0).astype(BF)
        enc_out.flush()

        def project(t, carry):
            at = pl.ds(pl.multiple_of(t * 384, 128), 384)
            kv_ref[:, at] = dot_nn(enc_ref[...], wkv_ref[:, at]).astype(BF)
            return carry

        lax.fori_loop(0, 2 * width // 384, project, 0)
        kv_out.flush()
        q0, q1 = half_masks(block_rows)
        k0, k1 = half_masks(tokens)
        qmask, kmask = (q0, q1), (k0, k1)
        low = lax.broadcasted_iota(jnp.int32, (block_rows, 128), 1) < 64

        def out_copy(slot, step):
            pair, block = step // blocks, lax.rem(step, blocks)
            return pltpu.make_async_copy(
                ebuf.at[slot],
                e_ref.at[pl.ds(2 * pair, 2), pl.ds(block * block_rows, block_rows)],
                sem.at[slot],
            )

        def attend(step, carry):
            slot = lax.rem(step, 2)
            pair, block = step // blocks, lax.rem(step, blocks)
            lo = pl.multiple_of(pair * 128, 128)
            at = pl.ds(pl.multiple_of(block * block_rows, block_rows), block_rows)

            @pl.when(step >= 2)
            def _():
                out_copy(slot, step - 2).wait()

            q = cq_ref[at, pl.ds(lo, 128)]
            k = kv_ref[:, pl.ds(lo, 128)]
            v = kv_ref[:, pl.ds(width + lo, 128)]
            outs = []
            for h in range(2):
                qa = q * qmask[h] + qfeat[at, :] * qmask[1 - h]
                ka = k * kmask[h] + kfeat[...] * kmask[1 - h]
                s = dot_nt(qa, ka)
                top = jnp.max(s, -1, keepdims=True)
                e = jnp.exp(s - top).astype(BF)
                ebuf[slot, h] = e
                outs.append(dot_nn(e, v * kmask[h] + kmask[1 - h]))
            out_copy(slot, step).start()
            total = jnp.where(low, pltpu.roll(outs[0], 64, 1), pltpu.roll(outs[1], 64, 1))
            inv = 1.0 / total
            inv_ref[at, pl.ds(lo, 128)] = inv
            o2_ref[at, pl.ds(lo, 128)] = (jnp.where(low, outs[0], outs[1]) * inv).astype(BF)
            return carry

        lax.fori_loop(0, steps, attend, 0)
        inv_out.flush()
        o2_out.flush()
        h2 = h1_ref[...] + dot_nn(o2_ref[...], wco_ref[...])
        h2_out.ref[...] = h2
        h2_out.flush()
        a3_ref[...] = (h2 * inv_rms(h2) * gf_ref[...]).astype(BF)
        for step in range(max(0, steps - 2), steps):
            out_copy(step % 2, jnp.int32(step)).wait()

    return call(
        "cross_forward",
        body,
        (
            shape_of(BF, tokens, width),
            shape_of(BF, tokens, 2 * width),
            shape_of(BF, 2 * pairs, rows, tokens),
            shape_of(F32, rows, width),
            shape_of(BF, rows, width),
            shape_of(F32, rows, width),
            shape_of(BF, rows, width),
        ),
        [VMEM] * len(pieces) + [SMEM] + [VMEM] * 5,
        (DRAIN, DRAIN, (HBM, ANY), DRAIN, DRAIN, DRAIN, NEAR),
        (*pieces, tgt_question, cq, h1, w_cross_kv, w_cross_out, gain_ff.reshape(1, width)),
        scratch=[
            pltpu.VMEM((tokens, 128), BF),
            pltpu.VMEM((rows, 128), BF),
            pltpu.VMEM((2, 2, block_rows, tokens), BF),
            pltpu.SemaphoreType.DMA((2,)),
        ],
        limit=big(tokens),
        ahead=ahead,
    )


def hidden_gradient(gy, w_ff_out, ahead):
    rows, width = gy.shape
    hidden = w_ff_out.shape[0]

    def body(gy_ref, w2_ref, out_ref):
        def tile(t, carry):
            at = pl.ds(pl.multiple_of(t * width, 128), width)
            out_ref[:, at] = dot_nt(gy_ref[...], w2_ref[at, :]).astype(BF)
            return carry

        lax.fori_loop(0, hidden // width, tile, 0)

    return call(
        "hidden_gradient",
        body,
        shape_of(BF, rows, hidden),
        [VMEM, VMEM],
        NEAR,
        (gy, w_ff_out),
        ahead=ahead,
    )


def feed_hidden(place, a3, gy, dhid, w_ff_in, columns):
    rows, width = a3.shape
    hidden = w_ff_in.shape[1]
    tile = width
    half = width // 2
    sub = hidden // width
    part = columns.part
    per_tile = columns.chunks * tile // hidden
    scale = math.sqrt(2.0 / math.pi)

    def body(place_ref, a3_ref, gy_ref, dhid_ref, w1_ref, dpre_ref, hid_out, both):
        def one(step, carry):
            at = pl.ds(pl.multiple_of(step * tile, 128), tile)
            pre = dot_nn(a3_ref[...], w1_ref[:, at])
            sq = pre * pre
            t = jnp.tanh(pre * (scale + (scale * 0.044715) * sq))
            up = 0.5 + 0.5 * t
            hid = (pre * up).astype(BF)
            slope = up + pre * (up - up * up) * ((2.0 * scale) + (2.0 * scale * 0.134145) * sq)
            hid_out.ref[:, at] = hid
            dpre_ref[:, at] = (dhid_ref[:, at].astype(F32) * slope).astype(BF)
            g = dot_tn(hid, gy_ref[...])
            for h in range(2):
                for i in range(per_tile):
                    for j in range(sub):
                        first = (i * sub + j) * part
                        columns.store(
                            both.ref, h, "out", g[first : first + part, h * half : (h + 1) * half],
                            place_ref, [step * per_tile + i], j * half // 128,
                        )
            return carry

        lax.fori_loop(0, hidden // tile, one, 0)

    return call(
        "feed_hidden",
        body,
        (shape_of(BF, rows, hidden), shape_of(BF, rows, hidden), columns.shape(), columns.shape()),
        [SMEM, VMEM, VMEM, VMEM, VMEM],
        (NEAR, DRAIN, PAIR, PAIR),
        (place, a3, gy, dhid, w_ff_in),
    )


def feed_weights(place, a3, dpre, columns, ahead):
    width = a3.shape[1]
    hidden = dpre.shape[1]

    def body(place_ref, a3_ref, dpre_ref, both):
        tiles = hidden // width

        def one(t, carry):
            at = pl.ds(pl.multiple_of(t * width, 128), width)
            g = dot_tn(a3_ref[...], dpre_ref[:, at])
            block = lax.rem(t, tiles // 2) * (width // 128)
            columns.store(both.ref, t // (tiles // 2), "in", g, place_ref, None, block)
            return carry

        lax.fori_loop(0, tiles, one, 0)

    return call(
        "feed_weights",
        body,
        (columns.shape(), columns.shape()),
        [SMEM, VMEM, VMEM],
        (PAIR, PAIR),
        (place, a3, dpre),
        ahead=ahead,
    )


def feed_back(dpre, w_ff_in, h2, gain_ff, gy):
    rows, width = h2.shape

    def body(dpre_ref, w1_ref, h2_ref, gf_ref, gy_ref, dh2_ref, gain_ref, da3):
        da3[...] = jnp.zeros_like(da3)

        def one(t, carry):
            at = pl.ds(pl.multiple_of(t * width, 128), width)
            da3[...] += dot_nt(dpre_ref[:, at], w1_ref[:, at])
            return carry

        lax.fori_loop(0, dpre_ref.shape[1] // width, one, 0)
        dv, dgain = rms_back(da3[...], h2_ref[...], gf_ref[...])
        dh2_ref[...] = gy_ref[...].astype(F32) + dv
        gain_ref[...] = dgain

    return call(
        "feed_back",
        body,
        (shape_of(F32, rows, width), shape_of(F32, 1, width)),
        [VMEM] * 5,
        (NEAR, VMEM),
        (dpre, w_ff_in, h2, gain_ff.reshape(1, width), gy),
        scratch=[pltpu.VMEM((rows, width), F32)],
    )


def feed_out(hid, w_ff_out, h2, ahead):
    rows, width = h2.shape

    def body(hid_ref, w2_ref, h2_ref, out, total):
        total[...] = h2_ref[...]

        def one(t, carry):
            at = pl.ds(pl.multiple_of(t * width, 128), width)
            total[...] += dot_nn(hid_ref[:, at], w2_ref[at, :])
            return carry

        lax.fori_loop(0, hid_ref.shape[1] // width, one, 0)
        out.ref[...] = total[...].astype(BF)

    return call(
        "feed_out",
        body,
        (shape_of(BF, rows, width),),
        [VMEM] * 3,
        (DRAIN,),
        (hid, w_ff_out, h2),
        scratch=[pltpu.VMEM((rows, width), F32)],
        ahead=ahead,
    )


def cross_backward(first_pair, last_pair, dh2, o2, inv, cq, kv, e, w_cross_out, ahead):
    rows, width = cq.shape
    pairs = width // 128
    count = last_pair - first_pair
    tokens = kv.shape[0]
    block_rows = query_block(rows, tokens)
    blocks = rows // block_rows

    def body(
        dh2_ref, wco_ref, o2_ref, inv_ref, cq_ref, k_ref, v_ref, e_ref,
        dcq_ref, dkt_ref, dvt_ref,
        do2,
    ):
        pair = pl.program_id(0)

        @pl.when(pair == 0)
        def _():
            do2v = dot_nt(dh2_ref[...].astype(BF), wco_ref[...]).astype(BF)
            for i in range(count):
                do2[i] = do2v[:, i * 128 : (i + 1) * 128]

        q0, q1 = half_masks(block_rows)
        k0, k1 = half_masks(tokens)
        qmask, kmask = (q0, q1), (k0, k1)
        lane = lax.broadcasted_iota(jnp.int32, (block_rows, 128), 1)
        low = lane < 64
        first = lax.rem(lane, 64) == 0
        second = lax.rem(lane, 64) == 1
        k, v = k_ref[...], v_ref[...]
        sums = [0.0] * 4
        for block in range(blocks):
            at = slice(block * block_rows, (block + 1) * block_rows)
            q = cq_ref[at, :]
            dof = do2[pair, at, :].astype(F32) * inv_ref[at, :]
            dob = dof.astype(BF)
            prod = dof * o2_ref[at, :].astype(F32)
            qt = jnp.transpose(q)
            dot_t = jnp.transpose(dob)
            dqs = []
            for h in range(2):
                own = low if h == 0 else jnp.logical_not(low)
                delta = -jnp.sum(jnp.where(own, prod, 0.0), -1, keepdims=True)
                hi = delta.astype(BF).astype(F32)
                feat = jnp.where(first, hi, jnp.where(second, delta - hi, 0.0)).astype(BF)
                doa = dob * qmask[h] + feat * qmask[1 - h]
                dp = dot_nt(doa, v * kmask[h] + kmask[1 - h])
                ev = e_ref[h, at, :]
                ds = (ev.astype(F32) * dp).astype(BF)
                dqs.append(dot_nn(ds, k))
                sums[h] = sums[h] + dot_nn(qt[h * 64 : (h + 1) * 64, :], ds)
                sums[2 + h] = sums[2 + h] + dot_nn(dot_t[h * 64 : (h + 1) * 64, :], ev)
            dcq_ref[at, :] = jnp.where(low, dqs[0], dqs[1]).astype(BF)
        for h in range(2):
            dkt_ref[h * 64 : (h + 1) * 64, :] = sums[h].astype(BF)
            dvt_ref[h * 64 : (h + 1) * 64, :] = sums[2 + h].astype(BF)

    near = HBM if big(tokens) else NEAR

    def column(n, first=first_pair):
        return pl.BlockSpec((n, 128), lambda p: (0, p + first))

    return call(
        "cross_backward",
        body,
        (
            shape_of(BF, rows, count * 128),
            shape_of(BF, count * 128, tokens),
            shape_of(BF, count * 128, tokens),
        ),
        [
            whole(rows, width),
            pl.BlockSpec((count * 128, width), lambda p: (first_pair // count, 0)),
            (HBM, column(rows)),
            (HBM, column(rows)),
            (HBM, column(rows)),
            (HBM, column(tokens)),
            (HBM, column(tokens, first_pair + pairs)),
            (HBM, pl.BlockSpec((2, rows, tokens), lambda p: (p + first_pair, 0, 0))),
        ],
        (
            (NEAR, column(rows, 0)),
            (near, pl.BlockSpec((128, tokens), lambda p: (p, 0))),
            (near, pl.BlockSpec((128, tokens), lambda p: (p, 0))),
        ),
        (dh2, w_cross_out, o2, inv, cq, kv, kv, e),
        scratch=[pltpu.VMEM((count, rows, 128), BF)],
        grid=(count,),
        ahead=ahead,
        limit=big(tokens),
    )


def cross_query_back(dcq, w_cross_q, h1, gain_cross, dh2):
    rows, width = h1.shape
    n = len(dcq)
    size = width // n

    def body(*refs):
        wcq_ref, h1_ref, gc_ref, dh2_ref, dh1_ref, gain_ref = refs[n:]
        da2 = 0.0
        for i in range(n):
            da2 = da2 + dot_nt(refs[i][...], wcq_ref[:, i * size : (i + 1) * size])
        dv, dgain = rms_back(da2, h1_ref[...], gc_ref[...])
        dh1_ref[...] = dh2_ref[...] + dv
        gain_ref[...] = dgain

    return call(
        "cross_query_back",
        body,
        (shape_of(F32, rows, width), shape_of(F32, 1, width)),
        [VMEM] * (n + 4),
        (NEAR, VMEM),
        (*dcq, w_cross_q, h1, gain_cross.reshape(1, width), dh2),
    )


def shard_rows_of(tokens, chunks):
    return tokens // chunks


def cross_weights(place, dh2, o2, dcq, dkt, dvt, enc, a2, w_cross_kv, dh1, o1, columns, ahead):
    rows, width = dh2.shape
    tokens = enc.shape[0]
    half = width // 2
    tile = max(shard_rows_of(tokens, columns.chunks), 512)
    n = len(dcq)
    size = width // n
    blocks = width // 128
    shard_rows = tokens // columns.chunks

    def body(place_ref, dh2_ref, dh1_ref, a2_ref, o2_ref, o1_ref, *refs):
        dcq_refs, dkt, dvt = refs[:n], refs[n : 2 * n], refs[2 * n : 3 * n]
        wkv_ref, enc_ref, genc_out, both, lhs, rhs, dkvt = refs[3 * n :]
        for i, r in enumerate(dcq_refs):
            rhs[0, :, i * size : (i + 1) * size] = r[...]
        rhs[1] = dh2_ref[...].astype(BF)
        rhs[2] = dh1_ref[...].astype(BF)
        for i, r in enumerate((a2_ref, o2_ref, o1_ref)):
            lhs[i] = r[...]
        for i, r in enumerate(dkt + dvt):
            dkvt[i * size : (i + 1) * size, :] = r[...]

        def square(i, carry):
            g = dot_tn(lhs[i], rhs[i])
            for h in range(2):
                columns.store(both.ref, h, "q", g[:, h * half : (h + 1) * half], place_ref, None, i * (half // 128))
            return carry

        lax.fori_loop(0, 3, square, 0)

        def encodings(t, carry):
            at = pl.ds(pl.multiple_of(t * tile, 128), tile)
            genct = dot_nn(wkv_ref[...], dkvt[:, at]).astype(BF)
            for i in range(tile // shard_rows):
                spot = t * (tile // shard_rows) + i
                for j in range(blocks):
                    genc_out.ref[spot * blocks + j] = genct[
                        j * 128 : (j + 1) * 128, i * shard_rows : (i + 1) * shard_rows
                    ]
            return carry

        lax.fori_loop(0, tokens // tile, encodings, 0)
        genc_out.flush()

        def key_value(h, carry):
            g = 0.0
            rows_at = pl.ds(pl.multiple_of(h * width, 128), width)
            for t in range(0, tokens, 1024):
                end = min(tokens, t + 1024)
                g = g + dot_nt(jnp.transpose(enc_ref[t:end, :]), dkvt[rows_at, t:end])
            columns.store(both.ref, h, "kv", g, place_ref)
            return carry

        lax.fori_loop(0, 2, key_value, 0)

    return call(
        "cross_weights",
        body,
        (shape_of(BF, columns.chunks * blocks, 128, shard_rows), columns.shape(), columns.shape()),
        [SMEM] + [VMEM] * (3 * n + 7),
        (DRAIN, PAIR, PAIR),
        (place, dh2, dh1, a2, o2, o1, *dcq, *dkt, *dvt, w_cross_kv, enc),
        scratch=[
            pltpu.VMEM((3, rows, width), BF),
            pltpu.VMEM((3, rows, width), BF),
            pltpu.VMEM((2 * width, tokens), BF),
        ],
        ahead=ahead,
        limit=big(tokens),
    )


def self_backward(dh1, w_self_out, qkv, p1, bucket_count, heads, ahead):
    rows, width = dh1.shape
    pairs = heads // 2
    groups = rows // GROUP
    firsts = bucket_firsts(bucket_count)
    ends = [first for _, first in firsts[1:]] + [TLEN]

    def body(dh1_ref, wso_ref, qkv_ref, p1_ref, dqkv_ref, gbias_ref, do1, acc):
        do1[...] = dot_nt(dh1_ref[...].astype(BF), wso_ref[...]).astype(BF)
        m0, m1 = half_masks(GROUP)
        acc[...] = jnp.zeros_like(acc)

        def attend(g, carry):
            at = pl.ds(pl.multiple_of(g * GROUP, GROUP), GROUP)
            for pair in range(pairs):
                lo = pair * 128
                q = qkv_ref[at, lo : lo + 128]
                k = qkv_ref[at, width + lo : width + lo + 128]
                v = qkv_ref[at, 2 * width + lo : 2 * width + lo + 128]
                do = do1[at, lo : lo + 128]
                do_two = jnp.concatenate([do * m0, do * m1], 0)
                pb = p1_ref[g, pair]
                pf = pb.astype(F32)
                dp = dot_nt(do_two, v)
                ds = (pf * (dp - jnp.sum(pf * dp, -1, keepdims=True))).astype(BF)
                dsf = ds.astype(F32)
                for h in range(2):
                    total = dsf[h * GROUP : h * GROUP + TLEN]
                    for t in range(1, GROUP // TLEN):
                        total = total + dsf[h * GROUP + t * TLEN : h * GROUP + (t + 1) * TLEN]
                    acc[2 * pair + h] += total
                dq = dot_nn(
                    jnp.concatenate([ds[:GROUP], ds[GROUP:]], 1),
                    jnp.concatenate([k * m0, k * m1], 0),
                )
                dk = dot_tn(ds, jnp.concatenate([q * m0, q * m1], 0))
                dv = dot_tn(pb, do_two)
                dqkv_ref[at, lo : lo + 128] = dq.astype(BF)
                dqkv_ref[at, width + lo : width + lo + 128] = dk.astype(BF)
                dqkv_ref[at, 2 * width + lo : 2 * width + lo + 128] = dv.astype(BF)
            return carry

        lax.fori_loop(0, groups, attend, 0)
        row = lax.broadcasted_iota(jnp.int32, (TLEN, GROUP), 0)
        distance = row - lax.rem(lax.broadcasted_iota(jnp.int32, (TLEN, GROUP), 1), TLEN)
        lane = lax.broadcasted_iota(jnp.int32, (16, 128), 1)
        bias = jnp.zeros((16, 128), F32)
        accv = acc[...]
        pad = jnp.zeros((16 - heads, 1), F32)
        for (b, first), end in zip(firsts, ends):
            here = jnp.logical_and(distance >= first, distance < end)
            part_sum = jnp.sum(jnp.where(here[None], accv, 0.0), axis=1)
            col = jnp.sum(part_sum, -1, keepdims=True)
            bias = jnp.where(lane == b, jnp.concatenate([col, pad], 0), bias)
        gbias_ref[...] = bias

    return call(
        "self_backward",
        body,
        (shape_of(BF, rows, 3 * width), shape_of(F32, 16, 128)),
        [VMEM] * 4,
        (NEAR, VMEM),
        (dh1, w_self_out, qkv, p1),
        ahead=ahead,
        scratch=[pltpu.VMEM((rows, width), BF), pltpu.VMEM((heads, TLEN, GROUP), F32)],
    )


def self_weights(
    place, dh1, a1, dqkv, x, gain_self, w_qkv, gbias, gain_cross_grad, gain_ff_grad, columns
):
    rows, width = dh1.shape
    half = width // 2
    part = columns.part
    misc_rows = 16 + width // 16
    more = -(-misc_rows // part)

    def body(
        place_ref, dh1_ref, wqkv_ref, x_ref, a1_ref, dqkv_ref, gs_ref, gb_ref, ggc_ref, ggf_ref,
        out, both, da1,
    ):
        da1[...] = jnp.zeros_like(da1)

        def one(t, carry):
            at = pl.ds(pl.multiple_of(t * width, 128), width)
            da1[...] += dot_nt(dqkv_ref[:, at], wqkv_ref[:, at])
            return carry

        lax.fori_loop(0, 3, one, 0)
        dv, dgain = rms_back(da1[...], x_ref[...].astype(F32), gs_ref[...])
        out.ref[...] = dh1_ref[...] + dv
        out.flush()

        def weights(h, carry):
            at = pl.ds(pl.multiple_of(h * 3 * half, 128), 3 * half)
            columns.store(both.ref, h, "qkv", dot_tn(a1_ref[...], dqkv_ref[:, at]), place_ref)
            return carry

        lax.fori_loop(0, 2, weights, 0)
        gains = jnp.concatenate([dgain, ggc_ref[...], ggf_ref[...], jnp.zeros((5, width), F32)], 0)
        misc = [gb_ref[...]] + [gains[:, j * 128 : (j + 1) * 128] for j in range(width // 128)]
        misc.append(jnp.zeros((more * part - misc_rows, 128), F32))
        misc = jnp.concatenate(misc, 0).astype(BF)
        for i in range(more):
            for slot in range(2):
                both.ref[slot, columns.units + i] = misc[i * part : (i + 1) * part]

    return call(
        "self_weights",
        body,
        (shape_of(F32, rows, width), columns.shape(more), columns.shape(more)),
        [SMEM] + [VMEM] * 9,
        (DRAIN, PAIR, PAIR),
        (
            place, dh1, w_qkv, x, a1, dqkv, gain_self.reshape(1, width), gbias,
            gain_cross_grad, gain_ff_grad,
        ),
        scratch=[pltpu.VMEM((rows, width), F32)],
    )


def swap(value, axis, bit):
    size = lax.axis_size(axis)
    return lax.ppermute(value, axis, [(i, i ^ bit) for i in range(size)])


class Bucket:
    def __init__(self, rows, terms, steps, keep_all=False):
        self.rows, self.terms, self.steps, self.keep_all = rows, terms, list(steps), keep_all


def sum_kernel(groups, dtype=BF):
    operands, specs, plan = [], [], []
    for i, jobs in enumerate(groups):
        at = 0
        for rows, terms in jobs:
            plan.append((i, at, rows, len(operands), len(terms)))
            at += rows
            for array, off in terms:
                operands.append(array)
                spec = (pl.Element(rows), pl.Element(128))
                specs.append(pl.BlockSpec(spec, functools.partial(lambda off, *_: (off, 0), off)))
    sizes = [sum(rows for rows, _ in jobs) for jobs in groups]

    def body(*refs):
        outs = refs[len(operands) :]
        for i, at, rows, first, count in plan:
            total = refs[first][...].astype(F32)
            for r in refs[first + 1 : first + count]:
                total = total + r[...].astype(F32)
            outs[i][at : at + rows, :] = total.astype(dtype)

    return call(
        "sum_kernel",
        body,
        tuple(shape_of(dtype, size, 128) for size in sizes),
        specs,
        tuple(whole(size, 128) for size in sizes),
        operands,
        grid=(1,),
    )


def send_round(cost, *members, settle=()):
    groups = {}
    for m in members:
        step = m.steps[0]
        groups.setdefault((step, m) if isinstance(m, Total) else step, []).append(m)
    jobs = []
    for group in groups.values():
        jobs.append([])
        for m in group:
            if isinstance(m, Total):
                jobs[-1] += m.next_jobs()
            elif m.keep_all:
                jobs[-1].append((m.rows, m.terms))
            else:
                m.rows //= 2
                jobs[-1].append((m.rows, [(array, off + m.rows) for array, off in m.terms]))
    settle = [b for b in settle if not b.steps]
    if settle:
        jobs.append([(b.rows, b.terms) for b in settle])
    sent = sum_kernel(jobs)
    at = 0
    for b in settle:
        b.terms = [(sent[-1], at)]
        at += b.rows
    for group, payload in zip(groups.values(), sent):
        axis, bit = group[0].steps[0]
        got = swap(payload, axis, bit)
        at = 0
        for m in group:
            m.steps.pop(0)
            if isinstance(m, Total):
                m.moved(payload, got)
                continue
            if m.keep_all:
                m.terms = [(payload, at), (got, at)]
            else:
                m.terms = m.terms + [(got, at)]
            at += m.rows
    shadow(cost)


def rest_of(*buckets):
    while any(b.steps for b in buckets):
        send_round(3, *[b for b in buckets if b.steps])


def weight_buckets(columns, keep, send, orders, y_bits):
    rows = columns.units * columns.part
    keep, send = in_hbm(keep.reshape(-1, 128)), send.reshape(-1, 128)
    got = swap(send, "dp", 1)
    over = [[("blk", b) for b in order] for order in orders]
    along = [("dp", 2 * b) for b in y_bits]
    buckets = []
    for _, blocks, order, unit in columns.sections:
        steps = along + over[0] if order == "y" else over[order]
        at = unit * columns.part
        size = blocks * columns.chunks * columns.part
        buckets.append(Bucket(size, [(keep, at), (got, at)], steps))
    if keep.shape[0] > rows:
        buckets.append(Bucket(keep.shape[0] - rows, [(keep, rows), (got, rows)], over[0], keep_all=True))
    return buckets


def join_encodings(buckets, shard_rows, width):
    terms = [(bucket, array, off) for bucket in buckets for array, off in bucket.terms]

    def body(*refs):
        out = refs[-1]
        first = col = 0
        for bucket in buckets:
            mine = refs[first : first + len(bucket.terms)]
            first += len(bucket.terms)
            for at in range(0, bucket.rows, 128):
                total = mine[0][at : at + 128, :].astype(F32)
                for r in mine[1:]:
                    total = total + r[at : at + 128, :].astype(F32)
                out[:, col : col + 128] = jnp.transpose(total)
                col += 128

    return call(
        "join_encodings",
        body,
        shape_of(F32, shard_rows, width),
        [
            pl.BlockSpec(
                (pl.Element(bucket.rows), pl.Element(shard_rows)),
                functools.partial(lambda off, *_: (off, 0), off),
            )
            for bucket, _, off in terms
        ],
        whole(shard_rows, width),
        [array for _, array, _ in terms],
        grid=(1,),
    )


class Total:
    def __init__(self, groups, small, dp_size):
        self.groups, self.small, self.dp_size = groups, small, dp_size
        self.jobs, self.bases = [], []
        at = 0
        for _, buckets in groups:
            base = []
            for bucket in buckets:
                self.jobs.append((bucket.rows, bucket.terms))
                base.append(at)
                at += bucket.rows
            self.bases.append(base)
        self.small_at = []
        for bucket in small:
            self.jobs.append((bucket.rows, bucket.terms))
            self.small_at.append((at, bucket.rows))
            at += bucket.rows
        self.rows = at
        self.steps = [("dp", 2 * m) for m in range(1, dp_size // 2)] + [("dp", 1)]
        self.parts = []

    def next_jobs(self):
        if len(self.steps) > 1 or not self.parts:
            return [(self.rows, [(self.parts[0], 0)])] if self.parts else self.jobs
        jobs, self.spots, at = [], [], 0
        for (columns, _), base in zip(self.groups, self.bases):
            spots = []
            for (_, blocks, order, _), first in zip(columns.sections, base):
                if order == "y":
                    rows = blocks // columns.y_parts * columns.part
                    spots.append([at + i * rows for i in range(len(self.parts))])
                    jobs += [(rows, [(p, first)]) for p in self.parts]
                    at += rows * len(self.parts)
                else:
                    rows = blocks * columns.part
                    spots.append(at)
                    jobs.append((rows, [(p, first) for p in self.parts]))
                    at += rows
            self.spots.append(spots)
        self.small_spots = []
        for first, rows in self.small_at:
            jobs.append((rows, [(p, first) for p in self.parts]))
            self.small_spots.append((at, rows))
            at += rows
        return jobs

    def moved(self, payload, got):
        if self.steps or not self.parts:
            self.parts = self.parts + [got] if self.parts else [payload, got]
        else:
            self.own, self.other = payload, got

    def finish(self, place, arrays):
        outs = []
        for (columns, _), spots, named in zip(self.groups, self.spots, arrays):
            for name, stack in named:
                outs.append((columns, spots, name, stack, dict(columns.names)[name] // stack))
        y_parts = self.dp_size // 2

        def body(place_ref, own_ref, other_ref, *refs):
            core, y = place_ref[0], place_ref[2]
            sides = ((core, own_ref), (1 - core, other_ref))

            def put(ref, columns, half, j, at):
                row, off = divmod(j * 128, half)
                for which, src in sides:
                    lane = pl.multiple_of(which * half + off, 128)
                    ref[row * columns.part : (row + 1) * columns.part, pl.ds(lane, 128)] = src[
                        at : at + columns.part, :
                    ].astype(F32)

            for ref, (columns, spots, name, stack, half) in zip(refs, outs):
                far = []
                for j in range(stack * half // 128):
                    i, y_of, k = columns.find(columns.first(name) + j)
                    if y_of is None:
                        put(ref, columns, half, j, spots[i] + k * columns.part)
                    else:
                        far.append((j, spots[i], y_of, k))
                for y_is in range(y_parts if far else 0):

                    @pl.when(y == y_is)
                    def _():
                        for j, at, y_of, k in far:
                            put(ref, columns, half, j, at[y_is ^ y_of] + k * columns.part)

            for ref, (at, rows) in zip(refs[len(outs) :], self.small_spots):
                ref[...] = own_ref[at : at + rows, :].astype(F32)

        shapes = [shape_of(F32, stack * columns.part, 2 * half) for columns, _, _, stack, half in outs]
        shapes += [shape_of(F32, rows, 128) for _, rows in self.small_spots]
        return call(
            "finish",
            body,
            tuple(shapes),
            [SMEM, VMEM, VMEM],
            (VMEM,) * len(shapes),
            (place, self.own, self.other),
        )


def gather_encodings(own, bits):
    if len(bits) == 3:
        x, z, far = bits
        r_far, r_x = swap(own, "blk", far), swap(own, "blk", x)

        def second():
            r_z, r_zf = swap(own, "blk", z), swap(r_far, "blk", z)
            r_xf = swap(r_far, "blk", x)

            def third():
                r_xz = swap(r_z, "blk", x)
                r_xzf = swap(r_xf, "blk", z)
                arrays = [own, r_far, r_x, r_z, r_zf, r_xf, r_xz, r_xzf]
                return arrays, [[0], [far], [x], [z], [z | far], [x | far], [x | z], [x | z | far]]

            return [r_z, r_zf, r_xf], third

        return [r_far, r_x], second
    got, rel = own, [0]
    for bit in reversed(bits):
        got = jnp.concatenate([got, swap(got, "blk", bit)], 0)
        rel = rel + [r ^ bit for r in rel]
    return [], lambda: ([], lambda: ([got], [rel]))


def local(
    dec_in,
    encodings,
    enc_question,
    enc_valid,
    tgt_question,
    gain_self,
    w_qkv,
    rel_bias,
    w_self_out,
    gain_cross,
    w_cross_q,
    w_cross_kv,
    w_cross_out,
    gain_ff,
    w_ff_in,
    w_ff_out,
    grad_out,
):
    x = dec_in[0]
    gy = grad_out[0]
    rows, width = x.shape
    bucket_count, heads = rel_bias.shape
    hidden = w_ff_in.shape[1]
    half = width // 2
    chunks = lax.axis_size("blk")
    part = width // chunks
    dp_size = lax.axis_size("dp")
    shard_rows = encodings.shape[1]
    bits = [1 << i for i in range(chunks.bit_length() - 1)]
    y_bits = [1 << i for i in range(dp_size.bit_length() - 2)]
    y_parts = dp_size // 2
    blk = lax.axis_index("blk")
    dp = lax.axis_index("dp")
    orders = [bits, bits[1::-1] + bits[2:]]

    def layout(names, *sections):
        return Columns(names, sections, y_parts, chunks, part)

    def along_y(blocks):
        return blocks // (2 * y_parts) * y_parts

    stack = hidden // width
    blocks = half // 128
    cols_out = layout([("out", stack * half)], (stack * blocks, "y"))
    cols_in = layout([("in", hidden // 2)], (stack * blocks // 2, 0), (stack * blocks // 2, 1))
    far_x, far_s = along_y(16 * blocks // 3), along_y(3 * blocks)
    near_x, near_s = 5 * blocks - far_x, 3 * blocks - far_s
    cols_x = layout(
        [("q", half), ("out", half), ("self", half), ("kv", width)],
        (near_x, 0), (far_x, "y"),
    )
    cols_s = layout([("qkv", 3 * half)], (near_s, 0), (far_s, "y"))

    places = [[chunk_place(c, blk, order) for c in range(chunks)] for order in orders]
    y_places = [chunk_place(y, dp // 2, y_bits) for y in range(y_parts)]
    numbers = [lax.rem(dp, 2), blk, dp // 2]
    for columns in (cols_out, cols_in, cols_x, cols_s):
        columns.at = len(numbers)
        numbers += columns.table(places, y_places)
    place = jnp.stack(numbers).astype(jnp.int32)

    ORDER.clear()
    ROOMY[:] = [chunks * shard_rows <= 1024]
    tags = jnp.where(enc_valid[0] == 1, enc_question[0], -1).astype(BF)
    tag_rows = jnp.zeros((16, width), BF).at[0, :shard_rows].set(tags)
    enc_own = jnp.concatenate([encodings[0], tag_rows], 0)[None]
    got, second = gather_encodings(enc_own, bits)
    shadow(10)
    a1, qkv, p1, o1_near, o1, wso_near, wcq_near, x_near = self_attention(
        x, gain_self, w_qkv, rel_bias, [w_self_out, w_cross_q, x]
    )
    more, third = second()
    shadow(10)
    h1_near, cq_near, h1, a2, cq, w2_near, gy = self_project(
        x_near, o1_near, wso_near, gain_cross, wcq_near, [w_ff_out, gy]
    )
    pieces, rel = third()
    shadow(10)
    dhid, wkv_near, wco_near = hidden_gradient(gy, w2_near, [w_cross_kv, w_cross_out])
    spots = [[int(chunk_spot(r, bits)) for r in group] for group in rel]
    enc, kv, e, inv, o2, h2, a3, w1_near = cross_forward(
        pieces, spots, shard_rows, tgt_question[0], cq_near, h1_near, wkv_near, wco_near, gain_ff, [w_ff_in]
    )

    dpre, hid, keep, send = feed_hidden(place, a3, gy, dhid, w1_near, cols_out)
    (b_out,) = weight_buckets(cols_out, keep, send, orders, y_bits)
    shadow(30)
    keep, send, h2_near = feed_weights(place, a3, dpre, cols_in, [h2])
    b_in, b_jn = weight_buckets(cols_in, keep, send, orders, y_bits)
    send_round(30, b_out)
    dh2, gain_ff_grad = feed_back(dpre, w1_near, h2_near, gain_ff, gy)
    send_round(8, b_in, b_jn)
    pairs = heads // 2
    parts_a = cross_backward(0, pairs // 2, dh2, o2, inv, cq, kv, e, wco_near, [])
    parts_b = cross_backward(
        pairs // 2, pairs, dh2, o2, inv, cq, kv, e, wco_near, [w_cross_q, h1, a2, o2, o1, enc, w_cross_kv]
    )
    wcq_near, h1_near, a2, o2, o1, enc, wkv_near = parts_b[3:]
    dcq, dkt, dvt = zip(parts_a, parts_b[:3])
    dh1, gain_cross_grad = cross_query_back(dcq, wcq_near, h1_near, gain_cross, dh2)
    send_round(12, b_jn, b_out, b_in)
    genc, keep, send, hid, w2_near, h2_near = cross_weights(
        place, dh2, o2, dcq, dkt, dvt, enc, a2, wkv_near, dh1, o1, cols_x, [hid, w_ff_out, h2]
    )
    enc_rows = chunks * shard_rows * width // 128
    b_enc = Bucket(
        enc_rows, [(in_hbm(genc.reshape(enc_rows, shard_rows)), 0)], [("blk", b) for b in bits]
    )
    b_xa, b_xb = weight_buckets(cols_x, keep, send, orders, y_bits)
    out, wso_near, qkv, p1 = feed_out(hid, w2_near, h2_near, [w_self_out, qkv, p1])
    send_round(40, b_in, b_jn, b_enc, b_out)
    dqkv, gbias, wqkv_near, x_near, a1 = self_backward(
        dh1, wso_near, qkv, p1, bucket_count, heads, [w_qkv, x, a1]
    )
    send_round(8, b_xa, b_xb, b_enc, b_out, settle=[b_in, b_jn])
    grad_dec, keep, send = self_weights(
        place, dh1, a1, dqkv, x_near, gain_self, wqkv_near, gbias, gain_cross_grad, gain_ff_grad, cols_s
    )
    b_sa, b_sb, b_misc = weight_buckets(cols_s, keep, send, orders, y_bits)
    send_round(25, b_xa, b_xb, b_enc, settle=[b_out])
    send_round(4, b_sa, b_misc, b_sb)
    rest_of(b_out, b_in, b_jn)
    total_ff = Total([(cols_out, [b_out]), (cols_in, [b_in, b_jn])], [], dp_size)
    send_round(4, b_xa, b_xb, total_ff)
    rest_of(b_enc)
    send_round(4, b_sa, b_misc, b_sb)
    send_round(4, b_xb, b_sa, b_misc, total_ff)
    grad_enc = join_encodings([b_enc], shard_rows, width)
    send_round(4, b_sb)
    rest_of(total_ff)
    grad_ff_out, grad_ff_in = total_ff.finish(place, [[("out", stack)], [("in", 1)]])
    rest_of(b_xa, b_xb)
    total_x = Total([(cols_x, [b_xa, b_xb])], [], dp_size)
    send_round(4, total_x)
    send_round(4, b_sb)
    rest_of(b_sa, b_sb, b_misc)
    total_s = Total([(cols_s, [b_sa, b_sb])], [b_misc], dp_size)
    send_round(4, total_s, total_x)
    rest_of(total_s, total_x)
    grad_cross_out, grad_cross_q, grad_self_out, grad_cross_kv = total_x.finish(
        place, [[("out", 1), ("q", 1), ("self", 1), ("kv", 1)]]
    )
    grad_qkv, misc = total_s.finish(place, [[("qkv", 1)]])
    gains = misc[16 : 16 + width // 16].reshape(width // 128, 8, 128)[:, :3].transpose(1, 0, 2).reshape(3, width)
    gains = lax.dynamic_slice(gains, (0, blk * part), (3, part))
    bias_part = bucket_count // chunks
    grad_bias = lax.dynamic_slice(misc, (0, blk * bias_part), (heads, bias_part)).T
    return (
        out[None],
        grad_dec[None],
        grad_enc[None],
        gains[0],
        grad_qkv,
        grad_bias,
        grad_self_out,
        gains[1],
        grad_cross_q,
        grad_cross_kv,
        grad_cross_out,
        gains[2],
        grad_ff_in,
        grad_ff_out,
    )


def solution(mesh):
    return jax.shard_map(
        local,
        mesh=mesh,
        in_specs=(
            P("dp", "blk", None),
            P("dp", "blk", None),
            P("dp", "blk"),
            P("dp", "blk"),
            P("dp", "blk"),
            P(),
            P(),
            P(),
            P(),
            P(),
            P(),
            P(),
            P(),
            P(),
            P(),
            P(),
            P("dp", "blk", None),
        ),
        out_specs=(
            P("dp", "blk", None),
            P("dp", "blk", None),
            P("dp", "blk", None),
            P("blk"),
            P("blk", None),
            P("blk", None),
            P("blk", None),
            P("blk"),
            P("blk", None),
            P("blk", None),
            P("blk", None),
            P("blk"),
            P("blk", None),
            P("blk", None),
        ),
        check_vma=False,
    )
```

profile of v0, /device:TPU:1, one launch (start us, length us, event | category | flops | bytes accessed | tf_op | source)
XLA Modules:
  0.0 244.5 jit_solution(1274077830019409382)
XLA Ops:
  2.3 3.2 %collective-permute-start = (bf16[1,144,768]{2,1,0:T(8,128)(2,1)S(1)}, bf16[1,144,768]{2,1,0:T(8,128)(2,1)S(1)}, u32[]{:S(2)}, u32[]{:S(2)}) collective-permute-start(bf16[1,144,768]{2,1,0:T(8,128)(2,1)S(1)} %fusion.2.refs_0_), channel_id=1, source_target_pairs={{0,4},{1,5},{2,6},{3,7},{4,0},{5,1},{6,2},{7,3},{8,12},{9,13},{10,... | collective-permute-start | bytes 663560 | tf_op jit(solution)/shard_map/ppermute | solution.py:1007
  8.0 13.0 %self_attention.1 = (bf16[512,768]{1,0:T(8,128)(2,1)}, bf16[512,2304]{1,0:T(8,128)(2,1)}, bf16[4,6,256,128]{3,2,1,0:T(8,128)(2,1)}, bf16[512,768]{1,0:T(8,128)(2...) custom-call(bf16[512,768]{1,0:T(8,128)(2,1)} %bitcast.458, ...), custom_call_target="tpu_custom_call" | custom-call | flops 1153000 | tf_op jit(solution)/shard_map/self_attention/pallas_call | solution.py:236
  22.1 4.5 %self_project.1 = (f32[512,768]{1,0:T(8,128)S(1)}, bf16[512,768]{1,0:T(8,128)(2,1)S(1)}, f32[512,768]{1,0:T(8,128)}, bf16[512,768]{1,0:T(8,128)(2,1)}, bf16[512,...) custom-call(bf16[512,768]{1,0:T(8,128)(2,1)S(1)} %get-tuple-element.167.refs_0, ...), custom_call_target="tpu_custom_call" | custom-call | flops 1153000 | tf_op jit(solution)/shard_map/self_project/pallas_call | solution.py:236
  33.0 3.3 %hidden_gradient.1 = (bf16[512,3072]{1,0:T(8,128)(2,1)S(1)}, bf16[768,1536]{1,0:T(8,128)(2,1)S(1)}, bf16[768,768]{1,0:T(8,128)(2,1)S(1)}, f32[8,128]{1,0:T(8,128)}) custom-call(bf16[512,768]{1,0:T(8,128)(2,1)S(1)} %get-tuple-element.174.refs_0_.refs_2_.refs_4_, bf16[3072,768]{1,0:T(8,128)(2,1)S(1)} %copy-done.1, bf16[768,1536]{1,0:T(8,128)(2,1)} %refs_14_.3, ...), custom_call_target="tpu_custom_call" | custom-call | flops 1153000 | tf_op jit(solution)/shard_map/hidden_gradient/pallas_call | solution.py:236
  36.7 19.9 %cross_forward.1 = (bf16[1024,768]{1,0:T(8,128)(2,1)}, bf16[1024,1536]{1,0:T(8,128)(2,1)}, bf16[12,512,1024]{2,1,0:T(8,128)(2,1)}, f32[512,768]{1,0:T(8,128)}, b...) custom-call(bf16[1,144,768]{2,1,0:T(8,128)(2,1)S(1)} %fusion.2.refs_, ...), custom_call_target="tpu_custom_call" | custom-call | flops 1153000 | tf_op jit(solution)/shard_map/cross_forward/pallas_call | solution.py:236
  56.6 12.7 %feed_hidden.1 = (bf16[512,3072]{1,0:T(8,128)(2,1)S(1)}, bf16[512,3072]{1,0:T(8,128)(2,1)}, bf16[96,96,128]{2,1,0:T(8,128)(2,1)}, bf16[96,96,128]{2,1,0:T(8,128)(2,1)}, f32[8,128]{1,0:T(8,128)}) custom-call(s32[387]{0:T(512)S(1)} %pad_add_fusion.refs_0_, bf16[512,768]{1,0:T(8,128)(2,1)S(1)} %get-tuple-element.180.refs_1_, ...), custom_call_target="tpu_custom_call" | custom-call | flops 1153000 | tf_op jit(solution)/shard_map/feed_hidden/pallas_call | solution.py:236
  69.3 2.8 %collective-permute-start.7 = (bf16[9216,128]{1,0:T(8,128)(2,1)}, bf16[9216,128]{1,0:T(8,128)(2,1)S(1)}, u32[]{:S(2)}, u32[]{:S(2)}) collective-permute-start(bf16[9216,128]{1,0:T(8,128)(2,1)} %bitcast.465), channel_id=1, source_target_pairs={{0,8},{8,0},{16,24},{24,16},{1,9},{9,1},{17,25},{25,17},{2,10},{10... | collective-permute-start | bytes 7077896 | tf_op jit(solution)/shard_map/ppermute | solution.py:1007
  72.1 6.0 %feed_weights.1 = (bf16[96,96,128]{2,1,0:T(8,128)(2,1)}, bf16[96,96,128]{2,1,0:T(8,128)(2,1)}, f32[512,768]{1,0:T(8,128)S(1)}, f32[8,128]{1,0:T(8,128)}) custom-call(s32[387]{0:T(512)S(1)} %pad_add_fusion.refs_0_, bf16[512,768]{1,0:T(8,128)(2,1)S(1)} %get-tuple-element.180.refs_1_, bf16[512,3072]{1,0:T(8,128)(2,1)S(1)} %get-tuple-element.184.refs_2_.refs_0_, ...), custom_call_target="tpu_custom_call" | custom-call | flops 1153000 | tf_op jit(solution)/shard_map/feed_weights/pallas_call | solution.py:236
  81.7 4.4 %feed_back.1 = (f32[512,768]{1,0:T(8,128)S(1)}, f32[1,768]{1,0:T(1,128)S(1)}, f32[8,128]{1,0:T(8,128)}) custom-call(bf16[512,3072]{1,0:T(8,128)(2,1)S(1)} %get-tuple-element.184.refs_2_.refs_0_, bf16[768,3072]{1,0:T(8,128)(2,1)S(1)} %get-tuple-element.182.refs_4_.refs_1_, f32[512,768]{1,0:T(8,128)S(1)} %get-tuple-element.187.refs_2_, ...), custom_call_target="tpu_custom_call" | custom-call | flops 1153000 | tf_op jit(solution)/shard_map/feed_back/pallas_call | solution.py:236
  89.1 8.9 %cross_backward.2 = (bf16[512,384]{1,0:T(8,128)(2,1)S(1)}, bf16[384,1024]{1,0:T(8,128)(2,1)S(1)}, bf16[384,1024]{1,0:T(8,128)(2,1)S(1)}, f32[8,128]{1,0:T(8,128)}) custom-call(f32[512,768]{1,0:T(8,128)S(1)} %get-tuple-element.192.refs_0_.refs_5_.refs_1_, bf16[768,768]{1,0:T(8,128)(2,1)S(1)} %get-tuple-element.178.refs_12_.refs_1_, ...), custom_call_target="tpu_custom_call" | custom-call | flops 1153000 | tf_op jit(solution)/shard_map/cross_backward/pallas_call | solution.py:236
  98.0 9.0 %cross_backward.3 = (bf16[512,384]{1,0:T(8,128)(2,1)S(1)}, bf16[384,1024]{1,0:T(8,128)(2,1)S(1)}, bf16[384,1024]{1,0:T(8,128)(2,1)S(1)}, bf16[768,768]{1,0:T(8,1...) custom-call(f32[512,768]{1,0:T(8,128)S(1)} %get-tuple-element.192.re, ...), custom_call_target="tpu_custom_call" | custom-call | flops 1153000 | tf_op jit(solution)/shard_map/cross_backward/pallas_call | solution.py:236
  111.8 13.0 %cross_weights.1 = (bf16[48,128,128]{2,1,0:T(8,128)(2,1)}, bf16[120,96,128]{2,1,0:T(8,128)(2,1)}, bf16[120,96,128]{2,1,0:T(8,128)(2,1)}, bf16[512,3072]{1,0:T(8,...) custom-call(s32[387]{0:T(512)S(1)} %pad_add_fusion.refs_0_, ...), custom_call_target="tpu_custom_call" | custom-call | flops 1153000 | tf_op jit(solution)/shard_map/cross_weights/pallas_call | solution.py:236
  126.8 4.5 %feed_out.1 = (bf16[512,768]{1,0:T(8,128)(2,1)}, bf16[768,768]{1,0:T(8,128)(2,1)S(1)}, bf16[512,2304]{1,0:T(8,128)(2,1)S(1)}, bf16[4,6,256,128]{3,2,1,0:T(8,128)(2,1)S(1)}, f32[8,128]{1,0:T(8,128)}) custom-call(bf16[512,3072]{1,0:T(8,128)(2,1)S(1)} %get-tuple-element.228.refs_0_, bf16[3072,768]{1,0:T(8,128)(2,1)S(1)} %get-tuple-element.229.refs_1_, ...), custom_call_target="tpu_custom_call" | custom-call | flops 1153000 | tf_op jit(solution)/shard_map/feed_out/pallas_call | solution.py:236
  134.6 9.5 %self_backward.1 = (bf16[512,2304]{1,0:T(8,128)(2,1)S(1)}, f32[16,128]{1,0:T(8,128)S(1)}, bf16[768,2304]{1,0:T(8,128)(2,1)S(1)}, bf16[512,768]{1,0:T(8,128)(2,1)...) custom-call(f32[512,768]{1,0:T(8,128)S(1)} %get-tuple-element.212.refs_2_.refs_0_.refs_1_, ...), custom_call_target="tpu_custom_call" | custom-call | flops 1153000 | tf_op jit(solution)/shard_map/self_backward/pallas_call | solution.py:236
  144.1 3.6 %collective-permute-done.16.refs_10_.refs_13_ = bf16[1152,128]{1,0:T(8,128)(2,1)S(1)} collective-permute-done((bf16[1152,128]{1,0:T(8,128)(2,1)S(1)}, bf16[1152,128]{1,0:T(8,128)(2,1)S(1)}, u32[]{:S(2)}, u32[]{:S(2)}) %collective-permute-start.16) | collective-permute-done | bytes 294944 | tf_op jit(solution)/shard_map/ppermute | solution.py:1007
  147.7 3.6 %collective-permute-done.15.refs_5_.refs_7_.refs_1_ = bf16[3072,128]{1,0:T(8,128)(2,1)S(1)} collective-permute-done((bf16[3072,128]{1,0:T(8,128)(2,1)S(1)}, bf16[3072,128]{1,0:T(8,128)(2,1)S(1)}, u32[]{:S(2)}, u32[]{:S(2)}) %collective-permute-start.15) | collective-permute-done | bytes 786464 | tf_op jit(solution)/shard_map/ppermute | solution.py:1007
  156.6 8.2 %self_weights.1 = (f32[512,768]{1,0:T(8,128)}, bf16[73,96,128]{2,1,0:T(8,128)(2,1)}, bf16[73,96,128]{2,1,0:T(8,128)(2,1)}, f32[8,128]{1,0:T(8,128)}) custom-call(s32[387]{0:T(512)S(1)} %pad_add_fusion.refs_0_, f32[512,768]{1,0:T(8,128)S(1)} %get-tuple-element.212.refs_2_.refs_0_.refs_1_, bf16[768,2304]{1,0:T(8,128)(2,1)S(1)} %get-tuple-element.244.refs_2_, ...), custom_call_target="tpu_custom_call" | custom-call | flops 1153000 | tf_op jit(solution)/shard_map/self_weights/pallas_call | solution.py:236
  164.9 2.4 collective-permute-start.25
  172.5 3.3 %collective-permute-start.23 = (bf16[1536,128]{1,0:T(8,128)(2,1)S(1)}, bf16[1536,128]{1,0:T(8,128)(2,1)S(1)}, u32[]{:S(2)}, u32[]{:S(2)}) collective-permute-start(bf16[1536,128]{1,0:T(8,128)(2,1)S(1)} %get-tuple-element.265), channel_id=1, source_target_pairs={{0,1},{1,0},{2,3},{3,2},{4,5},{5,4},{6,7},{7,6},{8,9},{9,8},{10,11... | collective-permute-start | bytes 1179656 | tf_op jit(solution)/shard_map/ppermute | solution.py:1007
  177.5 11.5 %collective-permute-done.24.refs_3_ = bf16[1344,128]{1,0:T(8,128)(2,1)S(1)} collective-permute-done((bf16[1344,128]{1,0:T(8,128)(2,1)S(1)}, bf16[1344,128]{1,0:T(8,128)(2,1)S(1)}, u32[]{:S(2)}, u32[]{:S(2)}) %collective-permute-start.24) | collective-permute-done | bytes 344096 | tf_op jit(solution)/shard_map/ppermute | solution.py:1007
  190.6 4.0 %collective-permute-done.27.refs_2_.refs_4_.refs_7_ = bf16[2016,128]{1,0:T(8,128)(2,1)S(1)} collective-permute-done((bf16[2016,128]{1,0:T(8,128)(2,1)S(1)}, bf16[2016,128]{1,0:T(8,128)(2,1)S(1)}, u32[]{:S(2)}, u32[]{:S(2)}) %collective-permute-start.27) | collective-permute-done | bytes 516128 | tf_op jit(solution)/shard_map/ppermute | solution.py:1007
  200.6 5.7 %collective-permute-done.29.refs_8_.refs_10_.refs_3_ = bf16[1056,128]{1,0:T(8,128)(2,1)S(1)} collective-permute-done((bf16[1056,128]{1,0:T(8,128)(2,1)S(1)}, bf16[1056,128]{1,0:T(8,128)(2,1)S(1)}, u32[]{:S(2)}, u32[]{:S(2)}) %collective-permute-start.29) | collective-permute-done | bytes 270368 | tf_op jit(solution)/shard_map/ppermute | solution.py:1007
  213.5 8.8 %collective-permute-done.31.refs_10_.refs_4_.refs_12_ = bf16[960,128]{1,0:T(8,128)(2,1)S(1)} collective-permute-done((bf16[960,128]{1,0:T(8,128)(2,1)S(1)}, bf16[960,128]{1,0:T(8,128)(2,1)S(1)}, u32[]{:S(2)}, u32[]{:S(2)}) %collective-permute-start.31) | collective-permute-done | bytes 245792 | tf_op jit(solution)/shard_map/ppermute | solution.py:1007
  225.9 3.8 %collective-permute-done.36.refs_10_ = bf16[192,128]{1,0:T(8,128)(2,1)S(1)} collective-permute-done((bf16[192,128]{1,0:T(8,128)(2,1)S(1)}, bf16[192,128]{1,0:T(8,128)(2,1)S(1)}, u32[]{:S(2)}, u32[]{:S(2)}) %collective-permute-start.36) | collective-permute-done | bytes 49184 | tf_op jit(solution)/shard_map/ppermute | solution.py:1007
  (156 shorter events, 73.3 us)
Async XLA Ops:
  2.3 18.8 %collective-permute-start = (bf16[1,144,768]{2,1,0:T(8,128)(2,1)S(1)}, bf16[1,144,768]{2,1,0:T(8,128)(2,1)S(1)}, u32[]{:S(2)}, u32[]{:S(2)}) collective-permute-start(bf16[1,144,768]{2,1,0:T(8,128)(2,1)S(1)} %fusion.2.refs_0_), channel_id=1, source_target_pairs={{0,4},{1,5},{2,6},{3,7},{4,0},{5,1},{6,2},{7,3},{8,12},{9,13},{10,... | collective-permute-start | bytes 663560 | tf_op jit(solution)/shard_map/ppermute | solution.py:1007
  5.5 21.4 %collective-permute-start.2 = (bf16[1,144,768]{2,1,0:T(8,128)(2,1)S(1)}, bf16[1,144,768]{2,1,0:T(8,128)(2,1)S(1)}, u32[]{:S(2)}, u32[]{:S(2)}) collective-permute-start(bf16[1,144,768]{2,1,0:T(8,128)(2,1)S(1)} %fusion.2.refs_0_), channel_id=1, source_target_pairs={{0,2},{1,3},{2,0},{3,1},{4,6},{5,7},{6,4},{7,5},{8,10},{9,11},{10,... | collective-permute-start | bytes 663560 | tf_op jit(solution)/shard_map/ppermute | solution.py:1007
  6.8 29.5 %collective-permute-start.1 = (bf16[1,144,768]{2,1,0:T(8,128)(2,1)S(1)}, bf16[1,144,768]{2,1,0:T(8,128)(2,1)}, u32[]{:S(2)}, u32[]{:S(2)}) collective-permute-start(bf16[1,144,768]{2,1,0:T(8,128)(2,1)S(1)} %fusion.2.refs_0_), channel_id=1, source_target_pairs={{0,1},{1,0},{2,3},{3,2},{4,5},{5,4},{6,7},{7,6},{8,9},{9,8},{10,11... | collective-permute-start | bytes 663560 | tf_op jit(solution)/shard_map/ppermute | solution.py:1007
  79.7 28.8 %collective-permute-start.10 = (bf16[4608,128]{1,0:T(8,128)(2,1)S(1)}, bf16[4608,128]{1,0:T(8,128)(2,1)S(1)}, u32[]{:S(2)}, u32[]{:S(2)}) collective-permute-start(bf16[4608,128]{1,0:T(8,128)(2,1)S(1)} %get-tuple-element.224), channel_id=1, source_target_pairs={{0,16},{8,24},{16,0},{24,8},{1,17},{9,25},{17,1},{25,9},{2,18},{10... | collective-permute-start | bytes 3538952 | tf_op jit(solution)/shard_map/ppermute | solution.py:1007
  87.6 20.9 %collective-permute-start.11 = (bf16[2304,128]{1,0:T(8,128)(2,1)S(1)}, bf16[2304,128]{1,0:T(8,128)(2,1)S(1)}, u32[]{:S(2)}, u32[]{:S(2)}) collective-permute-start(bf16[2304,128]{1,0:T(8,128)(2,1)S(1)} %get-tuple-element.225), channel_id=1, source_target_pairs={{0,1},{1,0},{2,3},{3,2},{4,5},{5,4},{6,7},{7,6},{8,9},{9,8},{10,11... | collective-permute-start | bytes 1769480 | tf_op jit(solution)/shard_map/ppermute | solution.py:1007
  88.9 19.6 %collective-permute-start.9 = (bf16[2304,128]{1,0:T(8,128)(2,1)S(1)}, bf16[2304,128]{1,0:T(8,128)(2,1)S(1)}, u32[]{:S(2)}, u32[]{:S(2)}) collective-permute-start(bf16[2304,128]{1,0:T(8,128)(2,1)S(1)} %get-tuple-element.223), channel_id=1, source_target_pairs={{0,2},{1,3},{2,0},{3,1},{4,6},{5,7},{6,4},{7,5},{8,10},{9,11},{10,... | collective-permute-start | bytes 1769480 | tf_op jit(solution)/shard_map/ppermute | solution.py:1007
  110.2 21.1 %collective-permute-start.13 = (bf16[3456,128]{1,0:T(8,128)(2,1)S(1)}, bf16[3456,128]{1,0:T(8,128)(2,1)S(1)}, u32[]{:S(2)}, u32[]{:S(2)}) collective-permute-start(bf16[3456,128]{1,0:T(8,128)(2,1)S(1)} %get-tuple-element.240), channel_id=1, source_target_pairs={{0,1},{1,0},{2,3},{3,2},{4,5},{5,4},{6,7},{7,6},{8,9},{9,8},{10,11... | collective-permute-start | bytes 2654216 | tf_op jit(solution)/shard_map/ppermute | solution.py:1007
  110.5 20.8 %collective-permute-start.12 = (bf16[1152,128]{1,0:T(8,128)(2,1)S(1)}, bf16[1152,128]{1,0:T(8,128)(2,1)S(1)}, u32[]{:S(2)}, u32[]{:S(2)}) collective-permute-start(bf16[1152,128]{1,0:T(8,128)(2,1)S(1)} %get-tuple-element.239), channel_id=1, source_target_pairs={{0,2},{1,3},{2,0},{3,1},{4,6},{5,7},{6,4},{7,5},{8,10},{9,11},{10,... | collective-permute-start | bytes 884744 | tf_op jit(solution)/shard_map/ppermute | solution.py:1007
  124.8 26.5 %collective-permute-start.14 = (bf16[11520,128]{1,0:T(8,128)(2,1)}, bf16[11520,128]{1,0:T(8,128)(2,1)S(1)}, u32[]{:S(2)}, u32[]{:S(2)}) collective-permute-start(bf16[11520,128]{1,0:T(8,128)(2,1)} %bitcast.463), channel_id=1, source_target_pairs={{0,8},{8,0},{16,24},{24,16},{1,9},{9,1},{17,25},{25,17},{2,10},{10... | collective-permute-start | bytes 8847368 | tf_op jit(solution)/shard_map/ppermute | solution.py:1007
  133.1 18.2 %collective-permute-start.15 = (bf16[3072,128]{1,0:T(8,128)(2,1)S(1)}, bf16[3072,128]{1,0:T(8,128)(2,1)S(1)}, u32[]{:S(2)}, u32[]{:S(2)}) collective-permute-start(bf16[3072,128]{1,0:T(8,128)(2,1)S(1)} %get-tuple-element.253), channel_id=1, source_target_pairs={{0,1},{1,0},{2,3},{3,2},{4,5},{5,4},{6,7},{7,6},{8,9},{9,8},{10,11... | collective-permute-start | bytes 2359304 | tf_op jit(solution)/shard_map/ppermute | solution.py:1007
  134.4 13.4 %collective-permute-start.16 = (bf16[1152,128]{1,0:T(8,128)(2,1)S(1)}, bf16[1152,128]{1,0:T(8,128)(2,1)S(1)}, u32[]{:S(2)}, u32[]{:S(2)}) collective-permute-start(bf16[1152,128]{1,0:T(8,128)(2,1)S(1)} %get-tuple-element.254), channel_id=1, source_target_pairs={{0,2},{1,3},{2,0},{3,1},{4,6},{5,7},{6,4},{7,5},{8,10},{9,11},{10,... | collective-permute-start | bytes 884744 | tf_op jit(solution)/shard_map/ppermute | solution.py:1007
  134.5 13.2 %collective-permute-start.17 = (bf16[1152,128]{1,0:T(8,128)(2,1)S(1)}, bf16[1152,128]{1,0:T(8,128)(2,1)S(1)}, u32[]{:S(2)}, u32[]{:S(2)}) collective-permute-start(bf16[1152,128]{1,0:T(8,128)(2,1)S(1)} %get-tuple-element.255), channel_id=1, source_target_pairs={{0,4},{1,5},{2,6},{3,7},{4,0},{5,1},{6,2},{7,3},{8,12},{9,13},{10,... | collective-permute-start | bytes 884744 | tf_op jit(solution)/shard_map/ppermute | solution.py:1007
  153.6 17.3 %collective-permute-start.20 = (bf16[3072,128]{1,0:T(8,128)(2,1)S(1)}, bf16[3072,128]{1,0:T(8,128)(2,1)S(1)}, u32[]{:S(2)}, u32[]{:S(2)}) collective-permute-start(bf16[3072,128]{1,0:T(8,128)(2,1)S(1)} %get-tuple-element.261), channel_id=1, source_target_pairs={{0,16},{8,24},{16,0},{24,8},{1,17},{9,25},{17,1},{25,9},{2,18},{10... | collective-permute-start | bytes 2359304 | tf_op jit(solution)/shard_map/ppermute | solution.py:1007
  153.8 16.1 %collective-permute-start.19 = (bf16[2688,128]{1,0:T(8,128)(2,1)S(1)}, bf16[2688,128]{1,0:T(8,128)(2,1)S(1)}, u32[]{:S(2)}, u32[]{:S(2)}) collective-permute-start(bf16[2688,128]{1,0:T(8,128)(2,1)S(1)} %get-tuple-element.260), channel_id=1, source_target_pairs={{0,1},{1,0},{2,3},{3,2},{4,5},{5,4},{6,7},{7,6},{8,9},{9,8},{10,11... | collective-permute-start | bytes 2064392 | tf_op jit(solution)/shard_map/ppermute | solution.py:1007
  155.9 13.2 %collective-permute-start.18 = (bf16[1536,128]{1,0:T(8,128)(2,1)S(1)}, bf16[1536,128]{1,0:T(8,128)(2,1)S(1)}, u32[]{:S(2)}, u32[]{:S(2)}) collective-permute-start(bf16[1536,128]{1,0:T(8,128)(2,1)S(1)} %get-tuple-element.259), channel_id=1, source_target_pairs={{0,2},{1,3},{2,0},{3,1},{4,6},{5,7},{6,4},{7,5},{8,10},{9,11},{10,... | collective-permute-start | bytes 1179656 | tf_op jit(solution)/shard_map/ppermute | solution.py:1007
  172.5 16.5 %collective-permute-start.23 = (bf16[1536,128]{1,0:T(8,128)(2,1)S(1)}, bf16[1536,128]{1,0:T(8,128)(2,1)S(1)}, u32[]{:S(2)}, u32[]{:S(2)}) collective-permute-start(bf16[1536,128]{1,0:T(8,128)(2,1)S(1)} %get-tuple-element.265), channel_id=1, source_target_pairs={{0,1},{1,0},{2,3},{3,2},{4,5},{5,4},{6,7},{7,6},{8,9},{9,8},{10,11... | collective-permute-start | bytes 1179656 | tf_op jit(solution)/shard_map/ppermute | solution.py:1007
  175.8 13.2 %collective-permute-start.24 = (bf16[1344,128]{1,0:T(8,128)(2,1)S(1)}, bf16[1344,128]{1,0:T(8,128)(2,1)S(1)}, u32[]{:S(2)}, u32[]{:S(2)}) collective-permute-start(bf16[1344,128]{1,0:T(8,128)(2,1)S(1)} %get-tuple-element.266), channel_id=1, source_target_pairs={{0,2},{1,3},{2,0},{3,1},{4,6},{5,7},{6,4},{7,5},{8,10},{9,11},{10,... | collective-permute-start | bytes 1032200 | tf_op jit(solution)/shard_map/ppermute | solution.py:1007
  175.8 32.7 %collective-permute-start.22 = (bf16[768,128]{1,0:T(8,128)(2,1)S(1)}, bf16[768,128]{1,0:T(8,128)(2,1)S(1)}, u32[]{:S(2)}, u32[]{:S(2)}) collective-permute-start(bf16[768,128]{1,0:T(8,128)(2,1)S(1)} %get-tuple-element.264), channel_id=1, source_target_pairs={{0,4},{1,5},{2,6},{3,7},{4,0},{5,1},{6,2},{7,3},{8,12},{9,13},{10,... | collective-permute-start | bytes 589832 | tf_op jit(solution)/shard_map/ppermute | solution.py:1007
  177.3 17.3 %collective-permute-start.27 = (bf16[2016,128]{1,0:T(8,128)(2,1)S(1)}, bf16[2016,128]{1,0:T(8,128)(2,1)S(1)}, u32[]{:S(2)}, u32[]{:S(2)}) collective-permute-start(bf16[2016,128]{1,0:T(8,128)(2,1)S(1)} %get-tuple-element.274.refs_3_), channel_id=1, source_target_pairs={{0,1},{1,0},{2,3},{3,2},{4,5},{5,4},{6,7},{7,6},{8,9},{9,8},{10,11... | collective-permute-start | bytes 1548296 | tf_op jit(solution)/shard_map/ppermute | solution.py:1007
  177.5 13.0 %collective-permute-start.28 = (bf16[1536,128]{1,0:T(8,128)(2,1)S(1)}, bf16[1536,128]{1,0:T(8,128)(2,1)S(1)}, u32[]{:S(2)}, u32[]{:S(2)}) collective-permute-start(bf16[1536,128]{1,0:T(8,128)(2,1)S(1)} %get-tuple-element.275), channel_id=1, source_target_pairs={{0,16},{8,24},{16,0},{24,8},{1,17},{9,25},{17,1},{25,9},{2,18},{10... | collective-permute-start | bytes 1179656 | tf_op jit(solution)/shard_map/ppermute | solution.py:1007
  190.5 23.0 %collective-permute-start.34 = (bf16[672,128]{1,0:T(8,128)(2,1)S(1)}, bf16[672,128]{1,0:T(8,128)(2,1)S(1)}, u32[]{:S(2)}, u32[]{:S(2)}) collective-permute-start(bf16[672,128]{1,0:T(8,128)(2,1)S(1)} %get-tuple-element.286), channel_id=1, source_target_pairs={{0,4},{1,5},{2,6},{3,7},{4,0},{5,1},{6,2},{7,3},{8,12},{9,13},{10,... | collective-permute-start | bytes 516104 | tf_op jit(solution)/shard_map/ppermute | solution.py:1007
  197.6 12.7 %collective-permute-start.32 = (bf16[768,128]{1,0:T(8,128)(2,1)S(1)}, bf16[768,128]{1,0:T(8,128)(2,1)S(1)}, u32[]{:S(2)}, u32[]{:S(2)}) collective-permute-start(bf16[768,128]{1,0:T(8,128)(2,1)S(1)} %get-tuple-element.283), channel_id=1, source_target_pairs={{0,1},{1,0},{2,3},{3,2},{4,5},{5,4},{6,7},{7,6},{8,9},{9,8},{10,11... | collective-permute-start | bytes 589832 | tf_op jit(solution)/shard_map/ppermute | solution.py:1007
  208.5 13.8 %collective-permute-start.31 = (bf16[960,128]{1,0:T(8,128)(2,1)S(1)}, bf16[960,128]{1,0:T(8,128)(2,1)S(1)}, u32[]{:S(2)}, u32[]{:S(2)}) collective-permute-start(bf16[960,128]{1,0:T(8,128)(2,1)S(1)} %get-tuple-element.282.refs_11_), channel_id=1, source_target_pairs={{0,4},{1,5},{2,6},{3,7},{4,0},{5,1},{6,2},{7,3},{8,12},{9,13},{10,... | collective-permute-start | bytes 737288 | tf_op jit(solution)/shard_map/ppermute | solution.py:1007
  211.3 13.6 %collective-permute-start.33 = (bf16[384,128]{1,0:T(8,128)(2,1)S(1)}, bf16[384,128]{1,0:T(8,128)(2,1)S(1)}, u32[]{:S(2)}, u32[]{:S(2)}) collective-permute-start(bf16[384,128]{1,0:T(8,128)(2,1)S(1)} %get-tuple-element.285), channel_id=1, source_target_pairs={{0,2},{1,3},{2,0},{3,1},{4,6},{5,7},{6,4},{7,5},{8,10},{9,11},{10,... | collective-permute-start | bytes 294920 | tf_op jit(solution)/shard_map/ppermute | solution.py:1007
  (33 other events, 197.0 us)
where the time goes:
time: 245 us; the launch traced here: 244 us
  Pallas kernels  145 us (59%)
  waiting for transfers between devices  52.6 us (21%)
  starting transfers between devices  36.7 us (15%)
  local copies, waits for them, and re-layouts  6.65 us (3%)
    pallas_call x52, Pallas kernels, call(): pl.pallas_call(ordered, out_shape=tuple(out_shape), grid_spec=pltpu.Prefe...  145 us
    ppermute x41, waiting for transfers between devices, swap(): return lax.ppermute(value, axis, [(i, i ^ bit) for i in range(size)])  52.6 us
    ppermute x41, starting transfers between devices, swap(): return lax.ppermute(value, axis, [(i, i ^ bit) for i in range(size)])  36.7 us
    unnamed x35, local copies, waits for them, and re-layouts  5.96 us
  transfers between devices with their start and end apart: 41, of which 15 were waited for; matrix products, arithmetic and copies ran while one was open for 0% of the time, Pallas kernels for 43%

commit v1 on v0

--- a/solution.py
+++ b/solution.py
@@ -108,11 +108,16 @@
 
 
 class Drain:
-    def __init__(self, copy, ref):
+    def __init__(self, copy, ref, out, sem):
         self.copy, self.ref, self.started = copy, ref, False
+        self.out, self.sem = out, sem
 
     def flush(self):
         self.copy.start()
+        self.started = True
+
+    def flush_part(self, at):
+        pltpu.make_async_copy(self.ref.at[at], self.out.at[at], self.sem).start()
         self.started = True
 
 
@@ -204,13 +209,18 @@
             held, sem = extra[:2]
             extra = extra[2:]
             if i in drains:
-                results[i] = Drain(pltpu.make_async_copy(held, results[i], sem), held)
+                copy = pltpu.make_async_copy(held, results[i], sem)
+                results[i] = Drain(copy, held, results[i], sem)
                 ends.append(results[i])
             else:
-                copies = [
-                    pltpu.make_async_copy(held.at[k], results[i + k], sem.at[k]) for k in range(2)
+                halves = [
+                    Drain(
+                        pltpu.make_async_copy(held.at[k], results[i + k], sem.at[k]),
+                        held.at[k], results[i + k], sem.at[k],
+                    )
+                    for k in range(2)
                 ]
-                results[i] = Pair([Drain(copy, held) for copy in copies], held)
+                results[i] = Pair(halves, held)
                 ends += results[i].drains
         for i in reversed(pairs[1::2]):
             del results[i]
@@ -295,6 +305,13 @@
                 y, k = divmod(block - first, blocks // self.y_parts)
                 return i, y, k
 
+    def runs(self):
+        found = []
+        for first, blocks, order, _ in self.sections:
+            size = blocks // self.y_parts if order == "y" else blocks
+            found += [(at, size) for at in range(first, first + blocks, size)]
+        return found
+
     def table(self, spots, y_spots):
         units = []
         for c in range(self.chunks):
@@ -317,7 +334,7 @@
                 ref[slot, unit] = value[n * self.part : (n + 1) * self.part, j * 128 : (j + 1) * 128].astype(BF)
 
 
-def self_attention(x, gain_self, w_qkv, rel_bias, ahead):
+def self_attention(x, gains, w_qkv, rel_bias, ahead):
     rows, width = x.shape
     bucket_count, heads = rel_bias.shape
     pairs = heads // 2
@@ -329,9 +346,25 @@
     ):
         a1_ref, qkv_ref, p1_ref = a1_out.ref, qkv_out.ref, p1_out.ref
         xf = x.ready()[...].astype(F32)
-        a1 = (xf * inv_rms(xf) * gs_ref[...]).astype(BF)
+        a1 = (xf * inv_rms(xf) * gs_ref[0:1, :]).astype(BF)
         a1_ref[...] = a1
         a1_out.flush()
+        row = lax.broadcasted_iota(jnp.int32, (TLEN, GROUP), 0)
+        col = lax.broadcasted_iota(jnp.int32, (TLEN, GROUP), 1)
+        distance = lax.rem(col, TLEN) - row
+
+        def make_bias(h, carry):
+            val = jnp.full((TLEN, GROUP), NEG_LARGE, F32)
+            for b, first in firsts:
+                val = jnp.where(distance >= first, rb_ref[h, b], val)
+            lanes = pl.ds(pl.multiple_of(lax.rem(h, 2) * GROUP, GROUP), GROUP)
+            for t in range(GROUP // TLEN):
+                bias[h // 2, t * TLEN : (t + 1) * TLEN, lanes] = jnp.where(
+                    col // TLEN == t, val, NEG_LARGE
+                )
+            return carry
+
+        lax.fori_loop(0, heads, make_bias, 0)
         wqkv_ref = wqkv.ready()
 
         def project(t, carry):
@@ -341,19 +374,6 @@
 
         lax.fori_loop(0, 3, project, 0)
         qkv_out.flush()
-        row = lax.broadcasted_iota(jnp.int32, (GROUP, GROUP), 0)
-        col = lax.broadcasted_iota(jnp.int32, (GROUP, GROUP), 1)
-        distance = row - col
-        allowed = jnp.logical_and(distance >= 0, row // TLEN == col // TLEN)
-
-        def make_bias(h, carry):
-            val = jnp.full((GROUP, GROUP), NEG_LARGE, F32)
-            for b, first in firsts:
-                val = jnp.where(distance >= first, rb_ref[h, b], val)
-            bias[h] = jnp.where(allowed, val, NEG_LARGE)
-            return carry
-
-        lax.fori_loop(0, heads, make_bias, 0)
         m0, m1 = half_masks(GROUP)
 
         def attend(g, carry):
@@ -363,20 +383,19 @@
                 q = qkv_ref[at, lo : lo + 128]
                 k = qkv_ref[at, width + lo : width + lo + 128]
                 v = qkv_ref[at, 2 * width + lo : 2 * width + lo + 128]
-                s = dot_nt(jnp.concatenate([q * m0, q * m1], 0), k)
-                s = s + jnp.concatenate([bias[2 * pair], bias[2 * pair + 1]], 0)
-                e = jnp.exp(s - jnp.max(s, -1, keepdims=True))
-                p = (e / jnp.sum(e, -1, keepdims=True)).astype(BF)
+                s = dot_nt(k, jnp.concatenate([q * m0, q * m1], 0)) + bias[pair]
+                e = jnp.exp(s - jnp.max(s, 0, keepdims=True))
+                p = (e / jnp.sum(e, 0, keepdims=True)).astype(BF)
                 p1_ref[g, pair] = p
-                o = dot_nn(
-                    jnp.concatenate([p[:GROUP], p[GROUP:]], 1),
+                o = dot_tn(
+                    jnp.concatenate([p[:, :GROUP], p[:, GROUP:]], 0),
                     jnp.concatenate([v * m0, v * m1], 0),
                 )
                 o1_ref[at, lo : lo + 128] = o.astype(BF)
+            p1_out.flush_part(pl.ds(g, 1))
             return carry
 
         lax.fori_loop(0, groups, attend, 0)
-        p1_out.flush()
         o1_out.ref[...] = o1_ref[...]
         o1_out.flush()
 
@@ -386,19 +405,19 @@
         (
             shape_of(BF, rows, width),
             shape_of(BF, rows, 3 * width),
-            shape_of(BF, groups, pairs, 2 * GROUP, GROUP),
+            shape_of(BF, groups, pairs, GROUP, 2 * GROUP),
             shape_of(BF, rows, width),
             shape_of(BF, rows, width),
         ),
         [STREAM, VMEM, STREAM, SMEM],
         (DRAIN, DRAIN, DRAIN, NEAR, DRAIN),
-        (x, gain_self.reshape(1, width), w_qkv, rel_bias.T),
+        (x, gains, w_qkv, rel_bias.T),
         ahead=ahead,
-        scratch=[pltpu.VMEM((heads, GROUP, GROUP), F32)],
-    )
-
-
-def self_project(x, o1, w_self_out, gain_cross, w_cross_q, ahead):
+        scratch=[pltpu.VMEM((pairs, GROUP, 2 * GROUP), F32)],
+    )
+
+
+def self_project(x, o1, w_self_out, gains, w_cross_q, ahead):
     rows, width = x.shape
 
     def body(x_ref, o1_ref, wso_ref, gc_ref, wcq_ref, h1_ref, cq_ref, h1_out, a2_out, cq_out):
@@ -406,7 +425,7 @@
         h1_ref[...] = h1
         h1_out.ref[...] = h1
         h1_out.flush()
-        a2 = (h1 * inv_rms(h1) * gc_ref[...]).astype(BF)
+        a2 = (h1 * inv_rms(h1) * gc_ref[1:2, :]).astype(BF)
         a2_out.ref[...] = a2
         a2_out.flush()
         cq = dot_nn(a2, wcq_ref[...]).astype(BF)
@@ -420,13 +439,13 @@
         (full, low, full, low, low),
         [VMEM] * 5,
         (NEAR, NEAR, DRAIN, DRAIN, DRAIN),
-        (x, o1, w_self_out, gain_cross.reshape(1, width), w_cross_q),
+        (x, o1, w_self_out, gains, w_cross_q),
         ahead=ahead,
     )
 
 
 def cross_forward(
-    pieces, order, shard_rows, tgt_question, cq, h1, w_cross_kv, w_cross_out, gain_ff, ahead
+    pieces, order, shard_rows, tgt_question, cq, h1, w_cross_kv, w_cross_out, gains, ahead
 ):
     rows, width = cq.shape
     pairs = width // 128
@@ -490,15 +509,30 @@
             q = cq_ref[at, pl.ds(lo, 128)]
             k = kv_ref[:, pl.ds(lo, 128)]
             v = kv_ref[:, pl.ds(width + lo, 128)]
-            outs = []
-            for h in range(2):
-                qa = q * qmask[h] + qfeat[at, :] * qmask[1 - h]
-                ka = k * kmask[h] + kfeat[...] * kmask[1 - h]
-                s = dot_nt(qa, ka)
-                top = jnp.max(s, -1, keepdims=True)
-                e = jnp.exp(s - top).astype(BF)
-                ebuf[slot, h] = e
-                outs.append(dot_nn(e, v * kmask[h] + kmask[1 - h]))
+            keys = [k * kmask[h] + kfeat[...] * kmask[1 - h] for h in range(2)]
+            values = [v * kmask[h] + kmask[1 - h] for h in range(2)]
+            size = min(block_rows, 256)
+            units = [(r, h) for r in range(0, block_rows, size) for h in range(2)]
+            tagged = qfeat[at, :]
+
+            def score(unit):
+                r, h = unit
+                qa = q[r : r + size] * qmask[h][:size] + tagged[r : r + size] * qmask[1 - h][:size]
+                return dot_nt(qa, keys[h])
+
+            outs, last = {}, None
+            s = score(units[0])
+            for i, unit in enumerate(units):
+                later = score(units[i + 1]) if i + 1 < len(units) else None
+                if last is not None:
+                    outs[last[0]] = dot_nn(last[1], values[last[0][1]])
+                e = jnp.exp(s - jnp.max(s, -1, keepdims=True)).astype(BF)
+                ebuf[slot, unit[1], unit[0] : unit[0] + size, :] = e
+                last, s = (unit, e), later
+            outs[last[0]] = dot_nn(last[1], values[last[0][1]])
+            outs = [
+                jnp.concatenate([outs[r, h] for r in range(0, block_rows, size)], 0) for h in range(2)
+            ]
             out_copy(slot, step).start()
             total = jnp.where(low, pltpu.roll(outs[0], 64, 1), pltpu.roll(outs[1], 64, 1))
             inv = 1.0 / total
@@ -512,7 +546,7 @@
         h2 = h1_ref[...] + dot_nn(o2_ref[...], wco_ref[...])
         h2_out.ref[...] = h2
         h2_out.flush()
-        a3_ref[...] = (h2 * inv_rms(h2) * gf_ref[...]).astype(BF)
+        a3_ref[...] = (h2 * inv_rms(h2) * gf_ref[2:3, :]).astype(BF)
         for step in range(max(0, steps - 2), steps):
             out_copy(step % 2, jnp.int32(step)).wait()
 
@@ -530,7 +564,7 @@
         ),
         [VMEM] * len(pieces) + [SMEM] + [VMEM] * 5,
         (DRAIN, DRAIN, (HBM, ANY), DRAIN, DRAIN, DRAIN, NEAR),
-        (*pieces, tgt_question, cq, h1, w_cross_kv, w_cross_out, gain_ff.reshape(1, width)),
+        (*pieces, tgt_question, cq, h1, w_cross_kv, w_cross_out, gains),
         scratch=[
             pltpu.VMEM((tokens, 128), BF),
             pltpu.VMEM((rows, 128), BF),
@@ -546,21 +580,32 @@
     rows, width = gy.shape
     hidden = w_ff_out.shape[0]
 
-    def body(gy_ref, w2_ref, out_ref):
+    tiles = hidden // width
+
+    def body(gy_ref, w2_ref, out_ref, w2, sem):
+        def copy(t):
+            at = pl.ds(pl.multiple_of(t * width, 128), width)
+            return pltpu.make_async_copy(w2_ref.at[at], w2.at[at], sem.at[t])
+
+        for t in range(tiles):
+            copy(t).start()
+
         def tile(t, carry):
+            copy(t).wait()
             at = pl.ds(pl.multiple_of(t * width, 128), width)
-            out_ref[:, at] = dot_nt(gy_ref[...], w2_ref[at, :]).astype(BF)
+            out_ref[:, at] = dot_nt(gy_ref[...], w2[at, :]).astype(BF)
             return carry
 
-        lax.fori_loop(0, hidden // width, tile, 0)
+        lax.fori_loop(0, tiles, tile, 0)
 
     return call(
         "hidden_gradient",
         body,
         shape_of(BF, rows, hidden),
-        [VMEM, VMEM],
+        [VMEM, (HBM, ANY)],
         NEAR,
         (gy, w_ff_out),
+        scratch=[pltpu.VMEM((hidden, width), BF), pltpu.SemaphoreType.DMA((tiles,))],
         ahead=ahead,
     )
 
@@ -576,9 +621,7 @@
     scale = math.sqrt(2.0 / math.pi)
 
     def body(place_ref, a3_ref, gy_ref, dhid_ref, w1_ref, dpre_ref, hid_out, both):
-        def one(step, carry):
-            at = pl.ds(pl.multiple_of(step * tile, 128), tile)
-            pre = dot_nn(a3_ref[...], w1_ref[:, at])
+        def activate(pre, at):
             sq = pre * pre
             t = jnp.tanh(pre * (scale + (scale * 0.044715) * sq))
             up = 0.5 + 0.5 * t
@@ -586,15 +629,36 @@
             slope = up + pre * (up - up * up) * ((2.0 * scale) + (2.0 * scale * 0.134145) * sq)
             hid_out.ref[:, at] = hid
             dpre_ref[:, at] = (dhid_ref[:, at].astype(F32) * slope).astype(BF)
-            g = dot_tn(hid, gy_ref[...])
-            for h in range(2):
-                for i in range(per_tile):
+            return hid
+
+        def one(step, carry):
+            parts = tile // 256
+            ats = [pl.ds(pl.multiple_of(step * tile + i * 256, 128), 256) for i in range(parts)]
+            a3, gyv = a3_ref[...], gy_ref[...]
+            pre = dot_nn(a3, w1_ref[:, ats[0]])
+            grads, hid = [], None
+            for i in range(parts):
+                later = dot_nn(a3, w1_ref[:, ats[i + 1]]) if i + 1 < parts else None
+                if hid is not None:
+                    grads.append(dot_tn(hid, gyv))
+                hid = activate(pre, ats[i])
+                pre = later
+            grads.append(dot_tn(hid, gyv))
+            hid_out.flush_part((slice(None), pl.ds(pl.multiple_of(step * tile, 128), tile)))
+            g = jnp.concatenate(grads, 0)
+            for i in range(per_tile):
+                chunk = step * per_tile + i
+                for h in range(2):
                     for j in range(sub):
                         first = (i * sub + j) * part
                         columns.store(
                             both.ref, h, "out", g[first : first + part, h * half : (h + 1) * half],
-                            place_ref, [step * per_tile + i], j * half // 128,
+                            place_ref, [chunk], j * half // 128,
                         )
+                for first, count in columns.runs():
+                    unit = place_ref[columns.at + chunk * columns.blocks + first]
+                    for drain in both.drains:
+                        drain.flush_part(pl.ds(unit, count))
             return carry
 
         lax.fori_loop(0, hidden // tile, one, 0)
@@ -621,6 +685,16 @@
             g = dot_tn(a3_ref[...], dpre_ref[:, at])
             block = lax.rem(t, tiles // 2) * (width // 128)
             columns.store(both.ref, t // (tiles // 2), "in", g, place_ref, None, block)
+            for slot in range(2):
+
+                @pl.when(jnp.logical_and(t == tiles // 2 - 1, place_ref[0] == slot))
+                def _():
+                    both.drains[slot].flush_part(pl.ds(0, columns.units))
+
+                @pl.when(jnp.logical_and(t == tiles - 1, place_ref[0] != slot))
+                def _():
+                    both.drains[slot].flush_part(pl.ds(0, columns.units))
+
             return carry
 
         lax.fori_loop(0, tiles, one, 0)
@@ -636,7 +710,7 @@
     )
 
 
-def feed_back(dpre, w_ff_in, h2, gain_ff, gy):
+def feed_back(dpre, w_ff_in, h2, gains, gy):
     rows, width = h2.shape
 
     def body(dpre_ref, w1_ref, h2_ref, gf_ref, gy_ref, dh2_ref, gain_ref, da3):
@@ -648,7 +722,7 @@
             return carry
 
         lax.fori_loop(0, dpre_ref.shape[1] // width, one, 0)
-        dv, dgain = rms_back(da3[...], h2_ref[...], gf_ref[...])
+        dv, dgain = rms_back(da3[...], h2_ref[...], gf_ref[2:3, :])
         dh2_ref[...] = gy_ref[...].astype(F32) + dv
         gain_ref[...] = dgain
 
@@ -657,8 +731,8 @@
         body,
         (shape_of(F32, rows, width), shape_of(F32, 1, width)),
         [VMEM] * 5,
-        (NEAR, VMEM),
-        (dpre, w_ff_in, h2, gain_ff.reshape(1, width), gy),
+        (NEAR, NEAR),
+        (dpre, w_ff_in, h2, gains, gy),
         scratch=[pltpu.VMEM((rows, width), F32)],
     )
 
@@ -781,7 +855,7 @@
     )
 
 
-def cross_query_back(dcq, w_cross_q, h1, gain_cross, dh2):
+def cross_query_back(dcq, w_cross_q, h1, gains, dh2):
     rows, width = h1.shape
     n = len(dcq)
     size = width // n
@@ -791,7 +865,7 @@
         da2 = 0.0
         for i in range(n):
             da2 = da2 + dot_nt(refs[i][...], wcq_ref[:, i * size : (i + 1) * size])
-        dv, dgain = rms_back(da2, h1_ref[...], gc_ref[...])
+        dv, dgain = rms_back(da2, h1_ref[...], gc_ref[1:2, :])
         dh1_ref[...] = dh2_ref[...] + dv
         gain_ref[...] = dgain
 
@@ -800,8 +874,8 @@
         body,
         (shape_of(F32, rows, width), shape_of(F32, 1, width)),
         [VMEM] * (n + 4),
-        (NEAR, VMEM),
-        (*dcq, w_cross_q, h1, gain_cross.reshape(1, width), dh2),
+        (NEAR, NEAR),
+        (*dcq, w_cross_q, h1, gains, dh2),
     )
 
 
@@ -817,6 +891,7 @@
     n = len(dcq)
     size = width // n
     blocks = width // 128
+    near = 2 * blocks // 3
     shard_rows = tokens // columns.chunks
 
     def body(place_ref, dh2_ref, dh1_ref, a2_ref, o2_ref, o1_ref, *refs):
@@ -843,9 +918,11 @@
             at = pl.ds(pl.multiple_of(t * tile, 128), tile)
             genct = dot_nn(wkv_ref[...], dkvt[:, at]).astype(BF)
             for i in range(tile // shard_rows):
-                spot = t * (tile // shard_rows) + i
                 for j in range(blocks):
-                    genc_out.ref[spot * blocks + j] = genct[
+                    order = 0 if j < near else 1
+                    size = blocks - near if order else near
+                    spot = place_ref[3 + order * columns.chunks + t * (tile // shard_rows) + i]
+                    genc_out.ref[order * columns.chunks * near + spot * size + j - order * near] = genct[
                         j * 128 : (j + 1) * 128, i * shard_rows : (i + 1) * shard_rows
                     ]
             return carry
@@ -904,20 +981,20 @@
                 do_two = jnp.concatenate([do * m0, do * m1], 0)
                 pb = p1_ref[g, pair]
                 pf = pb.astype(F32)
-                dp = dot_nt(do_two, v)
-                ds = (pf * (dp - jnp.sum(pf * dp, -1, keepdims=True))).astype(BF)
+                dp = dot_nt(v, do_two)
+                ds = (pf * (dp - jnp.sum(pf * dp, 0, keepdims=True))).astype(BF)
                 dsf = ds.astype(F32)
-                for h in range(2):
-                    total = dsf[h * GROUP : h * GROUP + TLEN]
-                    for t in range(1, GROUP // TLEN):
-                        total = total + dsf[h * GROUP + t * TLEN : h * GROUP + (t + 1) * TLEN]
-                    acc[2 * pair + h] += total
-                dq = dot_nn(
-                    jnp.concatenate([ds[:GROUP], ds[GROUP:]], 1),
+                total = dsf[:TLEN]
+                for t in range(1, GROUP // TLEN):
+                    total = total + dsf[t * TLEN : (t + 1) * TLEN]
+                acc[2 * pair] += total[:, :GROUP]
+                acc[2 * pair + 1] += total[:, GROUP:]
+                dq = dot_tn(
+                    jnp.concatenate([ds[:, :GROUP], ds[:, GROUP:]], 0),
                     jnp.concatenate([k * m0, k * m1], 0),
                 )
-                dk = dot_tn(ds, jnp.concatenate([q * m0, q * m1], 0))
-                dv = dot_tn(pb, do_two)
+                dk = dot_nn(ds, jnp.concatenate([q * m0, q * m1], 0))
+                dv = dot_nn(pb, do_two)
                 dqkv_ref[at, lo : lo + 128] = dq.astype(BF)
                 dqkv_ref[at, width + lo : width + lo + 128] = dk.astype(BF)
                 dqkv_ref[at, 2 * width + lo : 2 * width + lo + 128] = dv.astype(BF)
@@ -925,7 +1002,7 @@
 
         lax.fori_loop(0, groups, attend, 0)
         row = lax.broadcasted_iota(jnp.int32, (TLEN, GROUP), 0)
-        distance = row - lax.rem(lax.broadcasted_iota(jnp.int32, (TLEN, GROUP), 1), TLEN)
+        distance = lax.rem(lax.broadcasted_iota(jnp.int32, (TLEN, GROUP), 1), TLEN) - row
         lane = lax.broadcasted_iota(jnp.int32, (16, 128), 1)
         bias = jnp.zeros((16, 128), F32)
         accv = acc[...]
@@ -942,7 +1019,7 @@
         body,
         (shape_of(BF, rows, 3 * width), shape_of(F32, 16, 128)),
         [VMEM] * 4,
-        (NEAR, VMEM),
+        (NEAR, NEAR),
         (dh1, w_self_out, qkv, p1),
         ahead=ahead,
         scratch=[pltpu.VMEM((rows, width), BF), pltpu.VMEM((heads, TLEN, GROUP), F32)],
@@ -950,7 +1027,7 @@
 
 
 def self_weights(
-    place, dh1, a1, dqkv, x, gain_self, w_qkv, gbias, gain_cross_grad, gain_ff_grad, columns
+    place, dh1, a1, dqkv, x, gains, w_qkv, gbias, gain_cross_grad, gain_ff_grad, columns
 ):
     rows, width = dh1.shape
     half = width // 2
@@ -970,7 +1047,7 @@
             return carry
 
         lax.fori_loop(0, 3, one, 0)
-        dv, dgain = rms_back(da1[...], x_ref[...].astype(F32), gs_ref[...])
+        dv, dgain = rms_back(da1[...], x_ref[...].astype(F32), gs_ref[0:1, :])
         out.ref[...] = dh1_ref[...] + dv
         out.flush()
 
@@ -995,7 +1072,7 @@
         [SMEM] + [VMEM] * 9,
         (DRAIN, PAIR, PAIR),
         (
-            place, dh1, w_qkv, x, a1, dqkv, gain_self.reshape(1, width), gbias,
+            place, dh1, w_qkv, x, a1, dqkv, gains, gbias,
             gain_cross_grad, gain_ff_grad,
         ),
         scratch=[pltpu.VMEM((rows, width), F32)],
@@ -1312,7 +1389,7 @@
     blocks = half // 128
     cols_out = layout([("out", stack * half)], (stack * blocks, "y"))
     cols_in = layout([("in", hidden // 2)], (stack * blocks // 2, 0), (stack * blocks // 2, 1))
-    far_x, far_s = along_y(16 * blocks // 3), along_y(3 * blocks)
+    far_x, far_s = along_y(16 * blocks // 3), along_y(4 * blocks)
     near_x, near_s = 5 * blocks - far_x, 3 * blocks - far_s
     cols_x = layout(
         [("q", half), ("out", half), ("self", half), ("kv", width)],
@@ -1323,6 +1400,11 @@
     places = [[chunk_place(c, blk, order) for c in range(chunks)] for order in orders]
     y_places = [chunk_place(y, dp // 2, y_bits) for y in range(y_parts)]
     numbers = [lax.rem(dp, 2), blk, dp // 2]
+    for order in orders:
+        spots = [0] * chunks
+        for r in range(chunks):
+            spots[chunk_spot(r, bits)] = chunk_spot(r, order)
+        numbers += [jnp.int32(spot) for spot in spots]
     for columns in (cols_out, cols_in, cols_x, cols_s):
         columns.at = len(numbers)
         numbers += columns.table(places, y_places)
@@ -1333,22 +1415,23 @@
     tags = jnp.where(enc_valid[0] == 1, enc_question[0], -1).astype(BF)
     tag_rows = jnp.zeros((16, width), BF).at[0, :shard_rows].set(tags)
     enc_own = jnp.concatenate([encodings[0], tag_rows], 0)[None]
+    gains = jnp.stack([gain_self, gain_cross, gain_ff])
     got, second = gather_encodings(enc_own, bits)
     shadow(10)
     a1, qkv, p1, o1_near, o1, wso_near, wcq_near, x_near = self_attention(
-        x, gain_self, w_qkv, rel_bias, [w_self_out, w_cross_q, x]
+        x, gains, w_qkv, rel_bias, [w_self_out, w_cross_q, x]
     )
     more, third = second()
     shadow(10)
-    h1_near, cq_near, h1, a2, cq, w2_near, gy = self_project(
-        x_near, o1_near, wso_near, gain_cross, wcq_near, [w_ff_out, gy]
+    h1_near, cq_near, h1, a2, cq, gy = self_project(
+        x_near, o1_near, wso_near, gains, wcq_near, [gy]
     )
     pieces, rel = third()
     shadow(10)
-    dhid, wkv_near, wco_near = hidden_gradient(gy, w2_near, [w_cross_kv, w_cross_out])
+    dhid, wkv_near, wco_near = hidden_gradient(gy, w_ff_out, [w_cross_kv, w_cross_out])
     spots = [[int(chunk_spot(r, bits)) for r in group] for group in rel]
     enc, kv, e, inv, o2, h2, a3, w1_near = cross_forward(
-        pieces, spots, shard_rows, tgt_question[0], cq_near, h1_near, wkv_near, wco_near, gain_ff, [w_ff_in]
+        pieces, spots, shard_rows, tgt_question[0], cq_near, h1_near, wkv_near, wco_near, gains, [w_ff_in]
     )
 
     dpre, hid, keep, send = feed_hidden(place, a3, gy, dhid, w1_near, cols_out)
@@ -1357,7 +1440,7 @@
     keep, send, h2_near = feed_weights(place, a3, dpre, cols_in, [h2])
     b_in, b_jn = weight_buckets(cols_in, keep, send, orders, y_bits)
     send_round(30, b_out)
-    dh2, gain_ff_grad = feed_back(dpre, w1_near, h2_near, gain_ff, gy)
+    dh2, gain_ff_grad = feed_back(dpre, w1_near, h2_near, gains, gy)
     send_round(8, b_in, b_jn)
     pairs = heads // 2
     parts_a = cross_backward(0, pairs // 2, dh2, o2, inv, cq, kv, e, wco_near, [])
@@ -1366,42 +1449,43 @@
     )
     wcq_near, h1_near, a2, o2, o1, enc, wkv_near = parts_b[3:]
     dcq, dkt, dvt = zip(parts_a, parts_b[:3])
-    dh1, gain_cross_grad = cross_query_back(dcq, wcq_near, h1_near, gain_cross, dh2)
+    dh1, gain_cross_grad = cross_query_back(dcq, wcq_near, h1_near, gains, dh2)
     send_round(12, b_jn, b_out, b_in)
     genc, keep, send, hid, w2_near, h2_near = cross_weights(
         place, dh2, o2, dcq, dkt, dvt, enc, a2, wkv_near, dh1, o1, cols_x, [hid, w_ff_out, h2]
     )
     enc_rows = chunks * shard_rows * width // 128
-    b_enc = Bucket(
-        enc_rows, [(in_hbm(genc.reshape(enc_rows, shard_rows)), 0)], [("blk", b) for b in bits]
-    )
+    genc = in_hbm(genc.reshape(enc_rows, shard_rows))
+    cut = enc_rows // blocks * (2 * blocks // 3)
+    b_ea = Bucket(cut, [(genc, 0)], [("blk", b) for b in orders[0]])
+    b_eb = Bucket(enc_rows - cut, [(genc, cut)], [("blk", b) for b in orders[1]])
     b_xa, b_xb = weight_buckets(cols_x, keep, send, orders, y_bits)
     out, wso_near, qkv, p1 = feed_out(hid, w2_near, h2_near, [w_self_out, qkv, p1])
-    send_round(40, b_in, b_jn, b_enc, b_out)
+    send_round(40, b_ea, b_out, b_eb, b_jn)
     dqkv, gbias, wqkv_near, x_near, a1 = self_backward(
         dh1, wso_near, qkv, p1, bucket_count, heads, [w_qkv, x, a1]
     )
-    send_round(8, b_xa, b_xb, b_enc, b_out, settle=[b_in, b_jn])
+    send_round(8, b_xb, b_xa, b_eb, b_ea, b_in, b_out, settle=[b_jn])
     grad_dec, keep, send = self_weights(
-        place, dh1, a1, dqkv, x_near, gain_self, wqkv_near, gbias, gain_cross_grad, gain_ff_grad, cols_s
+        place, dh1, a1, dqkv, x_near, gains, wqkv_near, gbias, gain_cross_grad, gain_ff_grad, cols_s
     )
     b_sa, b_sb, b_misc = weight_buckets(cols_s, keep, send, orders, y_bits)
-    send_round(25, b_xa, b_xb, b_enc, settle=[b_out])
-    send_round(4, b_sa, b_misc, b_sb)
+    send_round(25, b_xb, b_xa, b_ea, b_eb, settle=[b_in, b_out])
+    send_round(4, b_sb, b_sa, b_misc)
     rest_of(b_out, b_in, b_jn)
     total_ff = Total([(cols_out, [b_out]), (cols_in, [b_in, b_jn])], [], dp_size)
-    send_round(4, b_xa, b_xb, total_ff)
-    rest_of(b_enc)
+    send_round(4, b_xa, b_xb, total_ff, settle=[b_ea, b_eb])
+    rest_of(b_ea, b_eb)
     send_round(4, b_sa, b_misc, b_sb)
     send_round(4, b_xb, b_sa, b_misc, total_ff)
-    grad_enc = join_encodings([b_enc], shard_rows, width)
+    grad_enc = join_encodings([b_ea, b_eb], shard_rows, width)
     send_round(4, b_sb)
     rest_of(total_ff)
     grad_ff_out, grad_ff_in = total_ff.finish(place, [[("out", stack)], [("in", 1)]])
+    send_round(4, b_sb)
     rest_of(b_xa, b_xb)
     total_x = Total([(cols_x, [b_xa, b_xb])], [], dp_size)
     send_round(4, total_x)
-    send_round(4, b_sb)
     rest_of(b_sa, b_sb, b_misc)
     total_s = Total([(cols_s, [b_sa, b_sb])], [b_misc], dp_size)
     send_round(4, total_s, total_x)

time: 245 us -> 230 us (0.939)
  Pallas kernels: 145 us -> 136 us
  local copies, waits for them, and re-layouts: 6.65 us -> 2.05 us
    pallas_call x52, Pallas kernels: 145 us -> 136 us  [call(): pl.pallas_call(ordered, out_shape=tuple(out_shape), grid_spec=pltpu.Prefe...]
    unnamed x35 -> x19, local copies, waits for them, and re-layouts: 5.96 us -> 1.36 us
where the time goes in v1:
time: 230 us; the launch traced here: 229 us
  Pallas kernels  136 us (59%)
  waiting for transfers between devices  51.4 us (22%)
  starting transfers between devices  37.1 us (16%)
    pallas_call x52, Pallas kernels, call(): pl.pallas_call(ordered, out_shape=tuple(out_shape), grid_spec=pltpu.Prefe...  136 us
    ppermute x41, waiting for transfers between devices, swap(): return lax.ppermute(value, axis, [(i, i ^ bit) for i in range(size)])  51.4 us
    ppermute x41, starting transfers between devices, swap(): return lax.ppermute(value, axis, [(i, i ^ bit) for i in range(size)])  37.1 us
  transfers between devices with their start and end apart: 41, of which 15 were waited for; matrix products, arithmetic and copies ran while one was open for 0% of the time, Pallas kernels for 43%

profile of v1, /device:TPU:1, one launch (start us, length us, event | category | flops | bytes accessed | tf_op | source)
XLA Modules:
  0.0 228.9 jit_solution(9190414397048605738)
XLA Ops:
  2.3 3.2 %collective-permute-start = (bf16[1,144,768]{2,1,0:T(8,128)(2,1)S(1)}, bf16[1,144,768]{2,1,0:T(8,128)(2,1)S(1)}, u32[]{:S(2)}, u32[]{:S(2)}) collective-permute-start(bf16[1,144,768]{2,1,0:T(8,128)(2,1)S(1)} %fusion.2.refs_0_), channel_id=1, source_target_pairs={{0,4},{1,5},{2,6},{3,7},{4,0},{5,1},{6,2},{7,3},{8,12},{9,13},{10,... | collective-permute-start | bytes 663560 | tf_op jit(solution)/shard_map/ppermute | solution.py:1084
  8.1 11.2 %self_attention.1 = (bf16[512,768]{1,0:T(8,128)(2,1)}, bf16[512,2304]{1,0:T(8,128)(2,1)}, bf16[4,6,128,256]{3,2,1,0:T(8,128)(2,1)}, bf16[512,768]{1,0:T(8,128)(2...) custom-call(bf16[512,768]{1,0:T(8,128)(2,1)} %bitcast.462, ...), custom_call_target="tpu_custom_call" | custom-call | flops 1153000 | tf_op jit(solution)/shard_map/self_attention/pallas_call | solution.py:246
  19.6 2.8 %self_project.1 = (f32[512,768]{1,0:T(8,128)S(1)}, bf16[512,768]{1,0:T(8,128)(2,1)S(1)}, f32[512,768]{1,0:T(8,128)}, bf16[512,768]{1,0:T(8,128)(2,1)}, bf16[512,...) custom-call(bf16[512,768]{1,0:T(8,128)(2,1)S(1)} %get-tuple-element.167.refs_0_, ...), custom_call_target="tpu_custom_call" | custom-call | flops 1153000 | tf_op jit(solution)/shard_map/self_project/pallas_call | solution.py:246
  25.9 4.7 %hidden_gradient.1 = (bf16[512,3072]{1,0:T(8,128)(2,1)S(1)}, bf16[768,1536]{1,0:T(8,128)(2,1)S(1)}, bf16[768,768]{1,0:T(8,128)(2,1)S(1)}, f32[8,128]{1,0:T(8,128)}) custom-call(bf16[512,768]{1,0:T(8,128)(2,1)S(1)} %get-tuple-element.174.refs_0_.refs_2_.refs_4_, bf16[3072,768]{1,0:T(8,128)(2,1)} %refs_15_.1, bf16[768,1536]{1,0:T(8,128)(2,1)} %refs_14_.3, ...), custom_call_target="tpu_custom_call" | custom-call | flops 1153000 | tf_op jit(solution)/shard_map/hidden_gradient/pallas_call | solution.py:246
  32.7 17.5 %cross_forward.1 = (bf16[1024,768]{1,0:T(8,128)(2,1)}, bf16[1024,1536]{1,0:T(8,128)(2,1)}, bf16[12,512,1024]{2,1,0:T(8,128)(2,1)}, f32[512,768]{1,0:T(8,128)}, b...) custom-call(bf16[1,144,768]{2,1,0:T(8,128)(2,1)S(1)} %fusion.2.refs_, ...), custom_call_target="tpu_custom_call" | custom-call | flops 1153000 | tf_op jit(solution)/shard_map/cross_forward/pallas_call | solution.py:246
  50.2 10.1 %feed_hidden.1 = (bf16[512,3072]{1,0:T(8,128)(2,1)S(1)}, bf16[512,3072]{1,0:T(8,128)(2,1)}, bf16[96,96,128]{2,1,0:T(8,128)(2,1)}, bf16[96,96,128]{2,1,0:T(8,128)(2,1)}, f32[8,128]{1,0:T(8,128)}) custom-call(s32[403]{0:T(512)S(1)} %pad_add_fusion.refs_0_, bf16[512,768]{1,0:T(8,128)(2,1)S(1)} %get-tuple-element.179.refs_1_, ...), custom_call_target="tpu_custom_call" | custom-call | flops 1153000 | tf_op jit(solution)/shard_map/feed_hidden/pallas_call | solution.py:246
  63.0 5.4 %feed_weights.1 = (bf16[96,96,128]{2,1,0:T(8,128)(2,1)}, bf16[96,96,128]{2,1,0:T(8,128)(2,1)}, f32[512,768]{1,0:T(8,128)S(1)}, f32[8,128]{1,0:T(8,128)}) custom-call(s32[403]{0:T(512)S(1)} %pad_add_fusion.refs_0_, bf16[512,768]{1,0:T(8,128)(2,1)S(1)} %get-tuple-element.179.refs_1_, bf16[512,3072]{1,0:T(8,128)(2,1)S(1)} %get-tuple-element.183.refs_2_.refs_0_, ...), custom_call_target="tpu_custom_call" | custom-call | flops 1153000 | tf_op jit(solution)/shard_map/feed_weights/pallas_call | solution.py:246
  71.3 4.4 %feed_back.1 = (f32[512,768]{1,0:T(8,128)S(1)}, f32[1,768]{1,0:T(1,128)S(1)}, f32[8,128]{1,0:T(8,128)}) custom-call(bf16[512,3072]{1,0:T(8,128)(2,1)S(1)} %get-tuple-element.183.refs_2_.refs_0_, bf16[768,3072]{1,0:T(8,128)(2,1)S(1)} %get-tuple-element.181.refs_4_.refs_1_, f32[512,768]{1,0:T(8,128)S(1)} %get-tuple-element.186.refs_2_, ...), custom_call_target="tpu_custom_call" | custom-call | flops 1153000 | tf_op jit(solution)/shard_map/feed_back/pallas_call | solution.py:246
  78.7 8.9 %cross_backward.2 = (bf16[512,384]{1,0:T(8,128)(2,1)S(1)}, bf16[384,1024]{1,0:T(8,128)(2,1)S(1)}, bf16[384,1024]{1,0:T(8,128)(2,1)S(1)}, f32[8,128]{1,0:T(8,128)}) custom-call(f32[512,768]{1,0:T(8,128)S(1)} %get-tuple-element.191.refs_0_.refs_5_.refs_1_, bf16[768,768]{1,0:T(8,128)(2,1)S(1)} %get-tuple-element.177.refs_12_.refs_1_, ...), custom_call_target="tpu_custom_call" | custom-call | flops 1153000 | tf_op jit(solution)/shard_map/cross_backward/pallas_call | solution.py:246
  87.6 9.0 %cross_backward.3 = (bf16[512,384]{1,0:T(8,128)(2,1)S(1)}, bf16[384,1024]{1,0:T(8,128)(2,1)S(1)}, bf16[384,1024]{1,0:T(8,128)(2,1)S(1)}, bf16[768,768]{1,0:T(8,1...) custom-call(f32[512,768]{1,0:T(8,128)S(1)} %get-tuple-element.191.re, ...), custom_call_target="tpu_custom_call" | custom-call | flops 1153000 | tf_op jit(solution)/shard_map/cross_backward/pallas_call | solution.py:246
  100.8 13.2 %cross_weights.1 = (bf16[48,128,128]{2,1,0:T(8,128)(2,1)}, bf16[120,96,128]{2,1,0:T(8,128)(2,1)}, bf16[120,96,128]{2,1,0:T(8,128)(2,1)}, bf16[512,3072]{1,0:T(8,...) custom-call(s32[403]{0:T(512)S(1)} %pad_add_fusion.refs_0_, ...), custom_call_target="tpu_custom_call" | custom-call | flops 1153000 | tf_op jit(solution)/shard_map/cross_weights/pallas_call | solution.py:246
  116.8 4.4 %feed_out.1 = (bf16[512,768]{1,0:T(8,128)(2,1)}, bf16[768,768]{1,0:T(8,128)(2,1)S(1)}, bf16[512,2304]{1,0:T(8,128)(2,1)S(1)}, bf16[4,6,128,256]{3,2,1,0:T(8,128)(2,1)S(1)}, f32[8,128]{1,0:T(8,128)}) custom-call(bf16[512,3072]{1,0:T(8,128)(2,1)S(1)} %get-tuple-element.227.refs_0_, bf16[3072,768]{1,0:T(8,128)(2,1)S(1)} %get-tuple-element.228.refs_1_, ...), custom_call_target="tpu_custom_call" | custom-call | flops 1153000 | tf_op jit(solution)/shard_map/feed_out/pallas_call | solution.py:246
  124.4 7.5 %self_backward.1 = (bf16[512,2304]{1,0:T(8,128)(2,1)S(1)}, f32[16,128]{1,0:T(8,128)S(1)}, bf16[768,2304]{1,0:T(8,128)(2,1)S(1)}, bf16[512,768]{1,0:T(8,128)(2,1)...) custom-call(f32[512,768]{1,0:T(8,128)S(1)} %get-tuple-element.211.refs_2_.refs_0_.refs_1_, ...), custom_call_target="tpu_custom_call" | custom-call | flops 1153000 | tf_op jit(solution)/shard_map/self_backward/pallas_call | solution.py:246
  131.9 4.5 %collective-permute-done.17.refs_21_ = bf16[576,128]{1,0:T(8,128)(2,1)S(1)} collective-permute-done((bf16[576,128]{1,0:T(8,128)(2,1)S(1)}, bf16[576,128]{1,0:T(8,128)(2,1)S(1)}, u32[]{:S(2)}, u32[]{:S(2)}) %collective-permute-start.17) | collective-permute-done | bytes 147488 | tf_op jit(solution)/shard_map/ppermute | solution.py:1084
  144.1 8.2 %self_weights.1 = (f32[512,768]{1,0:T(8,128)}, bf16[73,96,128]{2,1,0:T(8,128)(2,1)}, bf16[73,96,128]{2,1,0:T(8,128)(2,1)}, f32[8,128]{1,0:T(8,128)}) custom-call(s32[403]{0:T(512)S(1)} %pad_add_fusion.refs_0_, f32[512,768]{1,0:T(8,128)S(1)} %get-tuple-element.211.refs_2_.refs_0_.refs_1_, bf16[768,2304]{1,0:T(8,128)(2,1)S(1)} %get-tuple-element.242.refs_2_, ...), custom_call_target="tpu_custom_call" | custom-call | flops 1153000 | tf_op jit(solution)/shard_map/self_weights/pallas_call | solution.py:246
  152.3 3.2 %collective-permute-start.25 = (bf16[7008,128]{1,0:T(8,128)(2,1)}, bf16[7008,128]{1,0:T(8,128)(2,1)S(1)}, u32[]{:S(2)}, u32[]{:S(2)}) collective-permute-start(bf16[7008,128]{1,0:T(8,128)(2,1)} %bitcast.470), channel_id=1, source_target_pairs={{0,8},{8,0},{16,24},{24,16},{1,9},{9,1},{17,25},{25,17},{2,10},{10... | collective-permute-start | bytes 5382152 | tf_op jit(solution)/shard_map/ppermute | solution.py:1084
  155.5 3.1 %collective-permute-done.21.refs_16_.refs_22_ = bf16[1152,128]{1,0:T(8,128)(2,1)S(1)} collective-permute-done((bf16[1152,128]{1,0:T(8,128)(2,1)S(1)}, bf16[1152,128]{1,0:T(8,128)(2,1)S(1)}, u32[]{:S(2)}, u32[]{:S(2)}) %collective-permute-start.21) | collective-permute-done | bytes 294944 | tf_op jit(solution)/shard_map/ppermute | solution.py:1084
  166.2 7.3 %collective-permute-done.24.refs_14_.refs_18_ = bf16[768,128]{1,0:T(8,128)(2,1)S(1)} collective-permute-done((bf16[768,128]{1,0:T(8,128)(2,1)S(1)}, bf16[768,128]{1,0:T(8,128)(2,1)S(1)}, u32[]{:S(2)}, u32[]{:S(2)}) %collective-permute-start.24) | collective-permute-done | bytes 196640 | tf_op jit(solution)/shard_map/ppermute | solution.py:1084
  173.5 3.6 %collective-permute-done.22.refs_3_ = bf16[1344,128]{1,0:T(8,128)(2,1)S(1)} collective-permute-done((bf16[1344,128]{1,0:T(8,128)(2,1)S(1)}, bf16[1344,128]{1,0:T(8,128)(2,1)S(1)}, u32[]{:S(2)}, u32[]{:S(2)}) %collective-permute-start.22) | collective-permute-done | bytes 344096 | tf_op jit(solution)/shard_map/ppermute | solution.py:1084
  181.7 6.5 %collective-permute-done.26.refs_4_.refs_9_ = bf16[768,128]{1,0:T(8,128)(2,1)S(1)} collective-permute-done((bf16[768,128]{1,0:T(8,128)(2,1)S(1)}, bf16[768,128]{1,0:T(8,128)(2,1)S(1)}, u32[]{:S(2)}, u32[]{:S(2)}) %collective-permute-start.26) | collective-permute-done | bytes 196640 | tf_op jit(solution)/shard_map/ppermute | solution.py:1084
  188.6 3.2 %collective-permute-done.29.refs_8_.refs_10_.refs_3_ = bf16[672,128]{1,0:T(8,128)(2,1)S(1)} collective-permute-done((bf16[672,128]{1,0:T(8,128)(2,1)S(1)}, bf16[672,128]{1,0:T(8,128)(2,1)S(1)}, u32[]{:S(2)}, u32[]{:S(2)}) %collective-permute-start.29) | collective-permute-done | bytes 172064 | tf_op jit(solution)/shard_map/ppermute | solution.py:1084
  200.6 5.9 %collective-permute-done.33.refs_4_.refs_9_ = bf16[576,128]{1,0:T(8,128)(2,1)S(1)} collective-permute-done((bf16[576,128]{1,0:T(8,128)(2,1)S(1)}, bf16[576,128]{1,0:T(8,128)(2,1)S(1)}, u32[]{:S(2)}, u32[]{:S(2)}) %collective-permute-start.33) | collective-permute-done | bytes 147488 | tf_op jit(solution)/shard_map/ppermute | solution.py:1084
  209.0 4.1 %collective-permute-done.35.refs_10_ = bf16[288,128]{1,0:T(8,128)(2,1)S(1)} collective-permute-done((bf16[288,128]{1,0:T(8,128)(2,1)S(1)}, bf16[288,128]{1,0:T(8,128)(2,1)S(1)}, u32[]{:S(2)}, u32[]{:S(2)}) %collective-permute-start.35) | collective-permute-done | bytes 73760 | tf_op jit(solution)/shard_map/ppermute | solution.py:1084
  221.2 3.1 %collective-permute-start.39 = (bf16[960,128]{1,0:T(8,128)(2,1)S(1)}, bf16[960,128]{1,0:T(8,128)(2,1)S(1)}, u32[]{:S(2)}, u32[]{:S(2)}) collective-permute-start(bf16[960,128]{1,0:T(8,128)(2,1)S(1)} %get-tuple-element.296.refs_1_), channel_id=1, source_target_pairs={{0,8},{8,0},{16,24},{24,16},{1,9},{9,1},{17,25},{25,17},{2,10},{10... | collective-permute-start | bytes 737288 | tf_op jit(solution)/shard_map/ppermute | solution.py:1084
  (141 shorter events, 72.9 us)
Async XLA Ops:
  2.3 17.0 %collective-permute-start = (bf16[1,144,768]{2,1,0:T(8,128)(2,1)S(1)}, bf16[1,144,768]{2,1,0:T(8,128)(2,1)S(1)}, u32[]{:S(2)}, u32[]{:S(2)}) collective-permute-start(bf16[1,144,768]{2,1,0:T(8,128)(2,1)S(1)} %fusion.2.refs_0_), channel_id=1, source_target_pairs={{0,4},{1,5},{2,6},{3,7},{4,0},{5,1},{6,2},{7,3},{8,12},{9,13},{10,... | collective-permute-start | bytes 663560 | tf_op jit(solution)/shard_map/ppermute | solution.py:1084
  5.5 17.2 %collective-permute-start.2 = (bf16[1,144,768]{2,1,0:T(8,128)(2,1)S(1)}, bf16[1,144,768]{2,1,0:T(8,128)(2,1)}, u32[]{:S(2)}, u32[]{:S(2)}) collective-permute-start(bf16[1,144,768]{2,1,0:T(8,128)(2,1)S(1)} %fusion.2.refs_0_), channel_id=1, source_target_pairs={{0,2},{1,3},{2,0},{3,1},{4,6},{5,7},{6,4},{7,5},{8,10},{9,11},{10,... | collective-permute-start | bytes 663560 | tf_op jit(solution)/shard_map/ppermute | solution.py:1084
  6.8 23.8 %collective-permute-start.1 = (bf16[1,144,768]{2,1,0:T(8,128)(2,1)S(1)}, bf16[1,144,768]{2,1,0:T(8,128)(2,1)}, u32[]{:S(2)}, u32[]{:S(2)}) collective-permute-start(bf16[1,144,768]{2,1,0:T(8,128)(2,1)S(1)} %fusion.2.refs_0_), channel_id=1, source_target_pairs={{0,1},{1,0},{2,3},{3,2},{4,5},{5,4},{6,7},{7,6},{8,9},{9,8},{10,11... | collective-permute-start | bytes 663560 | tf_op jit(solution)/shard_map/ppermute | solution.py:1084
  70.0 28.1 %collective-permute-start.10 = (bf16[4608,128]{1,0:T(8,128)(2,1)S(1)}, bf16[4608,128]{1,0:T(8,128)(2,1)S(1)}, u32[]{:S(2)}, u32[]{:S(2)}) collective-permute-start(bf16[4608,128]{1,0:T(8,128)(2,1)S(1)} %get-tuple-element.223), channel_id=1, source_target_pairs={{0,16},{8,24},{16,0},{24,8},{1,17},{9,25},{17,1},{25,9},{2,18},{10... | collective-permute-start | bytes 3538952 | tf_op jit(solution)/shard_map/ppermute | solution.py:1084
  77.2 20.9 %collective-permute-start.11 = (bf16[2304,128]{1,0:T(8,128)(2,1)S(1)}, bf16[2304,128]{1,0:T(8,128)(2,1)S(1)}, u32[]{:S(2)}, u32[]{:S(2)}) collective-permute-start(bf16[2304,128]{1,0:T(8,128)(2,1)S(1)} %get-tuple-element.224), channel_id=1, source_target_pairs={{0,1},{1,0},{2,3},{3,2},{4,5},{5,4},{6,7},{7,6},{8,9},{9,8},{10,11... | collective-permute-start | bytes 1769480 | tf_op jit(solution)/shard_map/ppermute | solution.py:1084
  78.5 19.6 %collective-permute-start.9 = (bf16[2304,128]{1,0:T(8,128)(2,1)S(1)}, bf16[2304,128]{1,0:T(8,128)(2,1)S(1)}, u32[]{:S(2)}, u32[]{:S(2)}) collective-permute-start(bf16[2304,128]{1,0:T(8,128)(2,1)S(1)} %get-tuple-element.222), channel_id=1, source_target_pairs={{0,2},{1,3},{2,0},{3,1},{4,6},{5,7},{6,4},{7,5},{8,10},{9,11},{10,... | collective-permute-start | bytes 1769480 | tf_op jit(solution)/shard_map/ppermute | solution.py:1084
  100.4 20.9 %collective-permute-start.12 = (bf16[3456,128]{1,0:T(8,128)(2,1)S(1)}, bf16[3456,128]{1,0:T(8,128)(2,1)S(1)}, u32[]{:S(2)}, u32[]{:S(2)}) collective-permute-start(bf16[3456,128]{1,0:T(8,128)(2,1)S(1)} %get-tuple-element.239), channel_id=1, source_target_pairs={{0,1},{1,0},{2,3},{3,2},{4,5},{5,4},{6,7},{7,6},{8,9},{9,8},{10,11... | collective-permute-start | bytes 2654216 | tf_op jit(solution)/shard_map/ppermute | solution.py:1084
  114.0 25.0 %collective-permute-start.13 = (bf16[11520,128]{1,0:T(8,128)(2,1)}, bf16[11520,128]{1,0:T(8,128)(2,1)S(1)}, u32[]{:S(2)}, u32[]{:S(2)}) collective-permute-start(bf16[11520,128]{1,0:T(8,128)(2,1)} %bitcast.467), channel_id=1, source_target_pairs={{0,8},{8,0},{16,24},{24,16},{1,9},{9,1},{17,25},{25,17},{2,10},{10... | collective-permute-start | bytes 8847368 | tf_op jit(solution)/shard_map/ppermute | solution.py:1084
  115.7 16.2 %collective-permute-start.16 = (bf16[1152,128]{1,0:T(8,128)(2,1)}, bf16[1152,128]{1,0:T(8,128)(2,1)S(1)}, u32[]{:S(2)}, u32[]{:S(2)}) collective-permute-start(bf16[1152,128]{1,0:T(8,128)(2,1)} %get-tuple-element.253), channel_id=1, source_target_pairs={{0,2},{1,3},{2,0},{3,1},{4,6},{5,7},{6,4},{7,5},{8,10},{9,11},{10,... | collective-permute-start | bytes 884744 | tf_op jit(solution)/shard_map/ppermute | solution.py:1084
  122.9 16.1 %collective-permute-start.14 = (bf16[2176,128]{1,0:T(8,128)(2,1)S(1)}, bf16[2176,128]{1,0:T(8,128)(2,1)S(1)}, u32[]{:S(2)}, u32[]{:S(2)}) collective-permute-start(bf16[2176,128]{1,0:T(8,128)(2,1)S(1)} %get-tuple-element.251), channel_id=1, source_target_pairs={{0,2},{1,3},{2,0},{3,1},{4,6},{5,7},{6,4},{7,5},{8,10},{9,11},{10,... | collective-permute-start | bytes 1671176 | tf_op jit(solution)/shard_map/ppermute | solution.py:1084
  123.3 13.1 %collective-permute-start.15 = (bf16[2048,128]{1,0:T(8,128)(2,1)S(1)}, bf16[2048,128]{1,0:T(8,128)(2,1)S(1)}, u32[]{:S(2)}, u32[]{:S(2)}) collective-permute-start(bf16[2048,128]{1,0:T(8,128)(2,1)S(1)} %get-tuple-element.252), channel_id=1, source_target_pairs={{0,1},{1,0},{2,3},{3,2},{4,5},{5,4},{6,7},{7,6},{8,9},{9,8},{10,11... | collective-permute-start | bytes 1572872 | tf_op jit(solution)/shard_map/ppermute | solution.py:1084
  124.3 12.1 %collective-permute-start.17 = (bf16[576,128]{1,0:T(8,128)(2,1)S(1)}, bf16[576,128]{1,0:T(8,128)(2,1)S(1)}, u32[]{:S(2)}, u32[]{:S(2)}) collective-permute-start(bf16[576,128]{1,0:T(8,128)(2,1)S(1)} %get-tuple-element.254), channel_id=1, source_target_pairs={{0,4},{1,5},{2,6},{3,7},{4,0},{5,1},{6,2},{7,3},{8,12},{9,13},{10,... | collective-permute-start | bytes 442376 | tf_op jit(solution)/shard_map/ppermute | solution.py:1084
  141.4 19.8 %collective-permute-start.18 = (bf16[3200,128]{1,0:T(8,128)(2,1)S(1)}, bf16[3200,128]{1,0:T(8,128)(2,1)S(1)}, u32[]{:S(2)}, u32[]{:S(2)}) collective-permute-start(bf16[3200,128]{1,0:T(8,128)(2,1)S(1)} %get-tuple-element.258), channel_id=1, source_target_pairs={{0,1},{1,0},{2,3},{3,2},{4,5},{5,4},{6,7},{7,6},{8,9},{9,8},{10,11... | collective-permute-start | bytes 2457608 | tf_op jit(solution)/shard_map/ppermute | solution.py:1084
  143.6 17.6 %collective-permute-start.19 = (bf16[3072,128]{1,0:T(8,128)(2,1)S(1)}, bf16[3072,128]{1,0:T(8,128)(2,1)S(1)}, u32[]{:S(2)}, u32[]{:S(2)}) collective-permute-start(bf16[3072,128]{1,0:T(8,128)(2,1)S(1)} %get-tuple-element.259), channel_id=1, source_target_pairs={{0,16},{8,24},{16,0},{24,8},{1,17},{9,25},{17,1},{25,9},{2,18},{10... | collective-permute-start | bytes 2359304 | tf_op jit(solution)/shard_map/ppermute | solution.py:1084
  143.6 14.9 %collective-permute-start.21 = (bf16[1152,128]{1,0:T(8,128)(2,1)S(1)}, bf16[1152,128]{1,0:T(8,128)(2,1)S(1)}, u32[]{:S(2)}, u32[]{:S(2)}) collective-permute-start(bf16[1152,128]{1,0:T(8,128)(2,1)S(1)} %get-tuple-element.261), channel_id=1, source_target_pairs={{0,4},{1,5},{2,6},{3,7},{4,0},{5,1},{6,2},{7,3},{8,12},{9,13},{10,... | collective-permute-start | bytes 884744 | tf_op jit(solution)/shard_map/ppermute | solution.py:1084
  152.3 11.7 %collective-permute-start.25 = (bf16[7008,128]{1,0:T(8,128)(2,1)}, bf16[7008,128]{1,0:T(8,128)(2,1)S(1)}, u32[]{:S(2)}, u32[]{:S(2)}) collective-permute-start(bf16[7008,128]{1,0:T(8,128)(2,1)} %bitcast.470), channel_id=1, source_target_pairs={{0,8},{8,0},{16,24},{24,16},{1,9},{9,1},{17,25},{25,17},{2,10},{10... | collective-permute-start | bytes 5382152 | tf_op jit(solution)/shard_map/ppermute | solution.py:1084
  163.0 14.1 %collective-permute-start.23 = (bf16[1536,128]{1,0:T(8,128)(2,1)S(1)}, bf16[1536,128]{1,0:T(8,128)(2,1)S(1)}, u32[]{:S(2)}, u32[]{:S(2)}) collective-permute-start(bf16[1536,128]{1,0:T(8,128)(2,1)S(1)} %get-tuple-element.264), channel_id=1, source_target_pairs={{0,1},{1,0},{2,3},{3,2},{4,5},{5,4},{6,7},{7,6},{8,9},{9,8},{10,11... | collective-permute-start | bytes 1179656 | tf_op jit(solution)/shard_map/ppermute | solution.py:1084
  164.0 13.1 %collective-permute-start.22 = (bf16[1344,128]{1,0:T(8,128)(2,1)S(1)}, bf16[1344,128]{1,0:T(8,128)(2,1)S(1)}, u32[]{:S(2)}, u32[]{:S(2)}) collective-permute-start(bf16[1344,128]{1,0:T(8,128)(2,1)S(1)} %get-tuple-element.263), channel_id=1, source_target_pairs={{0,2},{1,3},{2,0},{3,1},{4,6},{5,7},{6,4},{7,5},{8,10},{9,11},{10,... | collective-permute-start | bytes 1032200 | tf_op jit(solution)/shard_map/ppermute | solution.py:1084
  165.5 13.3 %collective-permute-start.28 = (bf16[2304,128]{1,0:T(8,128)(2,1)S(1)}, bf16[2304,128]{1,0:T(8,128)(2,1)S(1)}, u32[]{:S(2)}, u32[]{:S(2)}) collective-permute-start(bf16[2304,128]{1,0:T(8,128)(2,1)S(1)} %get-tuple-element.275), channel_id=1, source_target_pairs={{0,16},{8,24},{16,0},{24,8},{1,17},{9,25},{17,1},{25,9},{2,18},{10... | collective-permute-start | bytes 1769480 | tf_op jit(solution)/shard_map/ppermute | solution.py:1084
  165.6 13.2 %collective-permute-start.27 = (bf16[1248,128]{1,0:T(8,128)(2,1)S(1)}, bf16[1248,128]{1,0:T(8,128)(2,1)S(1)}, u32[]{:S(2)}, u32[]{:S(2)}) collective-permute-start(bf16[1248,128]{1,0:T(8,128)(2,1)S(1)} %get-tuple-element.274.refs_3_), channel_id=1, source_target_pairs={{0,1},{1,0},{2,3},{3,2},{4,5},{5,4},{6,7},{7,6},{8,9},{9,8},{10,11... | collective-permute-start | bytes 958472 | tf_op jit(solution)/shard_map/ppermute | solution.py:1084
  178.7 28.7 %collective-permute-start.36 = (bf16[672,128]{1,0:T(8,128)(2,1)S(1)}, bf16[672,128]{1,0:T(8,128)(2,1)S(1)}, u32[]{:S(2)}, u32[]{:S(2)}) collective-permute-start(bf16[672,128]{1,0:T(8,128)(2,1)S(1)} %get-tuple-element.290), channel_id=1, source_target_pairs={{0,4},{1,5},{2,6},{3,7},{4,0},{5,1},{6,2},{7,3},{8,12},{9,13},{10,... | collective-permute-start | bytes 516104 | tf_op jit(solution)/shard_map/ppermute | solution.py:1084
  180.0 11.8 %collective-permute-start.29 = (bf16[672,128]{1,0:T(8,128)(2,1)S(1)}, bf16[672,128]{1,0:T(8,128)(2,1)S(1)}, u32[]{:S(2)}, u32[]{:S(2)}) collective-permute-start(bf16[672,128]{1,0:T(8,128)(2,1)S(1)} %get-tuple-element.277.refs_9_), channel_id=1, source_target_pairs={{0,2},{1,3},{2,0},{3,1},{4,6},{5,7},{6,4},{7,5},{8,10},{9,11},{10,... | collective-permute-start | bytes 516104 | tf_op jit(solution)/shard_map/ppermute | solution.py:1084
  181.5 14.3 %collective-permute-start.32 = (bf16[1152,128]{1,0:T(8,128)(2,1)S(1)}, bf16[1152,128]{1,0:T(8,128)(2,1)S(1)}, u32[]{:S(2)}, u32[]{:S(2)}) collective-permute-start(bf16[1152,128]{1,0:T(8,128)(2,1)S(1)} %get-tuple-element.283), channel_id=1, source_target_pairs={{0,1},{1,0},{2,3},{3,2},{4,5},{5,4},{6,7},{7,6},{8,9},{9,8},{10,11... | collective-permute-start | bytes 884744 | tf_op jit(solution)/shard_map/ppermute | solution.py:1084
  194.6 12.8 %collective-permute-start.31 = (bf16[768,128]{1,0:T(8,128)(2,1)S(1)}, bf16[768,128]{1,0:T(8,128)(2,1)S(1)}, u32[]{:S(2)}, u32[]{:S(2)}) collective-permute-start(bf16[768,128]{1,0:T(8,128)(2,1)S(1)} %get-tuple-element.282.refs_11_), channel_id=1, source_target_pairs={{0,4},{1,5},{2,6},{3,7},{4,0},{5,1},{6,2},{7,3},{8,12},{9,13},{10,... | collective-permute-start | bytes 589832 | tf_op jit(solution)/shard_map/ppermute | solution.py:1084
  (25 other events, 169.1 us)

commit v2 on v1

--- a/solution.py
+++ b/solution.py
@@ -264,8 +264,8 @@
     return got if outs or wanted else got[0]
 
 
-def shadow(cost):
-    call("shadow", lambda: None, (), (), (), (), cost=cost)
+def shadow(cost, *arrays):
+    call("shadow", lambda *_: None, (), [ANY] * len(arrays), (), arrays, cost=cost)
 
 
 def whole(*shape):
@@ -1137,7 +1137,6 @@
             else:
                 m.rows //= 2
                 jobs[-1].append((m.rows, [(array, off + m.rows) for array, off in m.terms]))
-    settle = [b for b in settle if not b.steps]
     if settle:
         jobs.append([(b.rows, b.terms) for b in settle])
     sent = sum_kernel(jobs)
@@ -1388,7 +1387,7 @@
     stack = hidden // width
     blocks = half // 128
     cols_out = layout([("out", stack * half)], (stack * blocks, "y"))
-    cols_in = layout([("in", hidden // 2)], (stack * blocks // 2, 0), (stack * blocks // 2, 1))
+    cols_in = layout([("in", hidden // 2)], (2 * stack * blocks // 3, 0), (stack * blocks // 3, 1))
     far_x, far_s = along_y(16 * blocks // 3), along_y(4 * blocks)
     near_x, near_s = 5 * blocks - far_x, 3 * blocks - far_s
     cols_x = layout(
@@ -1427,7 +1426,7 @@
         x_near, o1_near, wso_near, gains, wcq_near, [gy]
     )
     pieces, rel = third()
-    shadow(10)
+    shadow(10, *more[1:2])
     dhid, wkv_near, wco_near = hidden_gradient(gy, w_ff_out, [w_cross_kv, w_cross_out])
     spots = [[int(chunk_spot(r, bits)) for r in group] for group in rel]
     enc, kv, e, inv, o2, h2, a3, w1_near = cross_forward(
@@ -1460,8 +1459,8 @@
     b_ea = Bucket(cut, [(genc, 0)], [("blk", b) for b in orders[0]])
     b_eb = Bucket(enc_rows - cut, [(genc, cut)], [("blk", b) for b in orders[1]])
     b_xa, b_xb = weight_buckets(cols_x, keep, send, orders, y_bits)
+    send_round(40, b_ea, b_out, b_eb, b_jn, settle=[b_in])
     out, wso_near, qkv, p1 = feed_out(hid, w2_near, h2_near, [w_self_out, qkv, p1])
-    send_round(40, b_ea, b_out, b_eb, b_jn)
     dqkv, gbias, wqkv_near, x_near, a1 = self_backward(
         dh1, wso_near, qkv, p1, bucket_count, heads, [w_qkv, x, a1]
     )
@@ -1482,10 +1481,9 @@
     send_round(4, b_sb)
     rest_of(total_ff)
     grad_ff_out, grad_ff_in = total_ff.finish(place, [[("out", stack)], [("in", 1)]])
-    send_round(4, b_sb)
     rest_of(b_xa, b_xb)
     total_x = Total([(cols_x, [b_xa, b_xb])], [], dp_size)
-    send_round(4, total_x)
+    send_round(4, b_sb, total_x)
     rest_of(b_sa, b_sb, b_misc)
     total_s = Total([(cols_s, [b_sa, b_sb])], [b_misc], dp_size)
     send_round(4, total_s, total_x)

time: 230 us -> 223 us (0.970)
  waiting for transfers between devices: 51.4 us -> 35.7 us
  starting transfers between devices: 37.1 us -> 46.2 us
    ppermute x41, waiting for transfers between devices: 51.4 us -> 35.7 us  [swap(): return lax.ppermute(value, axis, [(i, i ^ bit) for i in range(size)])]
    ppermute x41, starting transfers between devices: 37.1 us -> 46.2 us  [swap(): return lax.ppermute(value, axis, [(i, i ^ bit) for i in range(size)])]
    pallas_call x52 -> x50, Pallas kernels: 136 us -> 134 us  [call(): pl.pallas_call(ordered, out_shape=tuple(out_shape), grid_spec=pltpu.Prefe...]
  transfers between devices with their start and end apart: 41 -> 41, of which waited for: 15 -> 12; matrix products, arithmetic and copies ran while one was open for 0% -> 0% of each run, Pallas kernels for 43% -> 44%
where the time goes in v2:
time: 223 us
  Pallas kernels  134 us (60%)
  starting transfers between devices  46.2 us (21%)
  waiting for transfers between devices  35.7 us (16%)
  local copies, waits for them, and re-layouts  3.49 us (2%)
    pallas_call x50, Pallas kernels, call(): pl.pallas_call(ordered, out_shape=tuple(out_shape), grid_spec=pltpu.Prefe...  134 us
    ppermute x41, starting transfers between devices, swap(): return lax.ppermute(value, axis, [(i, i ^ bit) for i in range(size)])  46.2 us
    ppermute x41, waiting for transfers between devices, swap(): return lax.ppermute(value, axis, [(i, i ^ bit) for i in range(size)])  35.7 us
  transfers between devices with their start and end apart: 41, of which 12 were waited for; matrix products, arithmetic and copies ran while one was open for 0% of the time, Pallas kernels for 44%

profile of v2, /device:TPU:1, one launch (start us, length us, event | category | flops | bytes accessed | tf_op | source)
XLA Modules:
  0.0 222.5 jit_solution(14484458539086048656)
XLA Ops:
  2.3 3.2 %collective-permute-start = (bf16[1,144,768]{2,1,0:T(8,128)(2,1)S(1)}, bf16[1,144,768]{2,1,0:T(8,128)(2,1)}, u32[]{:S(2)}, u32[]{:S(2)}) collective-permute-start(bf16[1,144,768]{2,1,0:T(8,128)(2,1)S(1)} %fusion.2.refs_0_), channel_id=1, source_target_pairs={{0,4},{1,5},{2,6},{3,7},{4,0},{5,1},{6,2},{7,3},{8,12},{9,13},{10,... | collective-permute-start | bytes 663560 | tf_op jit(solution)/shard_map/ppermute | solution.py:1084
  8.1 11.2 %self_attention.1 = (bf16[512,768]{1,0:T(8,128)(2,1)}, bf16[512,2304]{1,0:T(8,128)(2,1)}, bf16[4,6,128,256]{3,2,1,0:T(8,128)(2,1)}, bf16[512,768]{1,0:T(8,128)(2...) custom-call(bf16[512,768]{1,0:T(8,128)(2,1)} %bitcast.461, ...), custom_call_target="tpu_custom_call" | custom-call | flops 1153000 | tf_op jit(solution)/shard_map/self_attention/pallas_call | solution.py:246
  21.9 2.9 %self_project.1 = (f32[512,768]{1,0:T(8,128)S(1)}, bf16[512,768]{1,0:T(8,128)(2,1)S(1)}, f32[512,768]{1,0:T(8,128)}, bf16[512,768]{1,0:T(8,128)(2,1)}, bf16[512,...) custom-call(bf16[512,768]{1,0:T(8,128)(2,1)S(1)} %copy-done.2, ...), custom_call_target="tpu_custom_call" | custom-call | flops 1153000 | tf_op jit(solution)/shard_map/self_project/pallas_call | solution.py:246
  27.0 4.6 %hidden_gradient.1 = (bf16[512,3072]{1,0:T(8,128)(2,1)S(1)}, bf16[768,1536]{1,0:T(8,128)(2,1)S(1)}, bf16[768,768]{1,0:T(8,128)(2,1)S(1)}, f32[8,128]{1,0:T(8,128)}) custom-call(bf16[512,768]{1,0:T(8,128)(2,1)S(1)} %get-tuple-element.174.refs_0_.refs_2_.refs_4_, bf16[3072,768]{1,0:T(8,128)(2,1)} %refs_15_.1, bf16[768,1536]{1,0:T(8,128)(2,1)} %refs_14_.3, ...), custom_call_target="tpu_custom_call" | custom-call | flops 1153000 | tf_op jit(solution)/shard_map/hidden_gradient/pallas_call | solution.py:246
  31.7 17.6 %cross_forward.1 = (bf16[1024,768]{1,0:T(8,128)(2,1)}, bf16[1024,1536]{1,0:T(8,128)(2,1)}, bf16[12,512,1024]{2,1,0:T(8,128)(2,1)}, f32[512,768]{1,0:T(8,128)}, b...) custom-call(bf16[1,144,768]{2,1,0:T(8,128)(2,1)S(1)} %fusion.2.refs_, ...), custom_call_target="tpu_custom_call" | custom-call | flops 1153000 | tf_op jit(solution)/shard_map/cross_forward/pallas_call | solution.py:246
  49.3 10.1 %feed_hidden.1 = (bf16[512,3072]{1,0:T(8,128)(2,1)S(1)}, bf16[512,3072]{1,0:T(8,128)(2,1)}, bf16[96,96,128]{2,1,0:T(8,128)(2,1)}, bf16[96,96,128]{2,1,0:T(8,128)(2,1)}, f32[8,128]{1,0:T(8,128)}) custom-call(s32[403]{0:T(512)S(1)} %pad_add_fusion.refs_0_, bf16[512,768]{1,0:T(8,128)(2,1)S(1)} %get-tuple-element.179.refs_1_, ...), custom_call_target="tpu_custom_call" | custom-call | flops 1153000 | tf_op jit(solution)/shard_map/feed_hidden/pallas_call | solution.py:246
  59.4 2.7 %collective-permute-start.7 = (bf16[9216,128]{1,0:T(8,128)(2,1)}, bf16[9216,128]{1,0:T(8,128)(2,1)S(1)}, u32[]{:S(2)}, u32[]{:S(2)}) collective-permute-start(bf16[9216,128]{1,0:T(8,128)(2,1)} %bitcast.468), channel_id=1, source_target_pairs={{0,8},{8,0},{16,24},{24,16},{1,9},{9,1},{17,25},{25,17},{2,10},{10... | collective-permute-start | bytes 7077896 | tf_op jit(solution)/shard_map/ppermute | solution.py:1084
  62.1 5.4 %feed_weights.1 = (bf16[96,96,128]{2,1,0:T(8,128)(2,1)}, bf16[96,96,128]{2,1,0:T(8,128)(2,1)}, f32[512,768]{1,0:T(8,128)S(1)}, f32[8,128]{1,0:T(8,128)}) custom-call(s32[403]{0:T(512)S(1)} %pad_add_fusion.refs_0_, bf16[512,768]{1,0:T(8,128)(2,1)S(1)} %get-tuple-element.179.refs_1_, bf16[512,3072]{1,0:T(8,128)(2,1)S(1)} %get-tuple-element.183.refs_2_.refs_0_, ...), custom_call_target="tpu_custom_call" | custom-call | flops 1153000 | tf_op jit(solution)/shard_map/feed_weights/pallas_call | solution.py:246
  70.4 4.4 %feed_back.1 = (f32[512,768]{1,0:T(8,128)S(1)}, f32[1,768]{1,0:T(1,128)S(1)}, f32[8,128]{1,0:T(8,128)}) custom-call(bf16[512,3072]{1,0:T(8,128)(2,1)S(1)} %get-tuple-element.183.refs_2_.refs_0_, bf16[768,3072]{1,0:T(8,128)(2,1)S(1)} %get-tuple-element.181.refs_4_.refs_1_, f32[512,768]{1,0:T(8,128)S(1)} %get-tuple-element.186.refs_2_, ...), custom_call_target="tpu_custom_call" | custom-call | flops 1153000 | tf_op jit(solution)/shard_map/feed_back/pallas_call | solution.py:246
  77.9 8.9 %cross_backward.2 = (bf16[512,384]{1,0:T(8,128)(2,1)S(1)}, bf16[384,1024]{1,0:T(8,128)(2,1)S(1)}, bf16[384,1024]{1,0:T(8,128)(2,1)S(1)}, f32[8,128]{1,0:T(8,128)}) custom-call(f32[512,768]{1,0:T(8,128)S(1)} %get-tuple-element.191.refs_0_.refs_5_.refs_1_, bf16[768,768]{1,0:T(8,128)(2,1)S(1)} %get-tuple-element.177.refs_12_.refs_1_, ...), custom_call_target="tpu_custom_call" | custom-call | flops 1153000 | tf_op jit(solution)/shard_map/cross_backward/pallas_call | solution.py:246
  86.8 9.0 %cross_backward.3 = (bf16[512,384]{1,0:T(8,128)(2,1)S(1)}, bf16[384,1024]{1,0:T(8,128)(2,1)S(1)}, bf16[384,1024]{1,0:T(8,128)(2,1)S(1)}, bf16[768,768]{1,0:T(8,1...) custom-call(f32[512,768]{1,0:T(8,128)S(1)} %get-tuple-element.191.re, ...), custom_call_target="tpu_custom_call" | custom-call | flops 1153000 | tf_op jit(solution)/shard_map/cross_backward/pallas_call | solution.py:246
  100.6 13.2 %cross_weights.1 = (bf16[48,128,128]{2,1,0:T(8,128)(2,1)}, bf16[120,96,128]{2,1,0:T(8,128)(2,1)}, bf16[120,96,128]{2,1,0:T(8,128)(2,1)}, bf16[512,3072]{1,0:T(8,...) custom-call(s32[403]{0:T(512)S(1)} %pad_add_fusion.refs_0_, ...), custom_call_target="tpu_custom_call" | custom-call | flops 1153000 | tf_op jit(solution)/shard_map/cross_weights/pallas_call | solution.py:246
  120.3 4.5 %feed_out.1 = (bf16[512,768]{1,0:T(8,128)(2,1)}, bf16[768,768]{1,0:T(8,128)(2,1)S(1)}, bf16[512,2304]{1,0:T(8,128)(2,1)S(1)}, bf16[4,6,128,256]{3,2,1,0:T(8,128)(2,1)S(1)}, f32[8,128]{1,0:T(8,128)}) custom-call(bf16[512,3072]{1,0:T(8,128)(2,1)S(1)} %get-tuple-element.227.refs_0_, bf16[3072,768]{1,0:T(8,128)(2,1)S(1)} %get-tuple-element.228.refs_1_, ...), custom_call_target="tpu_custom_call" | custom-call | flops 1153000 | tf_op jit(solution)/shard_map/feed_out/pallas_call | solution.py:246
  124.8 7.5 %self_backward.1 = (bf16[512,2304]{1,0:T(8,128)(2,1)S(1)}, f32[16,128]{1,0:T(8,128)S(1)}, bf16[768,2304]{1,0:T(8,128)(2,1)S(1)}, bf16[512,768]{1,0:T(8,128)(2,1)...) custom-call(f32[512,768]{1,0:T(8,128)S(1)} %get-tuple-element.211.refs_2_.refs_0_.refs_1_, ...), custom_call_target="tpu_custom_call" | custom-call | flops 1153000 | tf_op jit(solution)/shard_map/self_backward/pallas_call | solution.py:246
  138.6 8.2 %self_weights.1 = (f32[512,768]{1,0:T(8,128)}, bf16[73,96,128]{2,1,0:T(8,128)(2,1)}, bf16[73,96,128]{2,1,0:T(8,128)(2,1)}, f32[8,128]{1,0:T(8,128)}) custom-call(s32[403]{0:T(512)S(1)} %pad_add_fusion.refs_0_, f32[512,768]{1,0:T(8,128)S(1)} %get-tuple-element.211.refs_2_.refs_0_.refs_1_, bf16[768,2304]{1,0:T(8,128)(2,1)S(1)} %get-tuple-element.243.refs_2_, ...), custom_call_target="tpu_custom_call" | custom-call | flops 1153000 | tf_op jit(solution)/shard_map/self_weights/pallas_call | solution.py:246
  146.9 4.3 %collective-permute-start.25 = (bf16[7008,128]{1,0:T(8,128)(2,1)}, bf16[7008,128]{1,0:T(8,128)(2,1)S(1)}, u32[]{:S(2)}, u32[]{:S(2)}) collective-permute-start(bf16[7008,128]{1,0:T(8,128)(2,1)} %bitcast.469), channel_id=1, source_target_pairs={{0,8},{8,0},{16,24},{24,16},{1,9},{9,1},{17,25},{25,17},{2,10},{10... | collective-permute-start | bytes 5382152 | tf_op jit(solution)/shard_map/ppermute | solution.py:1084
  151.1 2.8 %collective-permute-done.21.refs_13_.refs_19_ = bf16[1344,128]{1,0:T(8,128)(2,1)S(1)} collective-permute-done((bf16[1344,128]{1,0:T(8,128)(2,1)S(1)}, bf16[1344,128]{1,0:T(8,128)(2,1)S(1)}, u32[]{:S(2)}, u32[]{:S(2)}) %collective-permute-start.21) | collective-permute-done | bytes 344096 | tf_op jit(solution)/shard_map/ppermute | solution.py:1084
  162.5 3.9 %collective-permute-done.24.refs_14_.refs_18_ = bf16[768,128]{1,0:T(8,128)(2,1)S(1)} collective-permute-done((bf16[768,128]{1,0:T(8,128)(2,1)S(1)}, bf16[768,128]{1,0:T(8,128)(2,1)S(1)}, u32[]{:S(2)}, u32[]{:S(2)}) %collective-permute-start.24) | collective-permute-done | bytes 196640 | tf_op jit(solution)/shard_map/ppermute | solution.py:1084
  166.4 4.0 %collective-permute-done.22.refs_3_.refs_8_ = bf16[1344,128]{1,0:T(8,128)(2,1)S(1)} collective-permute-done((bf16[1344,128]{1,0:T(8,128)(2,1)S(1)}, bf16[1344,128]{1,0:T(8,128)(2,1)S(1)}, u32[]{:S(2)}, u32[]{:S(2)}) %collective-permute-start.22) | collective-permute-done | bytes 344096 | tf_op jit(solution)/shard_map/ppermute | solution.py:1084
  177.1 4.7 %collective-permute-done.26.refs_4_.refs_14_ = bf16[768,128]{1,0:T(8,128)(2,1)S(1)} collective-permute-done((bf16[768,128]{1,0:T(8,128)(2,1)S(1)}, bf16[768,128]{1,0:T(8,128)(2,1)S(1)}, u32[]{:S(2)}, u32[]{:S(2)}) %collective-permute-start.26) | collective-permute-done | bytes 196640 | tf_op jit(solution)/shard_map/ppermute | solution.py:1084
  195.4 5.6 %collective-permute-done.31.refs_15_.refs_4_.refs_12_ = bf16[768,128]{1,0:T(8,128)(2,1)S(1)} collective-permute-done((bf16[768,128]{1,0:T(8,128)(2,1)S(1)}, bf16[768,128]{1,0:T(8,128)(2,1)S(1)}, u32[]{:S(2)}, u32[]{:S(2)}) %collective-permute-start.31) | collective-permute-done | bytes 196640 | tf_op jit(solution)/shard_map/ppermute | solution.py:1084
  202.5 4.4 %collective-permute-done.36.refs_10_ = bf16[288,128]{1,0:T(8,128)(2,1)S(1)} collective-permute-done((bf16[288,128]{1,0:T(8,128)(2,1)S(1)}, bf16[288,128]{1,0:T(8,128)(2,1)S(1)}, u32[]{:S(2)}, u32[]{:S(2)}) %collective-permute-start.36) | collective-permute-done | bytes 73760 | tf_op jit(solution)/shard_map/ppermute | solution.py:1084
  210.4 2.4 %collective-permute-start.40 = (bf16[1440,128]{1,0:T(8,128)(2,1)S(1)}, bf16[1440,128]{1,0:T(8,128)(2,1)S(1)}, u32[]{:S(2)}, u32[]{:S(2)}) collective-permute-start(bf16[1440,128]{1,0:T(8,128)(2,1)S(1)} %get-tuple-element.297.refs_1_), channel_id=1, source_target_pairs={{0,8},{8,0},{16,24},{24,16},{1,9},{9,1},{17,25},{25,17},{2,10},{10... | collective-permute-start | bytes 1105928 | tf_op jit(solution)/shard_map/ppermute | solution.py:1084
  214.5 3.4 %collective-permute-start.39 = (bf16[960,128]{1,0:T(8,128)(2,1)S(1)}, bf16[960,128]{1,0:T(8,128)(2,1)S(1)}, u32[]{:S(2)}, u32[]{:S(2)}) collective-permute-start(bf16[960,128]{1,0:T(8,128)(2,1)S(1)} %get-tuple-element.296.refs_1_), channel_id=1, source_target_pairs={{0,8},{8,0},{16,24},{24,16},{1,9},{9,1},{17,25},{25,17},{2,10},{10... | collective-permute-start | bytes 737288 | tf_op jit(solution)/shard_map/ppermute | solution.py:1084
  (139 shorter events, 72.7 us)
Async XLA Ops:
  2.3 17.0 %collective-permute-start = (bf16[1,144,768]{2,1,0:T(8,128)(2,1)S(1)}, bf16[1,144,768]{2,1,0:T(8,128)(2,1)}, u32[]{:S(2)}, u32[]{:S(2)}) collective-permute-start(bf16[1,144,768]{2,1,0:T(8,128)(2,1)S(1)} %fusion.2.refs_0_), channel_id=1, source_target_pairs={{0,4},{1,5},{2,6},{3,7},{4,0},{5,1},{6,2},{7,3},{8,12},{9,13},{10,... | collective-permute-start | bytes 663560 | tf_op jit(solution)/shard_map/ppermute | solution.py:1084
  5.5 19.3 %collective-permute-start.2 = (bf16[1,144,768]{2,1,0:T(8,128)(2,1)S(1)}, bf16[1,144,768]{2,1,0:T(8,128)(2,1)}, u32[]{:S(2)}, u32[]{:S(2)}) collective-permute-start(bf16[1,144,768]{2,1,0:T(8,128)(2,1)S(1)} %fusion.2.refs_0_), channel_id=1, source_target_pairs={{0,2},{1,3},{2,0},{3,1},{4,6},{5,7},{6,4},{7,5},{8,10},{9,11},{10,... | collective-permute-start | bytes 663560 | tf_op jit(solution)/shard_map/ppermute | solution.py:1084
  6.8 24.8 %collective-permute-start.1 = (bf16[1,144,768]{2,1,0:T(8,128)(2,1)S(1)}, bf16[1,144,768]{2,1,0:T(8,128)(2,1)}, u32[]{:S(2)}, u32[]{:S(2)}) collective-permute-start(bf16[1,144,768]{2,1,0:T(8,128)(2,1)S(1)} %fusion.2.refs_0_), channel_id=1, source_target_pairs={{0,1},{1,0},{2,3},{3,2},{4,5},{5,4},{6,7},{7,6},{8,9},{9,8},{10,11... | collective-permute-start | bytes 663560 | tf_op jit(solution)/shard_map/ppermute | solution.py:1084
  69.1 28.2 %collective-permute-start.10 = (bf16[4608,128]{1,0:T(8,128)(2,1)S(1)}, bf16[4608,128]{1,0:T(8,128)(2,1)S(1)}, u32[]{:S(2)}, u32[]{:S(2)}) collective-permute-start(bf16[4608,128]{1,0:T(8,128)(2,1)S(1)} %get-tuple-element.223), channel_id=1, source_target_pairs={{0,16},{8,24},{16,0},{24,8},{1,17},{9,25},{17,1},{25,9},{2,18},{10... | collective-permute-start | bytes 3538952 | tf_op jit(solution)/shard_map/ppermute | solution.py:1084
  76.4 20.9 %collective-permute-start.11 = (bf16[3072,128]{1,0:T(8,128)(2,1)S(1)}, bf16[3072,128]{1,0:T(8,128)(2,1)S(1)}, u32[]{:S(2)}, u32[]{:S(2)}) collective-permute-start(bf16[3072,128]{1,0:T(8,128)(2,1)S(1)} %get-tuple-element.224), channel_id=1, source_target_pairs={{0,1},{1,0},{2,3},{3,2},{4,5},{5,4},{6,7},{7,6},{8,9},{9,8},{10,11... | collective-permute-start | bytes 2359304 | tf_op jit(solution)/shard_map/ppermute | solution.py:1084
  76.7 20.6 %collective-permute-start.9 = (bf16[1536,128]{1,0:T(8,128)(2,1)S(1)}, bf16[1536,128]{1,0:T(8,128)(2,1)S(1)}, u32[]{:S(2)}, u32[]{:S(2)}) collective-permute-start(bf16[1536,128]{1,0:T(8,128)(2,1)S(1)} %get-tuple-element.222), channel_id=1, source_target_pairs={{0,2},{1,3},{2,0},{3,1},{4,6},{5,7},{6,4},{7,5},{8,10},{9,11},{10,... | collective-permute-start | bytes 1179656 | tf_op jit(solution)/shard_map/ppermute | solution.py:1084
  99.0 17.8 %collective-permute-start.12 = (bf16[3072,128]{1,0:T(8,128)(2,1)S(1)}, bf16[3072,128]{1,0:T(8,128)(2,1)S(1)}, u32[]{:S(2)}, u32[]{:S(2)}) collective-permute-start(bf16[3072,128]{1,0:T(8,128)(2,1)S(1)} %get-tuple-element.233), channel_id=1, source_target_pairs={{0,1},{1,0},{2,3},{3,2},{4,5},{5,4},{6,7},{7,6},{8,9},{9,8},{10,11... | collective-permute-start | bytes 2359304 | tf_op jit(solution)/shard_map/ppermute | solution.py:1084
  100.3 15.4 %collective-permute-start.13 = (bf16[1536,128]{1,0:T(8,128)(2,1)S(1)}, bf16[1536,128]{1,0:T(8,128)(2,1)S(1)}, u32[]{:S(2)}, u32[]{:S(2)}) collective-permute-start(bf16[1536,128]{1,0:T(8,128)(2,1)S(1)} %get-tuple-element.234), channel_id=1, source_target_pairs={{0,2},{1,3},{2,0},{3,1},{4,6},{5,7},{6,4},{7,5},{8,10},{9,11},{10,... | collective-permute-start | bytes 1179656 | tf_op jit(solution)/shard_map/ppermute | solution.py:1084
  113.8 19.2 %collective-permute-start.14 = (bf16[11520,128]{1,0:T(8,128)(2,1)}, bf16[11520,128]{1,0:T(8,128)(2,1)S(1)}, u32[]{:S(2)}, u32[]{:S(2)}) collective-permute-start(bf16[11520,128]{1,0:T(8,128)(2,1)} %bitcast.466), channel_id=1, source_target_pairs={{0,8},{8,0},{16,24},{24,16},{1,9},{9,1},{17,25},{25,17},{2,10},{10... | collective-permute-start | bytes 8847368 | tf_op jit(solution)/shard_map/ppermute | solution.py:1084
  118.7 14.3 %collective-permute-start.15 = (bf16[2176,128]{1,0:T(8,128)(2,1)S(1)}, bf16[2176,128]{1,0:T(8,128)(2,1)S(1)}, u32[]{:S(2)}, u32[]{:S(2)}) collective-permute-start(bf16[2176,128]{1,0:T(8,128)(2,1)S(1)} %get-tuple-element.252), channel_id=1, source_target_pairs={{0,2},{1,3},{2,0},{3,1},{4,6},{5,7},{6,4},{7,5},{8,10},{9,11},{10,... | collective-permute-start | bytes 1671176 | tf_op jit(solution)/shard_map/ppermute | solution.py:1084
  119.0 13.3 %collective-permute-start.16 = (bf16[2048,128]{1,0:T(8,128)(2,1)S(1)}, bf16[2048,128]{1,0:T(8,128)(2,1)S(1)}, u32[]{:S(2)}, u32[]{:S(2)}) collective-permute-start(bf16[2048,128]{1,0:T(8,128)(2,1)S(1)} %get-tuple-element.253), channel_id=1, source_target_pairs={{0,1},{1,0},{2,3},{3,2},{4,5},{5,4},{6,7},{7,6},{8,9},{9,8},{10,11... | collective-permute-start | bytes 1572872 | tf_op jit(solution)/shard_map/ppermute | solution.py:1084
  120.3 12.0 %collective-permute-start.17 = (bf16[384,128]{1,0:T(8,128)(2,1)S(1)}, bf16[384,128]{1,0:T(8,128)(2,1)S(1)}, u32[]{:S(2)}, u32[]{:S(2)}) collective-permute-start(bf16[384,128]{1,0:T(8,128)(2,1)S(1)} %get-tuple-element.255), channel_id=1, source_target_pairs={{0,4},{1,5},{2,6},{3,7},{4,0},{5,1},{6,2},{7,3},{8,12},{9,13},{10,... | collective-permute-start | bytes 294920 | tf_op jit(solution)/shard_map/ppermute | solution.py:1084
  135.2 18.8 %collective-permute-start.18 = (bf16[3200,128]{1,0:T(8,128)(2,1)S(1)}, bf16[3200,128]{1,0:T(8,128)(2,1)S(1)}, u32[]{:S(2)}, u32[]{:S(2)}) collective-permute-start(bf16[3200,128]{1,0:T(8,128)(2,1)S(1)} %get-tuple-element.259), channel_id=1, source_target_pairs={{0,1},{1,0},{2,3},{3,2},{4,5},{5,4},{6,7},{7,6},{8,9},{9,8},{10,11... | collective-permute-start | bytes 2457608 | tf_op jit(solution)/shard_map/ppermute | solution.py:1084
  137.3 16.7 %collective-permute-start.19 = (bf16[3072,128]{1,0:T(8,128)(2,1)S(1)}, bf16[3072,128]{1,0:T(8,128)(2,1)S(1)}, u32[]{:S(2)}, u32[]{:S(2)}) collective-permute-start(bf16[3072,128]{1,0:T(8,128)(2,1)S(1)} %get-tuple-element.260), channel_id=1, source_target_pairs={{0,16},{8,24},{16,0},{24,8},{1,17},{9,25},{17,1},{25,9},{2,18},{10... | collective-permute-start | bytes 2359304 | tf_op jit(solution)/shard_map/ppermute | solution.py:1084
  137.3 16.7 %collective-permute-start.21 = (bf16[1344,128]{1,0:T(8,128)(2,1)S(1)}, bf16[1344,128]{1,0:T(8,128)(2,1)S(1)}, u32[]{:S(2)}, u32[]{:S(2)}) collective-permute-start(bf16[1344,128]{1,0:T(8,128)(2,1)S(1)} %get-tuple-element.262), channel_id=1, source_target_pairs={{0,4},{1,5},{2,6},{3,7},{4,0},{5,1},{6,2},{7,3},{8,12},{9,13},{10,... | collective-permute-start | bytes 1032200 | tf_op jit(solution)/shard_map/ppermute | solution.py:1084
  138.2 12.9 %collective-permute-start.20 = (bf16[1024,128]{1,0:T(8,128)(2,1)S(1)}, bf16[1024,128]{1,0:T(8,128)(2,1)S(1)}, u32[]{:S(2)}, u32[]{:S(2)}) collective-permute-start(bf16[1024,128]{1,0:T(8,128)(2,1)S(1)} %get-tuple-element.261), channel_id=1, source_target_pairs={{0,2},{1,3},{2,0},{3,1},{4,6},{5,7},{6,4},{7,5},{8,10},{9,11},{10,... | collective-permute-start | bytes 786440 | tf_op jit(solution)/shard_map/ppermute | solution.py:1084
  146.9 12.6 %collective-permute-start.25 = (bf16[7008,128]{1,0:T(8,128)(2,1)}, bf16[7008,128]{1,0:T(8,128)(2,1)S(1)}, u32[]{:S(2)}, u32[]{:S(2)}) collective-permute-start(bf16[7008,128]{1,0:T(8,128)(2,1)} %bitcast.469), channel_id=1, source_target_pairs={{0,8},{8,0},{16,24},{24,16},{1,9},{9,1},{17,25},{25,17},{2,10},{10... | collective-permute-start | bytes 5382152 | tf_op jit(solution)/shard_map/ppermute | solution.py:1084
  155.7 14.7 %collective-permute-start.23 = (bf16[1536,128]{1,0:T(8,128)(2,1)S(1)}, bf16[1536,128]{1,0:T(8,128)(2,1)S(1)}, u32[]{:S(2)}, u32[]{:S(2)}) collective-permute-start(bf16[1536,128]{1,0:T(8,128)(2,1)S(1)} %get-tuple-element.265), channel_id=1, source_target_pairs={{0,1},{1,0},{2,3},{3,2},{4,5},{5,4},{6,7},{7,6},{8,9},{9,8},{10,11... | collective-permute-start | bytes 1179656 | tf_op jit(solution)/shard_map/ppermute | solution.py:1084
  157.3 13.1 %collective-permute-start.22 = (bf16[1344,128]{1,0:T(8,128)(2,1)S(1)}, bf16[1344,128]{1,0:T(8,128)(2,1)S(1)}, u32[]{:S(2)}, u32[]{:S(2)}) collective-permute-start(bf16[1344,128]{1,0:T(8,128)(2,1)S(1)} %get-tuple-element.264), channel_id=1, source_target_pairs={{0,2},{1,3},{2,0},{3,1},{4,6},{5,7},{6,4},{7,5},{8,10},{9,11},{10,... | collective-permute-start | bytes 1032200 | tf_op jit(solution)/shard_map/ppermute | solution.py:1084
  160.9 14.5 %collective-permute-start.28 = (bf16[2304,128]{1,0:T(8,128)(2,1)S(1)}, bf16[2304,128]{1,0:T(8,128)(2,1)S(1)}, u32[]{:S(2)}, u32[]{:S(2)}) collective-permute-start(bf16[2304,128]{1,0:T(8,128)(2,1)S(1)} %get-tuple-element.276), channel_id=1, source_target_pairs={{0,16},{8,24},{16,0},{24,8},{1,17},{9,25},{17,1},{25,9},{2,18},{10... | collective-permute-start | bytes 1769480 | tf_op jit(solution)/shard_map/ppermute | solution.py:1084
  162.2 13.2 %collective-permute-start.27 = (bf16[1248,128]{1,0:T(8,128)(2,1)S(1)}, bf16[1248,128]{1,0:T(8,128)(2,1)S(1)}, u32[]{:S(2)}, u32[]{:S(2)}) collective-permute-start(bf16[1248,128]{1,0:T(8,128)(2,1)S(1)} %get-tuple-element.275.refs_3_), channel_id=1, source_target_pairs={{0,1},{1,0},{2,3},{3,2},{4,5},{5,4},{6,7},{7,6},{8,9},{9,8},{10,11... | collective-permute-start | bytes 958472 | tf_op jit(solution)/shard_map/ppermute | solution.py:1084
  171.9 12.3 %collective-permute-start.30 = (bf16[1728,128]{1,0:T(8,128)(2,1)S(1)}, bf16[1728,128]{1,0:T(8,128)(2,1)S(1)}, u32[]{:S(2)}, u32[]{:S(2)}) collective-permute-start(bf16[1728,128]{1,0:T(8,128)(2,1)S(1)} %get-tuple-element.279.refs_11_.refs_13_.refs_15_), channel_id=1, source_target_pairs={{0,16},{8,24},{16,0},{24,8},{1,17},{9,25},{17,1},{25,9},{2,18},{10... | collective-permute-start | bytes 1327112 | tf_op jit(solution)/shard_map/ppermute | solution.py:1084
  173.3 22.1 %collective-permute-start.34 = (bf16[672,128]{1,0:T(8,128)(2,1)S(1)}, bf16[672,128]{1,0:T(8,128)(2,1)S(1)}, u32[]{:S(2)}, u32[]{:S(2)}) collective-permute-start(bf16[672,128]{1,0:T(8,128)(2,1)S(1)} %get-tuple-element.287), channel_id=1, source_target_pairs={{0,4},{1,5},{2,6},{3,7},{4,0},{5,1},{6,2},{7,3},{8,12},{9,13},{10,... | collective-permute-start | bytes 516104 | tf_op jit(solution)/shard_map/ppermute | solution.py:1084
  176.7 14.0 %collective-permute-start.32 = (bf16[1152,128]{1,0:T(8,128)(2,1)S(1)}, bf16[1152,128]{1,0:T(8,128)(2,1)S(1)}, u32[]{:S(2)}, u32[]{:S(2)}) collective-permute-start(bf16[1152,128]{1,0:T(8,128)(2,1)S(1)} %get-tuple-element.284), channel_id=1, source_target_pairs={{0,1},{1,0},{2,3},{3,2},{4,5},{5,4},{6,7},{7,6},{8,9},{9,8},{10,11... | collective-permute-start | bytes 884744 | tf_op jit(solution)/shard_map/ppermute | solution.py:1084
  (25 other events, 155.6 us)

commit v3 on v2

--- a/solution.py
+++ b/solution.py
@@ -477,11 +477,11 @@
         enc_out.flush()
 
         def project(t, carry):
-            at = pl.ds(pl.multiple_of(t * 384, 128), 384)
+            at = pl.ds(pl.multiple_of(t * width, 128), width)
             kv_ref[:, at] = dot_nn(enc_ref[...], wkv_ref[:, at]).astype(BF)
             return carry
 
-        lax.fori_loop(0, 2 * width // 384, project, 0)
+        lax.fori_loop(0, 2, project, 0)
         kv_out.flush()
         q0, q1 = half_masks(block_rows)
         k0, k1 = half_masks(tokens)
@@ -538,11 +538,15 @@
             inv = 1.0 / total
             inv_ref[at, pl.ds(lo, 128)] = inv
             o2_ref[at, pl.ds(lo, 128)] = (jnp.where(low, outs[0], outs[1]) * inv).astype(BF)
+            if blocks == 1:
+                inv_out.flush_part((slice(None), pl.ds(lo, 128)))
+                o2_out.flush_part((slice(None), pl.ds(lo, 128)))
             return carry
 
         lax.fori_loop(0, steps, attend, 0)
-        inv_out.flush()
-        o2_out.flush()
+        if blocks > 1:
+            inv_out.flush()
+            o2_out.flush()
         h2 = h1_ref[...] + dot_nn(o2_ref[...], wco_ref[...])
         h2_out.ref[...] = h2
         h2_out.flush()
@@ -1268,7 +1272,7 @@
         else:
             self.own, self.other = payload, got
 
-    def finish(self, place, arrays):
+    def finish(self, place, arrays, small=None):
         outs = []
         for (columns, _), spots, named in zip(self.groups, self.spots, arrays):
             for name, stack in named:
@@ -1302,11 +1306,28 @@
                         for j, at, y_of, k in far:
                             put(ref, columns, half, j, at[y_is ^ y_of] + k * columns.part)
 
-            for ref, (at, rows) in zip(refs[len(outs) :], self.small_spots):
-                ref[...] = own_ref[at : at + rows, :].astype(F32)
+            if small:
+                bias_ref, *gain_refs = refs[len(outs) :]
+                blk = place_ref[1]
+                at, rows = self.small_spots[0]
+                misc = own_ref[at : at + rows, :].astype(F32)
+                bias = jnp.concatenate([misc[:16], jnp.zeros((112, 128), F32)], 0)
+                bias = pltpu.roll(bias, lax.rem(128 - blk * bias_part, 128), 1)
+                bias_ref[...] = jnp.transpose(bias)[:bias_part, :heads]
+                gains = jnp.concatenate(
+                    [misc[16 + 8 * j : 24 + 8 * j] for j in range(width // 128)], 1
+                )
+                gains = pltpu.roll(gains, lax.rem(width - blk * part, width), 1)
+                for i, ref in enumerate(gain_refs):
+                    ref[...] = gains[i : i + 1, :part]
 
         shapes = [shape_of(F32, stack * columns.part, 2 * half) for columns, _, _, stack, half in outs]
-        shapes += [shape_of(F32, rows, 128) for _, rows in self.small_spots]
+        if small:
+            heads, buckets, chunks = small
+            bias_part = buckets // chunks
+            part = self.groups[0][0].part
+            width = part * chunks
+            shapes += [shape_of(F32, bias_part, heads)] + [shape_of(F32, 1, part)] * 3
         return call(
             "finish",
             body,
@@ -1469,33 +1490,35 @@
         place, dh1, a1, dqkv, x_near, gains, wqkv_near, gbias, gain_cross_grad, gain_ff_grad, cols_s
     )
     b_sa, b_sb, b_misc = weight_buckets(cols_s, keep, send, orders, y_bits)
-    send_round(25, b_xb, b_xa, b_ea, b_eb, settle=[b_in, b_out])
+    send_round(25, b_xa, b_ea, b_eb, settle=[b_in, b_out, b_xb])
     send_round(4, b_sb, b_sa, b_misc)
+    send_round(4, b_xb)
+    send_round(4, b_sa, b_misc, b_sb)
     rest_of(b_out, b_in, b_jn)
     total_ff = Total([(cols_out, [b_out]), (cols_in, [b_in, b_jn])], [], dp_size)
     send_round(4, b_xa, b_xb, total_ff, settle=[b_ea, b_eb])
     rest_of(b_ea, b_eb)
-    send_round(4, b_sa, b_misc, b_sb)
-    send_round(4, b_xb, b_sa, b_misc, total_ff)
+    send_round(4, b_sb, b_sa, b_misc)
+    send_round(4, b_xb, total_ff)
     grad_enc = join_encodings([b_ea, b_eb], shard_rows, width)
     send_round(4, b_sb)
     rest_of(total_ff)
     grad_ff_out, grad_ff_in = total_ff.finish(place, [[("out", stack)], [("in", 1)]])
     rest_of(b_xa, b_xb)
     total_x = Total([(cols_x, [b_xa, b_xb])], [], dp_size)
-    send_round(4, b_sb, total_x)
+    send_round(4, total_x)
     rest_of(b_sa, b_sb, b_misc)
     total_s = Total([(cols_s, [b_sa, b_sb])], [b_misc], dp_size)
-    send_round(4, total_s, total_x)
-    rest_of(total_s, total_x)
+    send_round(0.5, total_s)
+    rest_of(total_x)
+    rest_of(total_s)
     grad_cross_out, grad_cross_q, grad_self_out, grad_cross_kv = total_x.finish(
         place, [[("out", 1), ("q", 1), ("self", 1), ("kv", 1)]]
     )
-    grad_qkv, misc = total_s.finish(place, [[("qkv", 1)]])
-    gains = misc[16 : 16 + width // 16].reshape(width // 128, 8, 128)[:, :3].transpose(1, 0, 2).reshape(3, width)
-    gains = lax.dynamic_slice(gains, (0, blk * part), (3, part))
-    bias_part = bucket_count // chunks
-    grad_bias = lax.dynamic_slice(misc, (0, blk * bias_part), (heads, bias_part)).T
+    grad_qkv, grad_bias, *gains = total_s.finish(
+        place, [[("qkv", 1)]], (heads, bucket_count, chunks)
+    )
+    gains = [gain.reshape(part) for gain in gains]
     return (
         out[None],
         grad_dec[None],

time: 223 us -> 217 us (0.973)
  waiting for transfers between devices: 35.7 us -> 24.1 us
  starting transfers between devices: 46.2 us -> 54.8 us
    ppermute x41 -> x42, waiting for transfers between devices: 35.7 us -> 24.1 us  [swap(): return lax.ppermute(value, axis, [(i, i ^ bit) for i in range(size)])]
    ppermute x41 -> x42, starting transfers between devices: 46.2 us -> 54.8 us  [swap(): return lax.ppermute(value, axis, [(i, i ^ bit) for i in range(size)])]
    pallas_call x50 -> x56, Pallas kernels: 134 us -> 133 us  [call(): pl.pallas_call(ordered, out_shape=tuple(out_shape), grid_spec=pltpu.Prefe...]
  transfers between devices with their start and end apart: 41 -> 42, of which waited for: 12 -> 12; matrix products, arithmetic and copies ran while one was open for 0% -> 0% of each run, Pallas kernels for 44% -> 47%
where the time goes in v3:
time: 217 us
  Pallas kernels  133 us (61%)
  starting transfers between devices  54.8 us (25%)
  waiting for transfers between devices  24.1 us (11%)
    pallas_call x56, Pallas kernels, call(): pl.pallas_call(ordered, out_shape=tuple(out_shape), grid_spec=pltpu.Prefe...  133 us
    ppermute x42, starting transfers between devices, swap(): return lax.ppermute(value, axis, [(i, i ^ bit) for i in range(size)])  54.8 us
    ppermute x42, waiting for transfers between devices, swap(): return lax.ppermute(value, axis, [(i, i ^ bit) for i in range(size)])  24.1 us
  transfers between devices with their start and end apart: 42, of which 12 were waited for; matrix products, arithmetic and copies ran while one was open for 0% of the time, Pallas kernels for 47%

profile of v3, /device:TPU:1, one launch (start us, length us, event | category | flops | bytes accessed | tf_op | source)
XLA Modules:
  0.0 216.6 jit_solution(3125608639738761802)
XLA Ops:
  5.7 2.3 %collective-permute-start = (bf16[1,144,768]{2,1,0:T(8,128)(2,1)S(1)}, bf16[1,144,768]{2,1,0:T(8,128)(2,1)}, u32[]{:S(2)}, u32[]{:S(2)}) collective-permute-start(bf16[1,144,768]{2,1,0:T(8,128)(2,1)S(1)} %fusion.2.refs_0_), channel_id=1, source_target_pairs={{0,4},{1,5},{2,6},{3,7},{4,0},{5,1},{6,2},{7,3},{8,12},{9,13},{10,... | collective-permute-start | bytes 663560 | tf_op jit(solution)/shard_map/ppermute | solution.py:1088
  8.1 11.2 %self_attention.1 = (bf16[512,768]{1,0:T(8,128)(2,1)}, bf16[512,2304]{1,0:T(8,128)(2,1)}, bf16[4,6,128,256]{3,2,1,0:T(8,128)(2,1)}, bf16[512,768]{1,0:T(8,128)(2...) custom-call(bf16[512,768]{1,0:T(8,128)(2,1)} %bitcast.447, ...), custom_call_target="tpu_custom_call" | custom-call | flops 1153000 | tf_op jit(solution)/shard_map/self_attention/pallas_call | solution.py:246
  21.9 2.9 %self_project.1 = (f32[512,768]{1,0:T(8,128)S(1)}, bf16[512,768]{1,0:T(8,128)(2,1)S(1)}, f32[512,768]{1,0:T(8,128)}, bf16[512,768]{1,0:T(8,128)(2,1)}, bf16[512,...) custom-call(bf16[512,768]{1,0:T(8,128)(2,1)S(1)} %copy-done.2, ...), custom_call_target="tpu_custom_call" | custom-call | flops 1153000 | tf_op jit(solution)/shard_map/self_project/pallas_call | solution.py:246
  27.0 4.6 %hidden_gradient.1 = (bf16[512,3072]{1,0:T(8,128)(2,1)S(1)}, bf16[768,1536]{1,0:T(8,128)(2,1)S(1)}, bf16[768,768]{1,0:T(8,128)(2,1)S(1)}, f32[8,128]{1,0:T(8,128)}) custom-call(bf16[512,768]{1,0:T(8,128)(2,1)S(1)} %get-tuple-element.181.refs_0_.refs_2_.refs_4_, bf16[3072,768]{1,0:T(8,128)(2,1)} %refs_15_.1, bf16[768,1536]{1,0:T(8,128)(2,1)} %refs_14_.3, ...), custom_call_target="tpu_custom_call" | custom-call | flops 1153000 | tf_op jit(solution)/shard_map/hidden_gradient/pallas_call | solution.py:246
  31.7 16.0 %cross_forward.1 = (bf16[1024,768]{1,0:T(8,128)(2,1)}, bf16[1024,1536]{1,0:T(8,128)(2,1)}, bf16[12,512,1024]{2,1,0:T(8,128)(2,1)}, f32[512,768]{1,0:T(8,128)}, b...) custom-call(bf16[1,144,768]{2,1,0:T(8,128)(2,1)S(1)} %fusion.2.refs_, ...), custom_call_target="tpu_custom_call" | custom-call | flops 1153000 | tf_op jit(solution)/shard_map/cross_forward/pallas_call | solution.py:246
  47.7 10.1 %feed_hidden.1 = (bf16[512,3072]{1,0:T(8,128)(2,1)S(1)}, bf16[512,3072]{1,0:T(8,128)(2,1)}, bf16[96,96,128]{2,1,0:T(8,128)(2,1)}, bf16[96,96,128]{2,1,0:T(8,128)(2,1)}, f32[8,128]{1,0:T(8,128)}) custom-call(s32[403]{0:T(512)S(1)} %pad_add_fusion.refs_0_, bf16[512,768]{1,0:T(8,128)(2,1)S(1)} %get-tuple-element.186.refs_1_, ...), custom_call_target="tpu_custom_call" | custom-call | flops 1153000 | tf_op jit(solution)/shard_map/feed_hidden/pallas_call | solution.py:246
  57.8 2.7 %collective-permute-start.7 = (bf16[9216,128]{1,0:T(8,128)(2,1)}, bf16[9216,128]{1,0:T(8,128)(2,1)S(1)}, u32[]{:S(2)}, u32[]{:S(2)}) collective-permute-start(bf16[9216,128]{1,0:T(8,128)(2,1)} %bitcast.454), channel_id=1, source_target_pairs={{0,8},{8,0},{16,24},{24,16},{1,9},{9,1},{17,25},{25,17},{2,10},{10... | collective-permute-start | bytes 7077896 | tf_op jit(solution)/shard_map/ppermute | solution.py:1088
  60.5 5.3 %feed_weights.1 = (bf16[96,96,128]{2,1,0:T(8,128)(2,1)}, bf16[96,96,128]{2,1,0:T(8,128)(2,1)}, f32[512,768]{1,0:T(8,128)S(1)}, f32[8,128]{1,0:T(8,128)}) custom-call(s32[403]{0:T(512)S(1)} %pad_add_fusion.refs_0_, bf16[512,768]{1,0:T(8,128)(2,1)S(1)} %get-tuple-element.186.refs_1_, bf16[512,3072]{1,0:T(8,128)(2,1)S(1)} %get-tuple-element.190.refs_2_.refs_0_, ...), custom_call_target="tpu_custom_call" | custom-call | flops 1153000 | tf_op jit(solution)/shard_map/feed_weights/pallas_call | solution.py:246
  68.8 4.3 %feed_back.1 = (f32[512,768]{1,0:T(8,128)S(1)}, f32[1,768]{1,0:T(1,128)S(1)}, f32[8,128]{1,0:T(8,128)}) custom-call(bf16[512,3072]{1,0:T(8,128)(2,1)S(1)} %get-tuple-element.190.refs_2_.refs_0_, bf16[768,3072]{1,0:T(8,128)(2,1)S(1)} %get-tuple-element.188.refs_4_.refs_1_, f32[512,768]{1,0:T(8,128)S(1)} %get-tuple-element.193.refs_2_, ...), custom_call_target="tpu_custom_call" | custom-call | flops 1153000 | tf_op jit(solution)/shard_map/feed_back/pallas_call | solution.py:246
  76.2 8.8 %cross_backward.2 = (bf16[512,384]{1,0:T(8,128)(2,1)S(1)}, bf16[384,1024]{1,0:T(8,128)(2,1)S(1)}, bf16[384,1024]{1,0:T(8,128)(2,1)S(1)}, f32[8,128]{1,0:T(8,128)}) custom-call(f32[512,768]{1,0:T(8,128)S(1)} %get-tuple-element.198.refs_0_.refs_5_.refs_1_, bf16[768,768]{1,0:T(8,128)(2,1)S(1)} %get-tuple-element.184.refs_12_.refs_1_, ...), custom_call_target="tpu_custom_call" | custom-call | flops 1153000 | tf_op jit(solution)/shard_map/cross_backward/pallas_call | solution.py:246
  85.1 9.0 %cross_backward.3 = (bf16[512,384]{1,0:T(8,128)(2,1)S(1)}, bf16[384,1024]{1,0:T(8,128)(2,1)S(1)}, bf16[384,1024]{1,0:T(8,128)(2,1)S(1)}, bf16[768,768]{1,0:T(8,1...) custom-call(f32[512,768]{1,0:T(8,128)S(1)} %get-tuple-element.198.re, ...), custom_call_target="tpu_custom_call" | custom-call | flops 1153000 | tf_op jit(solution)/shard_map/cross_backward/pallas_call | solution.py:246
  98.9 13.2 %cross_weights.1 = (bf16[48,128,128]{2,1,0:T(8,128)(2,1)}, bf16[120,96,128]{2,1,0:T(8,128)(2,1)}, bf16[120,96,128]{2,1,0:T(8,128)(2,1)}, bf16[512,3072]{1,0:T(8,...) custom-call(s32[403]{0:T(512)S(1)} %pad_add_fusion.refs_0_, ...), custom_call_target="tpu_custom_call" | custom-call | flops 1153000 | tf_op jit(solution)/shard_map/cross_weights/pallas_call | solution.py:246
  119.6 4.5 %feed_out.1 = (bf16[512,768]{1,0:T(8,128)(2,1)}, bf16[768,768]{1,0:T(8,128)(2,1)S(1)}, bf16[512,2304]{1,0:T(8,128)(2,1)S(1)}, bf16[4,6,128,256]{3,2,1,0:T(8,128)(2,1)S(1)}, f32[8,128]{1,0:T(8,128)}) custom-call(bf16[512,3072]{1,0:T(8,128)(2,1)S(1)} %get-tuple-element.234.refs_0_, bf16[3072,768]{1,0:T(8,128)(2,1)S(1)} %get-tuple-element.235.refs_1_, ...), custom_call_target="tpu_custom_call" | custom-call | flops 1153000 | tf_op jit(solution)/shard_map/feed_out/pallas_call | solution.py:246
  124.1 7.5 %self_backward.1 = (bf16[512,2304]{1,0:T(8,128)(2,1)S(1)}, f32[16,128]{1,0:T(8,128)S(1)}, bf16[768,2304]{1,0:T(8,128)(2,1)S(1)}, bf16[512,768]{1,0:T(8,128)(2,1)...) custom-call(f32[512,768]{1,0:T(8,128)S(1)} %get-tuple-element.218.refs_2_.refs_0_.refs_1_, ...), custom_call_target="tpu_custom_call" | custom-call | flops 1153000 | tf_op jit(solution)/shard_map/self_backward/pallas_call | solution.py:246
  134.9 2.3 %collective-permute-start.20 = (bf16[1344,128]{1,0:T(8,128)(2,1)S(1)}, bf16[1344,128]{1,0:T(8,128)(2,1)S(1)}, u32[]{:S(2)}, u32[]{:S(2)}) collective-permute-start(bf16[1344,128]{1,0:T(8,128)(2,1)S(1)} %get-tuple-element.268), channel_id=1, source_target_pairs={{0,4},{1,5},{2,6},{3,7},{4,0},{5,1},{6,2},{7,3},{8,12},{9,13},{10,... | collective-permute-start | bytes 1032200 | tf_op jit(solution)/shard_map/ppermute | solution.py:1088
  138.3 8.2 %self_weights.1 = (f32[512,768]{1,0:T(8,128)}, bf16[73,96,128]{2,1,0:T(8,128)(2,1)}, bf16[73,96,128]{2,1,0:T(8,128)(2,1)}, f32[8,128]{1,0:T(8,128)}) custom-call(s32[403]{0:T(512)S(1)} %pad_add_fusion.refs_0_, f32[512,768]{1,0:T(8,128)S(1)} %get-tuple-element.218.refs_2_.refs_0_.refs_1_, bf16[768,2304]{1,0:T(8,128)(2,1)S(1)} %get-tuple-element.250.refs_2_, ...), custom_call_target="tpu_custom_call" | custom-call | flops 1153000 | tf_op jit(solution)/shard_map/self_weights/pallas_call | solution.py:246
  146.5 4.0 %collective-permute-start.23 = (bf16[7008,128]{1,0:T(8,128)(2,1)}, bf16[7008,128]{1,0:T(8,128)(2,1)S(1)}, u32[]{:S(2)}, u32[]{:S(2)}) collective-permute-start(bf16[7008,128]{1,0:T(8,128)(2,1)} %bitcast.455), channel_id=1, source_target_pairs={{0,8},{8,0},{16,24},{24,16},{1,9},{9,1},{17,25},{25,17},{2,10},{10... | collective-permute-start | bytes 5382152 | tf_op jit(solution)/shard_map/ppermute | solution.py:1088
  161.5 4.5 %collective-permute-done.26.refs_2_.refs_4_.refs_6_ = bf16[1248,128]{1,0:T(8,128)(2,1)S(1)} collective-permute-done((bf16[1248,128]{1,0:T(8,128)(2,1)S(1)}, bf16[1248,128]{1,0:T(8,128)(2,1)S(1)}, u32[]{:S(2)}, u32[]{:S(2)}) %collective-permute-start.26) | collective-permute-done | bytes 319520 | tf_op jit(solution)/shard_map/ppermute | solution.py:1088
  166.0 3.2 %collective-permute-done.27.refs_7_.refs_2_ = bf16[2304,128]{1,0:T(8,128)(2,1)S(1)} collective-permute-done((bf16[2304,128]{1,0:T(8,128)(2,1)S(1)}, bf16[2304,128]{1,0:T(8,128)(2,1)S(1)}, u32[]{:S(2)}, u32[]{:S(2)}) %collective-permute-start.27) | collective-permute-done | bytes 589856 | tf_op jit(solution)/shard_map/ppermute | solution.py:1088
  175.9 4.3 %collective-permute-done.30.refs_3_.refs_8_ = bf16[1152,128]{1,0:T(8,128)(2,1)S(1)} collective-permute-done((bf16[1152,128]{1,0:T(8,128)(2,1)S(1)}, bf16[1152,128]{1,0:T(8,128)(2,1)S(1)}, u32[]{:S(2)}, u32[]{:S(2)}) %collective-permute-start.30) | collective-permute-done | bytes 294944 | tf_op jit(solution)/shard_map/ppermute | solution.py:1088
  183.7 7.6 %collective-permute-start.37 = (bf16[2304,128]{1,0:T(8,128)(2,1)S(1)}, bf16[2304,128]{1,0:T(8,128)(2,1)S(1)}, u32[]{:S(2)}, u32[]{:S(2)}) collective-permute-start(bf16[2304,128]{1,0:T(8,128)(2,1)S(1)} %get-tuple-element.299.refs_1_), channel_id=1, source_target_pairs={{0,8},{8,0},{16,24},{24,16},{1,9},{9,1},{17,25},{25,17},{2,10},{10... | collective-permute-start | bytes 1769480 | tf_op jit(solution)/shard_map/ppermute | solution.py:1088
  199.7 2.3 %collective-permute-start.39 = (bf16[1056,128]{1,0:T(8,128)(2,1)S(1)}, bf16[1056,128]{1,0:T(8,128)(2,1)S(1)}, u32[]{:S(2)}, u32[]{:S(2)}) collective-permute-start(bf16[1056,128]{1,0:T(8,128)(2,1)S(1)} %get-tuple-element.304.refs_0_.refs_2_), channel_id=1, source_target_pairs={{0,16},{8,24},{16,0},{24,8},{1,17},{9,25},{17,1},{25,9},{2,18},{10... | collective-permute-start | bytes 811016 | tf_op jit(solution)/shard_map/ppermute | solution.py:1088
  205.1 3.0 %collective-permute-done.39.refs_1_.refs_3_ = bf16[1056,128]{1,0:T(8,128)(2,1)S(1)} collective-permute-done((bf16[1056,128]{1,0:T(8,128)(2,1)S(1)}, bf16[1056,128]{1,0:T(8,128)(2,1)S(1)}, u32[]{:S(2)}, u32[]{:S(2)}) %collective-permute-start.39) | collective-permute-done | bytes 270368 | tf_op jit(solution)/shard_map/ppermute | solution.py:1088
  208.2 2.3 %collective-permute-start.41 = (bf16[1440,128]{1,0:T(8,128)(2,1)S(1)}, bf16[1440,128]{1,0:T(8,128)(2,1)S(1)}, u32[]{:S(2)}, u32[]{:S(2)}) collective-permute-start(bf16[1440,128]{1,0:T(8,128)(2,1)S(1)} %get-tuple-element.308.refs_1_), channel_id=1, source_target_pairs={{0,8},{8,0},{16,24},{24,16},{1,9},{9,1},{17,25},{25,17},{2,10},{10... | collective-permute-start | bytes 1105928 | tf_op jit(solution)/shard_map/ppermute | solution.py:1088
  (141 shorter events, 71.4 us)
Async XLA Ops:
  2.3 22.5 %collective-permute-start.2 = (bf16[1,144,768]{2,1,0:T(8,128)(2,1)S(1)}, bf16[1,144,768]{2,1,0:T(8,128)(2,1)}, u32[]{:S(2)}, u32[]{:S(2)}) collective-permute-start(bf16[1,144,768]{2,1,0:T(8,128)(2,1)S(1)} %fusion.2.refs_0_), channel_id=1, source_target_pairs={{0,2},{1,3},{2,0},{3,1},{4,6},{5,7},{6,4},{7,5},{8,10},{9,11},{10,... | collective-permute-start | bytes 663560 | tf_op jit(solution)/shard_map/ppermute | solution.py:1088
  4.5 27.1 %collective-permute-start.1 = (bf16[1,144,768]{2,1,0:T(8,128)(2,1)S(1)}, bf16[1,144,768]{2,1,0:T(8,128)(2,1)}, u32[]{:S(2)}, u32[]{:S(2)}) collective-permute-start(bf16[1,144,768]{2,1,0:T(8,128)(2,1)S(1)} %fusion.2.refs_0_), channel_id=1, source_target_pairs={{0,1},{1,0},{2,3},{3,2},{4,5},{5,4},{6,7},{7,6},{8,9},{9,8},{10,11... | collective-permute-start | bytes 663560 | tf_op jit(solution)/shard_map/ppermute | solution.py:1088
  5.7 13.6 %collective-permute-start = (bf16[1,144,768]{2,1,0:T(8,128)(2,1)S(1)}, bf16[1,144,768]{2,1,0:T(8,128)(2,1)}, u32[]{:S(2)}, u32[]{:S(2)}) collective-permute-start(bf16[1,144,768]{2,1,0:T(8,128)(2,1)S(1)} %fusion.2.refs_0_), channel_id=1, source_target_pairs={{0,4},{1,5},{2,6},{3,7},{4,0},{5,1},{6,2},{7,3},{8,12},{9,13},{10,... | collective-permute-start | bytes 663560 | tf_op jit(solution)/shard_map/ppermute | solution.py:1088
  67.5 28.1 %collective-permute-start.10 = (bf16[4608,128]{1,0:T(8,128)(2,1)S(1)}, bf16[4608,128]{1,0:T(8,128)(2,1)S(1)}, u32[]{:S(2)}, u32[]{:S(2)}) collective-permute-start(bf16[4608,128]{1,0:T(8,128)(2,1)S(1)} %get-tuple-element.230), channel_id=1, source_target_pairs={{0,16},{8,24},{16,0},{24,8},{1,17},{9,25},{17,1},{25,9},{2,18},{10... | collective-permute-start | bytes 3538952 | tf_op jit(solution)/shard_map/ppermute | solution.py:1088
  74.7 20.9 %collective-permute-start.9 = (bf16[1536,128]{1,0:T(8,128)(2,1)S(1)}, bf16[1536,128]{1,0:T(8,128)(2,1)S(1)}, u32[]{:S(2)}, u32[]{:S(2)}) collective-permute-start(bf16[1536,128]{1,0:T(8,128)(2,1)S(1)} %get-tuple-element.229), channel_id=1, source_target_pairs={{0,2},{1,3},{2,0},{3,1},{4,6},{5,7},{6,4},{7,5},{8,10},{9,11},{10,... | collective-permute-start | bytes 1179656 | tf_op jit(solution)/shard_map/ppermute | solution.py:1088
  76.0 19.6 %collective-permute-start.11 = (bf16[3072,128]{1,0:T(8,128)(2,1)S(1)}, bf16[3072,128]{1,0:T(8,128)(2,1)S(1)}, u32[]{:S(2)}, u32[]{:S(2)}) collective-permute-start(bf16[3072,128]{1,0:T(8,128)(2,1)S(1)} %get-tuple-element.231), channel_id=1, source_target_pairs={{0,1},{1,0},{2,3},{3,2},{4,5},{5,4},{6,7},{7,6},{8,9},{9,8},{10,11... | collective-permute-start | bytes 2359304 | tf_op jit(solution)/shard_map/ppermute | solution.py:1088
  97.3 16.7 %collective-permute-start.13 = (bf16[1536,128]{1,0:T(8,128)(2,1)S(1)}, bf16[1536,128]{1,0:T(8,128)(2,1)S(1)}, u32[]{:S(2)}, u32[]{:S(2)}) collective-permute-start(bf16[1536,128]{1,0:T(8,128)(2,1)S(1)} %get-tuple-element.241), channel_id=1, source_target_pairs={{0,2},{1,3},{2,0},{3,1},{4,6},{5,7},{6,4},{7,5},{8,10},{9,11},{10,... | collective-permute-start | bytes 1179656 | tf_op jit(solution)/shard_map/ppermute | solution.py:1088
  97.7 17.4 %collective-permute-start.12 = (bf16[3072,128]{1,0:T(8,128)(2,1)S(1)}, bf16[3072,128]{1,0:T(8,128)(2,1)S(1)}, u32[]{:S(2)}, u32[]{:S(2)}) collective-permute-start(bf16[3072,128]{1,0:T(8,128)(2,1)S(1)} %get-tuple-element.240), channel_id=1, source_target_pairs={{0,1},{1,0},{2,3},{3,2},{4,5},{5,4},{6,7},{7,6},{8,9},{9,8},{10,11... | collective-permute-start | bytes 2359304 | tf_op jit(solution)/shard_map/ppermute | solution.py:1088
  112.1 20.3 %collective-permute-start.14 = (bf16[11520,128]{1,0:T(8,128)(2,1)}, bf16[11520,128]{1,0:T(8,128)(2,1)S(1)}, u32[]{:S(2)}, u32[]{:S(2)}) collective-permute-start(bf16[11520,128]{1,0:T(8,128)(2,1)} %bitcast.452), channel_id=1, source_target_pairs={{0,8},{8,0},{16,24},{24,16},{1,9},{9,1},{17,25},{25,17},{2,10},{10... | collective-permute-start | bytes 8847368 | tf_op jit(solution)/shard_map/ppermute | solution.py:1088
  117.1 14.5 %collective-permute-start.17 = (bf16[384,128]{1,0:T(8,128)(2,1)S(1)}, bf16[384,128]{1,0:T(8,128)(2,1)S(1)}, u32[]{:S(2)}, u32[]{:S(2)}) collective-permute-start(bf16[384,128]{1,0:T(8,128)(2,1)S(1)} %get-tuple-element.262), channel_id=1, source_target_pairs={{0,4},{1,5},{2,6},{3,7},{4,0},{5,1},{6,2},{7,3},{8,12},{9,13},{10,... | collective-permute-start | bytes 294920 | tf_op jit(solution)/shard_map/ppermute | solution.py:1088
  117.8 13.8 %collective-permute-start.16 = (bf16[2048,128]{1,0:T(8,128)(2,1)S(1)}, bf16[2048,128]{1,0:T(8,128)(2,1)S(1)}, u32[]{:S(2)}, u32[]{:S(2)}) collective-permute-start(bf16[2048,128]{1,0:T(8,128)(2,1)S(1)} %get-tuple-element.260), channel_id=1, source_target_pairs={{0,1},{1,0},{2,3},{3,2},{4,5},{5,4},{6,7},{7,6},{8,9},{9,8},{10,11... | collective-permute-start | bytes 1572872 | tf_op jit(solution)/shard_map/ppermute | solution.py:1088
  119.0 13.4 %collective-permute-start.15 = (bf16[2176,128]{1,0:T(8,128)(2,1)S(1)}, bf16[2176,128]{1,0:T(8,128)(2,1)S(1)}, u32[]{:S(2)}, u32[]{:S(2)}) collective-permute-start(bf16[2176,128]{1,0:T(8,128)(2,1)S(1)} %get-tuple-element.259), channel_id=1, source_target_pairs={{0,2},{1,3},{2,0},{3,1},{4,6},{5,7},{6,4},{7,5},{8,10},{9,11},{10,... | collective-permute-start | bytes 1671176 | tf_op jit(solution)/shard_map/ppermute | solution.py:1088
  134.5 16.1 %collective-permute-start.19 = (bf16[1024,128]{1,0:T(8,128)(2,1)S(1)}, bf16[1024,128]{1,0:T(8,128)(2,1)S(1)}, u32[]{:S(2)}, u32[]{:S(2)}) collective-permute-start(bf16[1024,128]{1,0:T(8,128)(2,1)S(1)} %get-tuple-element.267), channel_id=1, source_target_pairs={{0,2},{1,3},{2,0},{3,1},{4,6},{5,7},{6,4},{7,5},{8,10},{9,11},{10,... | collective-permute-start | bytes 786440 | tf_op jit(solution)/shard_map/ppermute | solution.py:1088
  134.9 15.6 %collective-permute-start.20 = (bf16[1344,128]{1,0:T(8,128)(2,1)S(1)}, bf16[1344,128]{1,0:T(8,128)(2,1)S(1)}, u32[]{:S(2)}, u32[]{:S(2)}) collective-permute-start(bf16[1344,128]{1,0:T(8,128)(2,1)S(1)} %get-tuple-element.268), channel_id=1, source_target_pairs={{0,4},{1,5},{2,6},{3,7},{4,0},{5,1},{6,2},{7,3},{8,12},{9,13},{10,... | collective-permute-start | bytes 1032200 | tf_op jit(solution)/shard_map/ppermute | solution.py:1088
  137.2 15.5 %collective-permute-start.21 = (bf16[3072,128]{1,0:T(8,128)(2,1)S(1)}, bf16[3072,128]{1,0:T(8,128)(2,1)S(1)}, u32[]{:S(2)}, u32[]{:S(2)}) collective-permute-start(bf16[3072,128]{1,0:T(8,128)(2,1)S(1)} %get-tuple-element.269), channel_id=1, source_target_pairs={{0,16},{8,24},{16,0},{24,8},{1,17},{9,25},{17,1},{25,9},{2,18},{10... | collective-permute-start | bytes 2359304 | tf_op jit(solution)/shard_map/ppermute | solution.py:1088
  137.6 16.0 %collective-permute-start.18 = (bf16[3200,128]{1,0:T(8,128)(2,1)S(1)}, bf16[3200,128]{1,0:T(8,128)(2,1)S(1)}, u32[]{:S(2)}, u32[]{:S(2)}) collective-permute-start(bf16[3200,128]{1,0:T(8,128)(2,1)S(1)} %get-tuple-element.266), channel_id=1, source_target_pairs={{0,1},{1,0},{2,3},{3,2},{4,5},{5,4},{6,7},{7,6},{8,9},{9,8},{10,11... | collective-permute-start | bytes 2457608 | tf_op jit(solution)/shard_map/ppermute | solution.py:1088
  146.5 11.4 %collective-permute-start.23 = (bf16[7008,128]{1,0:T(8,128)(2,1)}, bf16[7008,128]{1,0:T(8,128)(2,1)S(1)}, u32[]{:S(2)}, u32[]{:S(2)}) collective-permute-start(bf16[7008,128]{1,0:T(8,128)(2,1)} %bitcast.455), channel_id=1, source_target_pairs={{0,8},{8,0},{16,24},{24,16},{1,9},{9,1},{17,25},{25,17},{2,10},{10... | collective-permute-start | bytes 5382152 | tf_op jit(solution)/shard_map/ppermute | solution.py:1088
  155.7 15.9 %collective-permute-start.25 = (bf16[768,128]{1,0:T(8,128)(2,1)S(1)}, bf16[768,128]{1,0:T(8,128)(2,1)S(1)}, u32[]{:S(2)}, u32[]{:S(2)}) collective-permute-start(bf16[768,128]{1,0:T(8,128)(2,1)S(1)} %get-tuple-element.279), channel_id=1, source_target_pairs={{0,4},{1,5},{2,6},{3,7},{4,0},{5,1},{6,2},{7,3},{8,12},{9,13},{10,... | collective-permute-start | bytes 589832 | tf_op jit(solution)/shard_map/ppermute | solution.py:1088
  156.9 14.8 %collective-permute-start.22 = (bf16[1344,128]{1,0:T(8,128)(2,1)S(1)}, bf16[1344,128]{1,0:T(8,128)(2,1)S(1)}, u32[]{:S(2)}, u32[]{:S(2)}) collective-permute-start(bf16[1344,128]{1,0:T(8,128)(2,1)S(1)} %get-tuple-element.271), channel_id=1, source_target_pairs={{0,2},{1,3},{2,0},{3,1},{4,6},{5,7},{6,4},{7,5},{8,10},{9,11},{10,... | collective-permute-start | bytes 1032200 | tf_op jit(solution)/shard_map/ppermute | solution.py:1088
  161.4 10.8 %collective-permute-start.24 = (bf16[1536,128]{1,0:T(8,128)(2,1)S(1)}, bf16[1536,128]{1,0:T(8,128)(2,1)S(1)}, u32[]{:S(2)}, u32[]{:S(2)}) collective-permute-start(bf16[1536,128]{1,0:T(8,128)(2,1)S(1)} %get-tuple-element.277), channel_id=1, source_target_pairs={{0,1},{1,0},{2,3},{3,2},{4,5},{5,4},{6,7},{7,6},{8,9},{9,8},{10,11... | collective-permute-start | bytes 1179656 | tf_op jit(solution)/shard_map/ppermute | solution.py:1088
  174.6 23.0 %collective-permute-start.35 = (bf16[672,128]{1,0:T(8,128)(2,1)S(1)}, bf16[672,128]{1,0:T(8,128)(2,1)S(1)}, u32[]{:S(2)}, u32[]{:S(2)}) collective-permute-start(bf16[672,128]{1,0:T(8,128)(2,1)S(1)} %get-tuple-element.297), channel_id=1, source_target_pairs={{0,4},{1,5},{2,6},{3,7},{4,0},{5,1},{6,2},{7,3},{8,12},{9,13},{10,... | collective-permute-start | bytes 516104 | tf_op jit(solution)/shard_map/ppermute | solution.py:1088
  181.3 20.7 %collective-permute-start.32 = (bf16[384,128]{1,0:T(8,128)(2,1)S(1)}, bf16[384,128]{1,0:T(8,128)(2,1)S(1)}, u32[]{:S(2)}, u32[]{:S(2)}) collective-permute-start(bf16[384,128]{1,0:T(8,128)(2,1)S(1)} %get-tuple-element.293.refs_11_), channel_id=1, source_target_pairs={{0,4},{1,5},{2,6},{3,7},{4,0},{5,1},{6,2},{7,3},{8,12},{9,13},{10,... | collective-permute-start | bytes 294920 | tf_op jit(solution)/shard_map/ppermute | solution.py:1088
  182.2 11.8 %collective-permute-start.33 = (bf16[576,128]{1,0:T(8,128)(2,1)S(1)}, bf16[576,128]{1,0:T(8,128)(2,1)S(1)}, u32[]{:S(2)}, u32[]{:S(2)}) collective-permute-start(bf16[576,128]{1,0:T(8,128)(2,1)S(1)} %get-tuple-element.294), channel_id=1, source_target_pairs={{0,2},{1,3},{2,0},{3,1},{4,6},{5,7},{6,4},{7,5},{8,10},{9,11},{10,... | collective-permute-start | bytes 442376 | tf_op jit(solution)/shard_map/ppermute | solution.py:1088
  183.7 11.9 %collective-permute-start.37 = (bf16[2304,128]{1,0:T(8,128)(2,1)S(1)}, bf16[2304,128]{1,0:T(8,128)(2,1)S(1)}, u32[]{:S(2)}, u32[]{:S(2)}) collective-permute-start(bf16[2304,128]{1,0:T(8,128)(2,1)S(1)} %get-tuple-element.299.refs_1_), channel_id=1, source_target_pairs={{0,8},{8,0},{16,24},{24,16},{1,9},{9,1},{17,25},{25,17},{2,10},{10... | collective-permute-start | bytes 1769480 | tf_op jit(solution)/shard_map/ppermute | solution.py:1088
  (26 other events, 161.6 us)

commit v4 on v3

--- a/solution.py
+++ b/solution.py
@@ -1461,16 +1461,14 @@
     b_in, b_jn = weight_buckets(cols_in, keep, send, orders, y_bits)
     send_round(30, b_out)
     dh2, gain_ff_grad = feed_back(dpre, w1_near, h2_near, gains, gy)
-    send_round(8, b_in, b_jn)
+    send_round(5.5, b_in, b_jn)
     pairs = heads // 2
-    parts_a = cross_backward(0, pairs // 2, dh2, o2, inv, cq, kv, e, wco_near, [])
-    parts_b = cross_backward(
-        pairs // 2, pairs, dh2, o2, inv, cq, kv, e, wco_near, [w_cross_q, h1, a2, o2, o1, enc, w_cross_kv]
-    )
-    wcq_near, h1_near, a2, o2, o1, enc, wkv_near = parts_b[3:]
-    dcq, dkt, dvt = zip(parts_a, parts_b[:3])
+    dcq, dkt, dvt, wcq_near, h1_near, a2, o2, o1, enc, wkv_near = cross_backward(
+        0, pairs, dh2, o2, inv, cq, kv, e, wco_near, [w_cross_q, h1, a2, o2, o1, enc, w_cross_kv]
+    )
+    dcq, dkt, dvt = [dcq], [dkt], [dvt]
     dh1, gain_cross_grad = cross_query_back(dcq, wcq_near, h1_near, gains, dh2)
-    send_round(12, b_jn, b_out, b_in)
+    send_round(5.5, b_jn, b_out, b_in)
     genc, keep, send, hid, w2_near, h2_near = cross_weights(
         place, dh2, o2, dcq, dkt, dvt, enc, a2, wkv_near, dh1, o1, cols_x, [hid, w_ff_out, h2]
     )
@@ -1485,7 +1483,7 @@
     dqkv, gbias, wqkv_near, x_near, a1 = self_backward(
         dh1, wso_near, qkv, p1, bucket_count, heads, [w_qkv, x, a1]
     )
-    send_round(8, b_xb, b_xa, b_eb, b_ea, b_in, b_out, settle=[b_jn])
+    send_round(5, b_xb, b_xa, b_eb, b_ea, b_in, b_out, settle=[b_jn])
     grad_dec, keep, send = self_weights(
         place, dh1, a1, dqkv, x_near, gains, wqkv_near, gbias, gain_cross_grad, gain_ff_grad, cols_s
     )

time: 217 us -> 217 us (level)
  waiting for transfers between devices: 24.1 us -> 28.2 us
  Pallas kernels: 133 us -> 130 us
    ppermute x42, waiting for transfers between devices: 24.1 us -> 28.2 us  [swap(): return lax.ppermute(value, axis, [(i, i ^ bit) for i in range(size)])]
    pallas_call x56 -> x55, Pallas kernels: 133 us -> 130 us  [call(): pl.pallas_call(ordered, out_shape=tuple(out_shape), grid_spec=pltpu.Prefe...]
  transfers between devices with their start and end apart: 42 -> 42, of which waited for: 12 -> 14; matrix products, arithmetic and copies ran while one was open for 0% -> 0% of each run, Pallas kernels for 47% -> 46%
where the time goes in v4:
time: 217 us; the launch traced here: 216 us
  Pallas kernels  130 us (60%)
  starting transfers between devices  53.1 us (24%)
  waiting for transfers between devices  28.2 us (13%)
  local copies, waits for them, and re-layouts  2.33 us (1%)
    pallas_call x55, Pallas kernels, call(): pl.pallas_call(ordered, out_shape=tuple(out_shape), grid_spec=pltpu.Prefe...  130 us
    ppermute x42, starting transfers between devices, swap(): return lax.ppermute(value, axis, [(i, i ^ bit) for i in range(size)])  53.1 us
    ppermute x42, waiting for transfers between devices, swap(): return lax.ppermute(value, axis, [(i, i ^ bit) for i in range(size)])  28.2 us
  transfers between devices with their start and end apart: 42, of which 14 were waited for; matrix products, arithmetic and copies ran while one was open for 0% of the time, Pallas kernels for 46%

profile of v4, /device:TPU:1, one launch (start us, length us, event | category | flops | bytes accessed | tf_op | source)
XLA Modules:
  0.0 216.5 jit_solution(9108026478621534697)
XLA Ops:
  5.7 2.3 %collective-permute-start = (bf16[1,144,768]{2,1,0:T(8,128)(2,1)S(1)}, bf16[1,144,768]{2,1,0:T(8,128)(2,1)}, u32[]{:S(2)}, u32[]{:S(2)}) collective-permute-start(bf16[1,144,768]{2,1,0:T(8,128)(2,1)S(1)} %fusion.2.refs_0_), channel_id=1, source_target_pairs={{0,4},{1,5},{2,6},{3,7},{4,0},{5,1},{6,2},{7,3},{8,12},{9,13},{10,... | collective-permute-start | bytes 663560 | tf_op jit(solution)/shard_map/ppermute | solution.py:1088
  8.1 11.2 %self_attention.1 = (bf16[512,768]{1,0:T(8,128)(2,1)}, bf16[512,2304]{1,0:T(8,128)(2,1)}, bf16[4,6,128,256]{3,2,1,0:T(8,128)(2,1)}, bf16[512,768]{1,0:T(8,128)(2...) custom-call(bf16[512,768]{1,0:T(8,128)(2,1)} %bitcast.447, ...), custom_call_target="tpu_custom_call" | custom-call | flops 1153000 | tf_op jit(solution)/shard_map/self_attention/pallas_call | solution.py:246
  21.9 2.9 %self_project.1 = (f32[512,768]{1,0:T(8,128)S(1)}, bf16[512,768]{1,0:T(8,128)(2,1)S(1)}, f32[512,768]{1,0:T(8,128)}, bf16[512,768]{1,0:T(8,128)(2,1)}, bf16[512,...) custom-call(bf16[512,768]{1,0:T(8,128)(2,1)S(1)} %copy-done.2, ...), custom_call_target="tpu_custom_call" | custom-call | flops 1153000 | tf_op jit(solution)/shard_map/self_project/pallas_call | solution.py:246
  27.0 4.6 %hidden_gradient.1 = (bf16[512,3072]{1,0:T(8,128)(2,1)S(1)}, bf16[768,1536]{1,0:T(8,128)(2,1)S(1)}, bf16[768,768]{1,0:T(8,128)(2,1)S(1)}, f32[8,128]{1,0:T(8,128)}) custom-call(bf16[512,768]{1,0:T(8,128)(2,1)S(1)} %get-tuple-element.177.refs_0_.refs_2_.refs_4_, bf16[3072,768]{1,0:T(8,128)(2,1)} %refs_12_.1, bf16[768,1536]{1,0:T(8,128)(2,1)} %refs_14_.3, ...), custom_call_target="tpu_custom_call" | custom-call | flops 1153000 | tf_op jit(solution)/shard_map/hidden_gradient/pallas_call | solution.py:246
  31.7 16.0 %cross_forward.1 = (bf16[1024,768]{1,0:T(8,128)(2,1)}, bf16[1024,1536]{1,0:T(8,128)(2,1)}, bf16[12,512,1024]{2,1,0:T(8,128)(2,1)}, f32[512,768]{1,0:T(8,128)}, b...) custom-call(bf16[1,144,768]{2,1,0:T(8,128)(2,1)S(1)} %fusion.2.refs_, ...), custom_call_target="tpu_custom_call" | custom-call | flops 1153000 | tf_op jit(solution)/shard_map/cross_forward/pallas_call | solution.py:246
  47.7 10.0 %feed_hidden.1 = (bf16[512,3072]{1,0:T(8,128)(2,1)S(1)}, bf16[512,3072]{1,0:T(8,128)(2,1)}, bf16[96,96,128]{2,1,0:T(8,128)(2,1)}, bf16[96,96,128]{2,1,0:T(8,128)(2,1)}, f32[8,128]{1,0:T(8,128)}) custom-call(s32[403]{0:T(512)S(1)} %pad_add_fusion.refs_0_, bf16[512,768]{1,0:T(8,128)(2,1)S(1)} %get-tuple-element.182.refs_1_, ...), custom_call_target="tpu_custom_call" | custom-call | flops 1153000 | tf_op jit(solution)/shard_map/feed_hidden/pallas_call | solution.py:246
  57.7 2.7 %collective-permute-start.7 = (bf16[9216,128]{1,0:T(8,128)(2,1)}, bf16[9216,128]{1,0:T(8,128)(2,1)S(1)}, u32[]{:S(2)}, u32[]{:S(2)}) collective-permute-start(bf16[9216,128]{1,0:T(8,128)(2,1)} %bitcast.454), channel_id=1, source_target_pairs={{0,8},{8,0},{16,24},{24,16},{1,9},{9,1},{17,25},{25,17},{2,10},{10... | collective-permute-start | bytes 7077896 | tf_op jit(solution)/shard_map/ppermute | solution.py:1088
  60.4 5.4 %feed_weights.1 = (bf16[96,96,128]{2,1,0:T(8,128)(2,1)}, bf16[96,96,128]{2,1,0:T(8,128)(2,1)}, f32[512,768]{1,0:T(8,128)S(1)}, f32[8,128]{1,0:T(8,128)}) custom-call(s32[403]{0:T(512)S(1)} %pad_add_fusion.refs_0_, bf16[512,768]{1,0:T(8,128)(2,1)S(1)} %get-tuple-element.182.refs_1_, bf16[512,3072]{1,0:T(8,128)(2,1)S(1)} %get-tuple-element.186.refs_2_.refs_0_, ...), custom_call_target="tpu_custom_call" | custom-call | flops 1153000 | tf_op jit(solution)/shard_map/feed_weights/pallas_call | solution.py:246
  68.8 4.3 %feed_back.1 = (f32[512,768]{1,0:T(8,128)S(1)}, f32[1,768]{1,0:T(1,128)S(1)}, f32[8,128]{1,0:T(8,128)}) custom-call(bf16[512,3072]{1,0:T(8,128)(2,1)S(1)} %get-tuple-element.186.refs_2_.refs_0_, bf16[768,3072]{1,0:T(8,128)(2,1)S(1)} %get-tuple-element.184.refs_4_.refs_1_, f32[512,768]{1,0:T(8,128)S(1)} %get-tuple-element.189.refs_2_, ...), custom_call_target="tpu_custom_call" | custom-call | flops 1153000 | tf_op jit(solution)/shard_map/feed_back/pallas_call | solution.py:246
  76.2 15.6 %cross_backward.1 = (bf16[512,768]{1,0:T(8,128)(2,1)S(1)}, bf16[768,1024]{1,0:T(8,128)(2,1)S(1)}, bf16[768,1024]{1,0:T(8,128)(2,1)S(1)}, bf16[768,768]{1,0:T(8,1...) custom-call(f32[512,768]{1,0:T(8,128)S(1)} %get-tuple-element.194.re, ...), custom_call_target="tpu_custom_call" | custom-call | flops 1153000 | tf_op jit(solution)/shard_map/cross_backward/pallas_call | solution.py:246
  97.8 13.2 %cross_weights.1 = (bf16[48,128,128]{2,1,0:T(8,128)(2,1)}, bf16[120,96,128]{2,1,0:T(8,128)(2,1)}, bf16[120,96,128]{2,1,0:T(8,128)(2,1)}, bf16[512,3072]{1,0:T(8,...) custom-call(s32[403]{0:T(512)S(1)} %pad_add_fusion.refs_0_, ...), custom_call_target="tpu_custom_call" | custom-call | flops 1153000 | tf_op jit(solution)/shard_map/cross_weights/pallas_call | solution.py:246
  117.6 4.3 %feed_out.1 = (bf16[512,768]{1,0:T(8,128)(2,1)}, bf16[768,768]{1,0:T(8,128)(2,1)S(1)}, bf16[512,2304]{1,0:T(8,128)(2,1)S(1)}, bf16[4,6,128,256]{3,2,1,0:T(8,128)(2,1)S(1)}, f32[8,128]{1,0:T(8,128)}) custom-call(bf16[512,3072]{1,0:T(8,128)(2,1)S(1)} %get-tuple-element.226.refs_0_, bf16[3072,768]{1,0:T(8,128)(2,1)S(1)} %get-tuple-element.227.refs_1_, ...), custom_call_target="tpu_custom_call" | custom-call | flops 1153000 | tf_op jit(solution)/shard_map/feed_out/pallas_call | solution.py:246
  121.9 7.7 %self_backward.1 = (bf16[512,2304]{1,0:T(8,128)(2,1)S(1)}, f32[16,128]{1,0:T(8,128)S(1)}, bf16[768,2304]{1,0:T(8,128)(2,1)S(1)}, bf16[512,768]{1,0:T(8,128)(2,1)...) custom-call(f32[512,768]{1,0:T(8,128)S(1)} %get-tuple-element.212.refs_2_.refs_0_.refs_1_, ...), custom_call_target="tpu_custom_call" | custom-call | flops 1153000 | tf_op jit(solution)/shard_map/self_backward/pallas_call | solution.py:246
  129.6 2.3 %collective-permute-done.15.refs_5_.refs_13_.refs_7_.refs_15_.refs_14_ = bf16[2176,128]{1,0:T(8,128)(2,1)S(1)} collective-permute-done((bf16[2176,128]{1,0:T(8,128)(2,1)S(1)}, bf16[2176,128]{1,0:T(8,128)(2,1)S(1)}, u32[]{:S(2)}, u32[]{:S(2)}) %collective-permute-start.15) | collective-permute-done | bytes 557088 | tf_op jit(solution)/shard_map/ppermute | solution.py:1088
  137.9 8.2 %self_weights.1 = (f32[512,768]{1,0:T(8,128)}, bf16[73,96,128]{2,1,0:T(8,128)(2,1)}, bf16[73,96,128]{2,1,0:T(8,128)(2,1)}, f32[8,128]{1,0:T(8,128)}) custom-call(s32[403]{0:T(512)S(1)} %pad_add_fusion.refs_0_, f32[512,768]{1,0:T(8,128)S(1)} %get-tuple-element.212.refs_2_.refs_0_.refs_1_, bf16[768,2304]{1,0:T(8,128)(2,1)S(1)} %get-tuple-element.242.refs_2_, ...), custom_call_target="tpu_custom_call" | custom-call | flops 1153000 | tf_op jit(solution)/shard_map/self_weights/pallas_call | solution.py:246
  146.2 3.9 %collective-permute-start.23 = (bf16[7008,128]{1,0:T(8,128)(2,1)}, bf16[7008,128]{1,0:T(8,128)(2,1)S(1)}, u32[]{:S(2)}, u32[]{:S(2)}) collective-permute-start(bf16[7008,128]{1,0:T(8,128)(2,1)} %bitcast.455), channel_id=1, source_target_pairs={{0,8},{8,0},{16,24},{24,16},{1,9},{9,1},{17,25},{25,17},{2,10},{10... | collective-permute-start | bytes 5382152 | tf_op jit(solution)/shard_map/ppermute | solution.py:1088
  153.7 2.6 %collective-permute-start.22 = (bf16[1344,128]{1,0:T(8,128)(2,1)S(1)}, bf16[1344,128]{1,0:T(8,128)(2,1)S(1)}, u32[]{:S(2)}, u32[]{:S(2)}) collective-permute-start(bf16[1344,128]{1,0:T(8,128)(2,1)S(1)} %get-tuple-element.263), channel_id=1, source_target_pairs={{0,2},{1,3},{2,0},{3,1},{4,6},{5,7},{6,4},{7,5},{8,10},{9,11},{10,... | collective-permute-start | bytes 1032200 | tf_op jit(solution)/shard_map/ppermute | solution.py:1088
  159.9 4.5 %collective-permute-done.26.refs_2_.refs_4_.refs_6_ = bf16[1248,128]{1,0:T(8,128)(2,1)S(1)} collective-permute-done((bf16[1248,128]{1,0:T(8,128)(2,1)S(1)}, bf16[1248,128]{1,0:T(8,128)(2,1)S(1)}, u32[]{:S(2)}, u32[]{:S(2)}) %collective-permute-start.26) | collective-permute-done | bytes 319520 | tf_op jit(solution)/shard_map/ppermute | solution.py:1088
  164.4 4.9 %collective-permute-done.27.refs_7_.refs_2_ = bf16[2304,128]{1,0:T(8,128)(2,1)S(1)} collective-permute-done((bf16[2304,128]{1,0:T(8,128)(2,1)S(1)}, bf16[2304,128]{1,0:T(8,128)(2,1)S(1)}, u32[]{:S(2)}, u32[]{:S(2)}) %collective-permute-start.27) | collective-permute-done | bytes 589856 | tf_op jit(solution)/shard_map/ppermute | solution.py:1088
  175.2 4.5 %collective-permute-done.30.refs_3_.refs_8_ = bf16[1152,128]{1,0:T(8,128)(2,1)S(1)} collective-permute-done((bf16[1152,128]{1,0:T(8,128)(2,1)S(1)}, bf16[1152,128]{1,0:T(8,128)(2,1)S(1)}, u32[]{:S(2)}, u32[]{:S(2)}) %collective-permute-start.30) | collective-permute-done | bytes 294944 | tf_op jit(solution)/shard_map/ppermute | solution.py:1088
  183.2 9.2 %collective-permute-start.37 = (bf16[2304,128]{1,0:T(8,128)(2,1)S(1)}, bf16[2304,128]{1,0:T(8,128)(2,1)S(1)}, u32[]{:S(2)}, u32[]{:S(2)}) collective-permute-start(bf16[2304,128]{1,0:T(8,128)(2,1)S(1)} %get-tuple-element.291.refs_1_), channel_id=1, source_target_pairs={{0,8},{8,0},{16,24},{24,16},{1,9},{9,1},{17,25},{25,17},{2,10},{10... | collective-permute-start | bytes 1769480 | tf_op jit(solution)/shard_map/ppermute | solution.py:1088
  194.2 2.4 %collective-permute-start.34 = (bf16[288,128]{1,0:T(8,128)(2,1)S(1)}, bf16[288,128]{1,0:T(8,128)(2,1)S(1)}, u32[]{:S(2)}, u32[]{:S(2)}) collective-permute-start(bf16[288,128]{1,0:T(8,128)(2,1)S(1)} %get-tuple-element.288), channel_id=1, source_target_pairs={{0,4},{1,5},{2,6},{3,7},{4,0},{5,1},{6,2},{7,3},{8,12},{9,13},{10,... | collective-permute-start | bytes 221192 | tf_op jit(solution)/shard_map/ppermute | solution.py:1088
  204.4 3.6 %collective-permute-done.39.refs_1_.refs_3_ = bf16[1056,128]{1,0:T(8,128)(2,1)S(1)} collective-permute-done((bf16[1056,128]{1,0:T(8,128)(2,1)S(1)}, bf16[1056,128]{1,0:T(8,128)(2,1)S(1)}, u32[]{:S(2)}, u32[]{:S(2)}) %collective-permute-start.39) | collective-permute-done | bytes 270368 | tf_op jit(solution)/shard_map/ppermute | solution.py:1088
  208.0 2.3 %collective-permute-start.41 = (bf16[1440,128]{1,0:T(8,128)(2,1)S(1)}, bf16[1440,128]{1,0:T(8,128)(2,1)S(1)}, u32[]{:S(2)}, u32[]{:S(2)}) collective-permute-start(bf16[1440,128]{1,0:T(8,128)(2,1)S(1)} %get-tuple-element.300.refs_1_), channel_id=1, source_target_pairs={{0,8},{8,0},{16,24},{24,16},{1,9},{9,1},{17,25},{25,17},{2,10},{10... | collective-permute-start | bytes 1105928 | tf_op jit(solution)/shard_map/ppermute | solution.py:1088
  (140 shorter events, 66.8 us)
Async XLA Ops:
  2.3 22.5 %collective-permute-start.2 = (bf16[1,144,768]{2,1,0:T(8,128)(2,1)S(1)}, bf16[1,144,768]{2,1,0:T(8,128)(2,1)}, u32[]{:S(2)}, u32[]{:S(2)}) collective-permute-start(bf16[1,144,768]{2,1,0:T(8,128)(2,1)S(1)} %fusion.2.refs_0_), channel_id=1, source_target_pairs={{0,2},{1,3},{2,0},{3,1},{4,6},{5,7},{6,4},{7,5},{8,10},{9,11},{10,... | collective-permute-start | bytes 663560 | tf_op jit(solution)/shard_map/ppermute | solution.py:1088
  4.5 27.1 %collective-permute-start.1 = (bf16[1,144,768]{2,1,0:T(8,128)(2,1)S(1)}, bf16[1,144,768]{2,1,0:T(8,128)(2,1)}, u32[]{:S(2)}, u32[]{:S(2)}) collective-permute-start(bf16[1,144,768]{2,1,0:T(8,128)(2,1)S(1)} %fusion.2.refs_0_), channel_id=1, source_target_pairs={{0,1},{1,0},{2,3},{3,2},{4,5},{5,4},{6,7},{7,6},{8,9},{9,8},{10,11... | collective-permute-start | bytes 663560 | tf_op jit(solution)/shard_map/ppermute | solution.py:1088
  5.7 13.6 %collective-permute-start = (bf16[1,144,768]{2,1,0:T(8,128)(2,1)S(1)}, bf16[1,144,768]{2,1,0:T(8,128)(2,1)}, u32[]{:S(2)}, u32[]{:S(2)}) collective-permute-start(bf16[1,144,768]{2,1,0:T(8,128)(2,1)S(1)} %fusion.2.refs_0_), channel_id=1, source_target_pairs={{0,4},{1,5},{2,6},{3,7},{4,0},{5,1},{6,2},{7,3},{8,12},{9,13},{10,... | collective-permute-start | bytes 663560 | tf_op jit(solution)/shard_map/ppermute | solution.py:1088
  67.5 27.1 %collective-permute-start.10 = (bf16[4608,128]{1,0:T(8,128)(2,1)S(1)}, bf16[4608,128]{1,0:T(8,128)(2,1)S(1)}, u32[]{:S(2)}, u32[]{:S(2)}) collective-permute-start(bf16[4608,128]{1,0:T(8,128)(2,1)S(1)} %get-tuple-element.222), channel_id=1, source_target_pairs={{0,16},{8,24},{16,0},{24,8},{1,17},{9,25},{17,1},{25,9},{2,18},{10... | collective-permute-start | bytes 3538952 | tf_op jit(solution)/shard_map/ppermute | solution.py:1088
  74.7 18.5 %collective-permute-start.11 = (bf16[3072,128]{1,0:T(8,128)(2,1)S(1)}, bf16[3072,128]{1,0:T(8,128)(2,1)S(1)}, u32[]{:S(2)}, u32[]{:S(2)}) collective-permute-start(bf16[3072,128]{1,0:T(8,128)(2,1)S(1)} %get-tuple-element.223), channel_id=1, source_target_pairs={{0,1},{1,0},{2,3},{3,2},{4,5},{5,4},{6,7},{7,6},{8,9},{9,8},{10,11... | collective-permute-start | bytes 2359304 | tf_op jit(solution)/shard_map/ppermute | solution.py:1088
  75.0 18.2 %collective-permute-start.9 = (bf16[1536,128]{1,0:T(8,128)(2,1)S(1)}, bf16[1536,128]{1,0:T(8,128)(2,1)S(1)}, u32[]{:S(2)}, u32[]{:S(2)}) collective-permute-start(bf16[1536,128]{1,0:T(8,128)(2,1)S(1)} %get-tuple-element.221), channel_id=1, source_target_pairs={{0,2},{1,3},{2,0},{3,1},{4,6},{5,7},{6,4},{7,5},{8,10},{9,11},{10,... | collective-permute-start | bytes 1179656 | tf_op jit(solution)/shard_map/ppermute | solution.py:1088
  96.3 17.8 %collective-permute-start.12 = (bf16[3072,128]{1,0:T(8,128)(2,1)S(1)}, bf16[3072,128]{1,0:T(8,128)(2,1)S(1)}, u32[]{:S(2)}, u32[]{:S(2)}) collective-permute-start(bf16[3072,128]{1,0:T(8,128)(2,1)S(1)} %get-tuple-element.232), channel_id=1, source_target_pairs={{0,1},{1,0},{2,3},{3,2},{4,5},{5,4},{6,7},{7,6},{8,9},{9,8},{10,11... | collective-permute-start | bytes 2359304 | tf_op jit(solution)/shard_map/ppermute | solution.py:1088
  96.6 16.3 %collective-permute-start.13 = (bf16[1536,128]{1,0:T(8,128)(2,1)S(1)}, bf16[1536,128]{1,0:T(8,128)(2,1)S(1)}, u32[]{:S(2)}, u32[]{:S(2)}) collective-permute-start(bf16[1536,128]{1,0:T(8,128)(2,1)S(1)} %get-tuple-element.233), channel_id=1, source_target_pairs={{0,2},{1,3},{2,0},{3,1},{4,6},{5,7},{6,4},{7,5},{8,10},{9,11},{10,... | collective-permute-start | bytes 1179656 | tf_op jit(solution)/shard_map/ppermute | solution.py:1088
  111.0 20.9 %collective-permute-start.14 = (bf16[11520,128]{1,0:T(8,128)(2,1)}, bf16[11520,128]{1,0:T(8,128)(2,1)S(1)}, u32[]{:S(2)}, u32[]{:S(2)}) collective-permute-start(bf16[11520,128]{1,0:T(8,128)(2,1)} %bitcast.452), channel_id=1, source_target_pairs={{0,8},{8,0},{16,24},{24,16},{1,9},{9,1},{17,25},{25,17},{2,10},{10... | collective-permute-start | bytes 8847368 | tf_op jit(solution)/shard_map/ppermute | solution.py:1088
  116.0 13.6 %collective-permute-start.17 = (bf16[384,128]{1,0:T(8,128)(2,1)S(1)}, bf16[384,128]{1,0:T(8,128)(2,1)S(1)}, u32[]{:S(2)}, u32[]{:S(2)}) collective-permute-start(bf16[384,128]{1,0:T(8,128)(2,1)S(1)} %get-tuple-element.254), channel_id=1, source_target_pairs={{0,4},{1,5},{2,6},{3,7},{4,0},{5,1},{6,2},{7,3},{8,12},{9,13},{10,... | collective-permute-start | bytes 294920 | tf_op jit(solution)/shard_map/ppermute | solution.py:1088
  116.8 12.7 %collective-permute-start.16 = (bf16[2048,128]{1,0:T(8,128)(2,1)S(1)}, bf16[2048,128]{1,0:T(8,128)(2,1)S(1)}, u32[]{:S(2)}, u32[]{:S(2)}) collective-permute-start(bf16[2048,128]{1,0:T(8,128)(2,1)S(1)} %get-tuple-element.252), channel_id=1, source_target_pairs={{0,1},{1,0},{2,3},{3,2},{4,5},{5,4},{6,7},{7,6},{8,9},{9,8},{10,11... | collective-permute-start | bytes 1572872 | tf_op jit(solution)/shard_map/ppermute | solution.py:1088
  117.0 14.8 %collective-permute-start.15 = (bf16[2176,128]{1,0:T(8,128)(2,1)S(1)}, bf16[2176,128]{1,0:T(8,128)(2,1)S(1)}, u32[]{:S(2)}, u32[]{:S(2)}) collective-permute-start(bf16[2176,128]{1,0:T(8,128)(2,1)S(1)} %get-tuple-element.251), channel_id=1, source_target_pairs={{0,2},{1,3},{2,0},{3,1},{4,6},{5,7},{6,4},{7,5},{8,10},{9,11},{10,... | collective-permute-start | bytes 1671176 | tf_op jit(solution)/shard_map/ppermute | solution.py:1088
  134.0 17.6 %collective-permute-start.18 = (bf16[3200,128]{1,0:T(8,128)(2,1)S(1)}, bf16[3200,128]{1,0:T(8,128)(2,1)S(1)}, u32[]{:S(2)}, u32[]{:S(2)}) collective-permute-start(bf16[3200,128]{1,0:T(8,128)(2,1)S(1)} %get-tuple-element.258), channel_id=1, source_target_pairs={{0,1},{1,0},{2,3},{3,2},{4,5},{5,4},{6,7},{7,6},{8,9},{9,8},{10,11... | collective-permute-start | bytes 2457608 | tf_op jit(solution)/shard_map/ppermute | solution.py:1088
  134.1 16.4 %collective-permute-start.21 = (bf16[3072,128]{1,0:T(8,128)(2,1)S(1)}, bf16[3072,128]{1,0:T(8,128)(2,1)S(1)}, u32[]{:S(2)}, u32[]{:S(2)}) collective-permute-start(bf16[3072,128]{1,0:T(8,128)(2,1)S(1)} %get-tuple-element.261), channel_id=1, source_target_pairs={{0,16},{8,24},{16,0},{24,8},{1,17},{9,25},{17,1},{25,9},{2,18},{10... | collective-permute-start | bytes 2359304 | tf_op jit(solution)/shard_map/ppermute | solution.py:1088
  135.4 14.7 %collective-permute-start.19 = (bf16[1024,128]{1,0:T(8,128)(2,1)S(1)}, bf16[1024,128]{1,0:T(8,128)(2,1)S(1)}, u32[]{:S(2)}, u32[]{:S(2)}) collective-permute-start(bf16[1024,128]{1,0:T(8,128)(2,1)S(1)} %get-tuple-element.259), channel_id=1, source_target_pairs={{0,2},{1,3},{2,0},{3,1},{4,6},{5,7},{6,4},{7,5},{8,10},{9,11},{10,... | collective-permute-start | bytes 786440 | tf_op jit(solution)/shard_map/ppermute | solution.py:1088
  135.6 14.4 %collective-permute-start.20 = (bf16[1344,128]{1,0:T(8,128)(2,1)S(1)}, bf16[1344,128]{1,0:T(8,128)(2,1)S(1)}, u32[]{:S(2)}, u32[]{:S(2)}) collective-permute-start(bf16[1344,128]{1,0:T(8,128)(2,1)S(1)} %get-tuple-element.260), channel_id=1, source_target_pairs={{0,4},{1,5},{2,6},{3,7},{4,0},{5,1},{6,2},{7,3},{8,12},{9,13},{10,... | collective-permute-start | bytes 1032200 | tf_op jit(solution)/shard_map/ppermute | solution.py:1088
  153.6 17.0 %collective-permute-start.25 = (bf16[768,128]{1,0:T(8,128)(2,1)S(1)}, bf16[768,128]{1,0:T(8,128)(2,1)S(1)}, u32[]{:S(2)}, u32[]{:S(2)}) collective-permute-start(bf16[768,128]{1,0:T(8,128)(2,1)S(1)} %get-tuple-element.271), channel_id=1, source_target_pairs={{0,4},{1,5},{2,6},{3,7},{4,0},{5,1},{6,2},{7,3},{8,12},{9,13},{10,... | collective-permute-start | bytes 589832 | tf_op jit(solution)/shard_map/ppermute | solution.py:1088
  153.7 16.9 %collective-permute-start.22 = (bf16[1344,128]{1,0:T(8,128)(2,1)S(1)}, bf16[1344,128]{1,0:T(8,128)(2,1)S(1)}, u32[]{:S(2)}, u32[]{:S(2)}) collective-permute-start(bf16[1344,128]{1,0:T(8,128)(2,1)S(1)} %get-tuple-element.263), channel_id=1, source_target_pairs={{0,2},{1,3},{2,0},{3,1},{4,6},{5,7},{6,4},{7,5},{8,10},{9,11},{10,... | collective-permute-start | bytes 1032200 | tf_op jit(solution)/shard_map/ppermute | solution.py:1088
  157.7 11.5 %collective-permute-start.27 = (bf16[2304,128]{1,0:T(8,128)(2,1)S(1)}, bf16[2304,128]{1,0:T(8,128)(2,1)S(1)}, u32[]{:S(2)}, u32[]{:S(2)}) collective-permute-start(bf16[2304,128]{1,0:T(8,128)(2,1)S(1)} %get-tuple-element.273), channel_id=1, source_target_pairs={{0,16},{8,24},{16,0},{24,8},{1,17},{9,25},{17,1},{25,9},{2,18},{10... | collective-permute-start | bytes 1769480 | tf_op jit(solution)/shard_map/ppermute | solution.py:1088
  158.8 12.8 %collective-permute-start.24 = (bf16[1536,128]{1,0:T(8,128)(2,1)S(1)}, bf16[1536,128]{1,0:T(8,128)(2,1)S(1)}, u32[]{:S(2)}, u32[]{:S(2)}) collective-permute-start(bf16[1536,128]{1,0:T(8,128)(2,1)S(1)} %get-tuple-element.269), channel_id=1, source_target_pairs={{0,1},{1,0},{2,3},{3,2},{4,5},{5,4},{6,7},{7,6},{8,9},{9,8},{10,11... | collective-permute-start | bytes 1179656 | tf_op jit(solution)/shard_map/ppermute | solution.py:1088
  174.4 24.4 %collective-permute-start.35 = (bf16[672,128]{1,0:T(8,128)(2,1)S(1)}, bf16[672,128]{1,0:T(8,128)(2,1)S(1)}, u32[]{:S(2)}, u32[]{:S(2)}) collective-permute-start(bf16[672,128]{1,0:T(8,128)(2,1)S(1)} %get-tuple-element.289), channel_id=1, source_target_pairs={{0,4},{1,5},{2,6},{3,7},{4,0},{5,1},{6,2},{7,3},{8,12},{9,13},{10,... | collective-permute-start | bytes 516104 | tf_op jit(solution)/shard_map/ppermute | solution.py:1088
  180.8 20.4 %collective-permute-start.32 = (bf16[384,128]{1,0:T(8,128)(2,1)S(1)}, bf16[384,128]{1,0:T(8,128)(2,1)S(1)}, u32[]{:S(2)}, u32[]{:S(2)}) collective-permute-start(bf16[384,128]{1,0:T(8,128)(2,1)S(1)} %get-tuple-element.285.refs_11_), channel_id=1, source_target_pairs={{0,4},{1,5},{2,6},{3,7},{4,0},{5,1},{6,2},{7,3},{8,12},{9,13},{10,... | collective-permute-start | bytes 294920 | tf_op jit(solution)/shard_map/ppermute | solution.py:1088
  181.4 11.8 %collective-permute-start.33 = (bf16[576,128]{1,0:T(8,128)(2,1)S(1)}, bf16[576,128]{1,0:T(8,128)(2,1)S(1)}, u32[]{:S(2)}, u32[]{:S(2)}) collective-permute-start(bf16[576,128]{1,0:T(8,128)(2,1)S(1)} %get-tuple-element.286), channel_id=1, source_target_pairs={{0,2},{1,3},{2,0},{3,1},{4,6},{5,7},{6,4},{7,5},{8,10},{9,11},{10,... | collective-permute-start | bytes 442376 | tf_op jit(solution)/shard_map/ppermute | solution.py:1088
  183.2 13.5 %collective-permute-start.37 = (bf16[2304,128]{1,0:T(8,128)(2,1)S(1)}, bf16[2304,128]{1,0:T(8,128)(2,1)S(1)}, u32[]{:S(2)}, u32[]{:S(2)}) collective-permute-start(bf16[2304,128]{1,0:T(8,128)(2,1)S(1)} %get-tuple-element.291.refs_1_), channel_id=1, source_target_pairs={{0,8},{8,0},{16,24},{24,16},{1,9},{9,1},{17,25},{25,17},{2,10},{10... | collective-permute-start | bytes 1769480 | tf_op jit(solution)/shard_map/ppermute | solution.py:1088
  (26 other events, 161.2 us)
